TPU v7x, 128 devices: a whole 4x4x4 slice. The times are simulated.
128 devices in a mesh: dp: 16 (over x, z_hi, core), ctx: 8 (over z_lo, y).
Axes of the slice: x: 4, y: 4, z: 4 (z_hi: 2, z_lo: 2; z = z_hi * 2 + z_lo), core: 2. Of those that a mesh axis runs over, the one named last changes fastest.
Arguments:
- normed: bfloat16 [16, 4096, 768], P('dp', 'ctx'), may hold values from -16 to 16
- cotangent: bfloat16 [16, 4096, 768], P('dp', 'ctx'), may hold values from -6 to 6
- qkv_weight: bfloat16 [768, 2304], replicated, may hold values from -0.375 to 0.375
- out_weight: bfloat16 [768, 768], replicated, may hold values from -0.21875 to 0.21875
Outputs:
- attention_out: bfloat16 [16, 4096, 768], P('dp', 'ctx')
- normed_grad: bfloat16 [16, 4096, 768], P('dp', 'ctx')
- qkv_grad: float32 [768, 2304], P('dp')
- out_grad: float32 [768, 768], P('dp')
All inputs are finite; a program needn't handle non-finite values.
Results may differ from a plain program's by a relative error of at most 0.025.
Values may be sent and summed in bfloat16 or wider, within the bound.
No kernel may reach another device: no remote copies, remote signals or barrier semaphores. Data moves between devices by JAX's collectives and lax.ppermute only.
A program may use at most 128 MiB of HBM per device.

v0:
```python
import jax
import jax.numpy as jnp
from jax import lax
from jax.sharding import PartitionSpec as P

HEAD_DIM = 64
ROW_LEN = 512


def shortened(shard):

    def short(part):
        return part.astype(jnp.bfloat16) if part.dtype == jnp.float32 else part

    return jax.tree.map(short, shard)


def attend(queries, key_part, value_part, grad_part):
    score_scale = queries.shape[-1] ** (-0.5)
    scores = (
        jnp.einsum("gihd,gjhd->ghij", queries, key_part, preferred_element_type=jnp.float32)
        * score_scale
    )
    length = queries.shape[1]
    causal = lax.broadcasted_iota(jnp.int32, (length, length), 1) <= lax.broadcasted_iota(
        jnp.int32, (length, length), 0
    )
    scores = jnp.where(causal, scores, -1e30)
    top = jnp.max(scores, axis=-1, keepdims=True)
    weights = jnp.exp(scores - top)
    weights = weights / jnp.sum(weights, axis=-1, keepdims=True)
    rounded = weights.astype(jnp.bfloat16)
    outputs = jnp.einsum(
        "ghij,gjhd->gihd", rounded, value_part, preferred_element_type=jnp.float32
    ).astype(jnp.bfloat16)
    grad_weights = jnp.einsum(
        "gihd,gjhd->ghij", grad_part, value_part, preferred_element_type=jnp.float32
    )
    row_delta = jnp.sum(weights * grad_weights, axis=-1, keepdims=True)
    grad_scores = (weights * (grad_weights - row_delta) * score_scale).astype(jnp.bfloat16)
    grad_queries = jnp.einsum(
        "ghij,gjhd->gihd", grad_scores, key_part, preferred_element_type=jnp.float32
    ).astype(jnp.bfloat16)
    grad_keys = jnp.einsum(
        "ghij,gihd->gjhd", grad_scores, queries, preferred_element_type=jnp.float32
    ).astype(jnp.bfloat16)
    grad_values = jnp.einsum(
        "ghij,gihd->gjhd", rounded, grad_part, preferred_element_type=jnp.float32
    ).astype(jnp.bfloat16)
    return (outputs, grad_queries, grad_keys, grad_values)


def body(normed, cotangent, qkv_weight, out_weight):
    inputs = normed[0]
    grad_out = cotangent[0]
    width = out_weight.shape[0]
    half_width = width // 2
    local_rows = inputs.shape[0] // ROW_LEN
    projected = jnp.dot(inputs, qkv_weight, preferred_element_type=jnp.float32).astype(jnp.bfloat16)
    grad_context = jnp.dot(grad_out, out_weight, preferred_element_type=jnp.float32).astype(
        jnp.bfloat16
    )
    pieces = [
        projected[:, :width],
        projected[:, width : 2 * width],
        projected[:, 2 * width :],
        grad_context,
    ]
    column_send = tuple(
        (piece[:, half_width:].reshape(local_rows, ROW_LEN, half_width) for piece in pieces)
    )
    column_recv = jax.tree.map(
        lambda part, own: part.astype(own.dtype),
        lax.all_to_all(shortened(column_send), "ctx", split_axis=1, concat_axis=0, tiled=True),
        column_send,
    )
    all_rows = column_recv[0].shape[0]
    col_width = column_recv[0].shape[1]
    column_views = [
        jnp.transpose(piece.reshape(all_rows, col_width, -1, HEAD_DIM), (1, 0, 2, 3))
        for piece in column_recv
    ]
    column_results = attend(column_views[0], column_views[1], column_views[2], column_views[3])
    column_flat = tuple(
        (
            jnp.transpose(piece, (1, 0, 2, 3)).reshape(all_rows, col_width, half_width)
            for piece in column_results
        )
    )
    row_views = [
        piece[:, :half_width].reshape(local_rows, ROW_LEN, -1, HEAD_DIM) for piece in pieces
    ]
    row_results = attend(row_views[0], row_views[1], row_views[2], row_views[3])
    column_back = jax.tree.map(
        lambda part, own: part.astype(own.dtype),
        lax.all_to_all(shortened(column_flat), "ctx", split_axis=0, concat_axis=1, tiled=True),
        column_flat,
    )
    joined = [
        jnp.concatenate(
            [
                row_results[index].reshape(-1, half_width),
                column_back[index].reshape(-1, half_width),
            ],
            axis=1,
        )
        for index in range(4)
    ]
    context = joined[0]
    grad_projected = jnp.concatenate([joined[1], joined[2], joined[3]], axis=1)
    attention_out = jnp.dot(context, out_weight.T, preferred_element_type=jnp.float32).astype(
        jnp.bfloat16
    )
    normed_grad = jnp.dot(grad_projected, qkv_weight.T, preferred_element_type=jnp.float32).astype(
        jnp.bfloat16
    )
    factor = (lax.axis_size("dp") * lax.axis_size("ctx") * inputs.shape[0]) ** (-0.5)
    qkv_term = jnp.dot(inputs.T, grad_projected, preferred_element_type=jnp.float32) * factor
    out_term = jnp.dot(grad_out.T, context, preferred_element_type=jnp.float32) * factor
    summed = (
        lax.psum(qkv_term.astype(jnp.bfloat16), "ctx").astype(jnp.float32),
        lax.psum(out_term.astype(jnp.bfloat16), "ctx").astype(jnp.float32),
    )
    qkv_grad, out_grad = (
        lax.psum_scatter(
            summed[0].astype(jnp.bfloat16), "dp", scatter_dimension=0, tiled=True
        ).astype(jnp.float32),
        lax.psum_scatter(
            summed[1].astype(jnp.bfloat16), "dp", scatter_dimension=0, tiled=True
        ).astype(jnp.float32),
    )
    return (attention_out[None], normed_grad[None], qkv_grad, out_grad)


def solution(mesh):
    placed = (P("dp", "ctx", None), P("dp", "ctx", None), P(), P())
    return jax.shard_map(
        body,
        mesh=mesh,
        in_specs=placed,
        out_specs=(P("dp", "ctx", None), P("dp", "ctx", None), P("dp", None), P("dp", None)),
        check_vma=False,
    )
```

profile of v0, /device:TPU:0, one launch (start us, length us, event | category | flops | bytes accessed | tf_op | source)
XLA Modules:
  0.0 452.2 jit_solution(8268136238588288435)
XLA Ops:
  12.4 4.7 %reduce.17 = bf16[512,384]{1,0:T(8,128)(2,1)} reduce(bf16[512,1,384]{2,1,0:T(2,128)(2,1)} %bitcast.128, bf16[]{:T(256)} %broadcast.61), dimensions={1}, to_apply=%bitcast.124.reduce_sub_computation | reduce | bytes 786434
  19.0 6.1 %all-to-all-start.4 = ((bf16[8,2,12288]{2,1,0:T(2,128)(2,1)}), bf16[8,2,12288]{2,1,0:T(2,128)(2,1)}, u32[]{:S(2)}, u32[]{:S(2)}) async-start(bf16[8,2,12288]{2,1,0:T(2,128)(2,1)} %reshape.211), calls=%async_computation.4 | async-start | bytes 786432 | tf_op jit(solution)/shard_map/all_to_all | solution.py:74
  38.2 6.3 %fusion.99 = (f32[6,512]{1,0:T(8,128)S(1)}, f32[6,512,512]{1,2,0:T(8,128)}) fusion(pred[512,512]{0,1:T(8,128)(4,1)} %iota_compare_fusion, bf16[512,6,64]{0,2,1:T(8,128)(2,1)} %bitcast.138, bf16[512,6,64]{0,2,1:T(8,128)(2,1)} %bitcast.140), kind=kOutput, calls=%fused_computation.102 | convolution fusion | flops 207618560 | bytes 7352320 | tf_op jit(solution)/shard_map/sub | solution.py:30
  44.4 4.9 %fusion.43 = bf16[6,64,512]{2,1,0:T(8,128)(2,1)} fusion(bf16[512,6,64]{0,2,1:T(8,128)(2,1)} %bitcast.132, f32[6,512,512]{1,2,0:T(8,128)} %get-tuple-element.29, f32[6,512]{1,0:T(8,128)S(1)} %get-tuple-element.28), kind=kOutput, calls=%fused_computation.47 | convolution fusion | flops 204668928 | bytes 7090176 | tf_op jit(solution)/shard_map/ghij,gihd->gjhd/dot_general | solution.py:47
  52.3 4.7 %reduce.15 = bf16[512,384]{1,0:T(8,128)(2,1)} reduce(bf16[512,1,384]{2,1,0:T(2,128)(2,1)} %bitcast.130, bf16[]{:T(256)} %broadcast.61), dimensions={1}, to_apply=%bitcast.125.reduce_sub_computation | reduce | bytes 786434
  58.8 6.0 %all-to-all-start.2 = ((bf16[8,2,12288]{2,1,0:T(2,128)(2,1)}), bf16[8,2,12288]{2,1,0:T(2,128)(2,1)}, u32[]{:S(2)}, u32[]{:S(2)}) async-start(bf16[8,2,12288]{2,1,0:T(2,128)(2,1)} %reshape.215), calls=%async_computation.2 | async-start | bytes 786432 | tf_op jit(solution)/shard_map/all_to_all | solution.py:74
  64.8 4.8 %fusion.100 = f32[6,512,512]{1,2,0:T(8,128)} fusion(bf16[512,6,64]{0,2,1:T(8,128)(2,1)} %bitcast.133, bf16[512,6,64]{0,2,1:T(8,128)(2,1)} %bitcast.134), kind=kOutput, calls=%fused_computation.111 | convolution fusion | flops 201326592 | bytes 7077888 | tf_op jit(solution)/shard_map/gihd,gjhd->ghij/dot_general | solution.py:36
  71.1 4.7 %reduce.16 = bf16[512,384]{1,0:T(8,128)(2,1)} reduce(bf16[512,1,384]{2,1,0:T(2,128)(2,1)} %bitcast.131, bf16[]{:T(256)} %broadcast.61), dimensions={1}, to_apply=%bitcast.126.reduce_sub_computation | reduce | bytes 786434
  77.6 11.8 %fusion.34 = bf16[6,64,512]{2,1,0:T(8,128)(2,1)} fusion(bf16[512,6,64]{0,2,1:T(8,128)(2,1)} %bitcast.141, f32[6,512,512]{1,2,0:T(8,128)} %fusion.100, f32[6,512,512]{1,2,0:T(8,128)} %get-tuple-element.29, f32[6,512]{1,0:T(8,128)S(1)} %get-tuple-element.28), kind=kOutput, calls=%fused_computation.44 | convolution fusion | flops 212536832 | bytes 13381632 | tf_op jit(solution)/shard_map/ghij,gjhd->gihd/dot_general | solution.py:41
  89.4 6.2 %all-to-all-start.1 = ((bf16[8,2,12288]{2,1,0:T(2,128)(2,1)}), bf16[8,2,12288]{2,1,0:T(2,128)(2,1)}, u32[]{:S(2)}, u32[]{:S(2)}) async-start(bf16[8,2,12288]{2,1,0:T(2,128)(2,1)} %reshape.217), calls=%async_computation.1 | async-start | bytes 786432 | tf_op jit(solution)/shard_map/all_to_all | solution.py:74
  95.6 11.4 %fusion.37 = bf16[6,64,512]{2,1,0:T(8,128)(2,1)} fusion(bf16[512,6,64]{0,2,1:T(8,128)(2,1)} %bitcast.139, f32[6,512,512]{1,2,0:T(8,128)} %fusion.100, f32[6,512,512]{1,2,0:T(8,128)} %get-tuple-element.29, f32[6,512]{1,0:T(8,128)S(1)} %get-tuple-element.28), kind=kOutput, calls=%fused_computation.45 | convolution fusion | flops 212536832 | bytes 13381632 | tf_op jit(solution)/shard_map/ghij,gihd->gjhd/dot_general | solution.py:44
  137.0 5.9 %all-to-all-start = ((bf16[8,2,12288]{2,1,0:T(2,128)(2,1)}), bf16[8,2,12288]{2,1,0:T(2,128)(2,1)}, u32[]{:S(2)}, u32[]{:S(2)}) async-start(bf16[8,2,12288]{2,1,0:T(2,128)(2,1)} %reshape.213), calls=%async_computation | async-start | bytes 786432 | tf_op jit(solution)/shard_map/all_to_all | solution.py:74
  169.8 5.1 %fusion.94 = (f32[64,6,8]{2,1,0:T(8,128)}, f32[64,6,8,8]{2,3,1,0:T(8,128)}) fusion(pred[8,8]{0,1:T(8,128)(4,1)S(1)} %iota_compare_fusion.1, bf16[8,64,6,64]{3,2,1,0:T(8,128)(2,1)} %reshape.201, bf16[8,64,6,64]{3,2,1,0:T(8,128)(2,1)} %reshape.200), kind=kOutput, calls=%fused_computation.101 | convolution fusion | flops 3244039 | bytes 897088 | tf_op jit(solution)/shard_map/sub | solution.py:30
  181.0 5.7 %all-to-all-start.3 = ((bf16[8,64,384]{2,1,0:T(8,128)(2,1)}), bf16[8,64,384]{2,1,0:T(8,128)(2,1)}, u32[]{:S(2)}, u32[]{:S(2)}) async-start(bf16[8,64,384]{2,1,0:T(8,128)(2,1)} %reshape.185), calls=%async_computation.3 | async-start | bytes 786432 | tf_op jit(solution)/shard_map/all_to_all | solution.py:96
  190.4 5.4 %fusion.29 = bf16[8,64,6,64]{3,0,2,1:T(8,128)(2,1)} fusion(f32[64,6,8,8]{2,3,1,0:T(8,128)} %fusion.51, bf16[8,64,6,64]{3,2,1,0:T(8,128)(2,1)} %reshape.201, f32[64,6,8,8]{2,3,1,0:T(8,128)} %get-tuple-element.27, f32[64,6,8]{2,1,0:T(8,128)} %get-tuple-element.26), kind=kOutput, calls=%fused_computation.39 | convolution fusion | flops 3517447 | bytes 995328 | tf_op jit(solution)/shard_map/ghij,gjhd->gihd/dot_general | solution.py:41
  200.6 5.7 %all-to-all-start.5 = ((bf16[8,64,384]{2,1,0:T(8,128)(2,1)}), bf16[8,64,384]{2,1,0:T(8,128)(2,1)}, u32[]{:S(2)}, u32[]{:S(2)}) async-start(bf16[8,64,384]{2,1,0:T(8,128)(2,1)} %reshape.191), calls=%async_computation.5 | async-start | bytes 786432 | tf_op jit(solution)/shard_map/all_to_all | solution.py:96
  213.7 5.3 %fusion.30 = bf16[8,64,6,64]{3,0,2,1:T(8,128)(2,1)} fusion(f32[64,6,8,8]{2,3,1,0:T(8,128)} %fusion.51, bf16[8,64,6,64]{3,2,1,0:T(8,128)(2,1)} %reshape.200, f32[64,6,8,8]{2,3,1,0:T(8,128)} %get-tuple-element.27, f32[64,6,8]{2,1,0:T(8,128)} %get-tuple-element.26), kind=kOutput, calls=%fused_computation.40 | convolution fusion | flops 3517447 | bytes 995328 | tf_op jit(solution)/shard_map/ghij,gihd->gjhd/dot_general | solution.py:44
  223.9 6.0 %all-to-all-start.6 = ((bf16[8,64,384]{2,1,0:T(8,128)(2,1)}), bf16[8,64,384]{2,1,0:T(8,128)(2,1)}, u32[]{:S(2)}, u32[]{:S(2)}) async-start(bf16[8,64,384]{2,1,0:T(8,128)(2,1)} %reshape.194), calls=%async_computation.6 | async-start | bytes 786432 | tf_op jit(solution)/shard_map/all_to_all | solution.py:96
  238.0 5.7 %all-to-all-start.7 = ((bf16[8,64,384]{2,1,0:T(8,128)(2,1)}), bf16[8,64,384]{2,1,0:T(8,128)(2,1)}, u32[]{:S(2)}, u32[]{:S(2)}) async-start(bf16[8,64,384]{2,1,0:T(8,128)(2,1)} %reshape.197), calls=%async_computation.7 | async-start | bytes 786432 | tf_op jit(solution)/shard_map/all_to_all | solution.py:96
  253.6 5.7 %fusion.6 = bf16[768,2304]{0,1:T(8,128)(2,1)} fusion(bf16[512,2304]{1,0:T(8,128)(2,1)} %constant_dynamic-update-slice_fusion, bf16[1,512,768]{2,1,0:T(8,128)(2,1)} %param.4), kind=kOutput, calls=%fused_computation.11 | convolution fusion | flops 1815478272 | bytes 6684672 | tf_op jit(solution)/shard_map/dot_general | solution.py:118
  259.3 5.8 %copy.102 = bf16[768,2304]{1,0:T(8,128)(2,1)} copy(bf16[768,2304]{0,1:T(8,128)(2,1)} %fusion.6) | data formatting | bytes 7077888
  265.2 17.7 %reduce-scatter.9.cloned.1.call-done = bf16[48,768]{1,0:T(8,128)(2,1)} async-done(((bf16[768,768]{1,0:T(8,128)(2,1)}), bf16[48,768]{1,0:T(8,128)(2,1)}) %reduce-scatter.9.cloned.1.call-update) | async-done | bytes 73744
  284.6 79.0 %reduce-scatter.7.cloned.1.call-done = bf16[48,2304]{1,0:T(8,128)(2,1)} async-done(((bf16[768,2304]{1,0:T(8,128)(2,1)}), bf16[48,2304]{1,0:T(8,128)(2,1)}) %reduce-scatter.7.cloned.1.call-update) | async-done | bytes 221200
  373.0 68.7 %all-reduce.3.cloned.1.call-done = (bf16[48,2304]{0,1:T(8,128)(2,1)}, bf16[48,768]{0,1:T(8,128)(2,1)}) async-done(((bf16[48,2304]{0,1:T(8,128)(2,1)}, bf16[48,768]{0,1:T(8,128)(2,1)}), (bf16[48,2304]{0,1:T(8,128)(2,1)}, bf16[48,768]{0,1:T(8,128)(2,1)})) %all-reduce.3.cloned.1.call-update) | async-done | bytes 294928 | tf_op jit(solution)/shard_map/psum | solution.py:121
  (90 shorter events, 144.9 us)
Async XLA Ops:
  7.2 20.7 %copy-start = (bf16[768,2304]{1,0:T(8,128)(2,1)S(1)}, bf16[768,2304]{1,0:T(8,128)(2,1)}, u32[]{:S(2)}) copy-start(bf16[768,2304]{1,0:T(8,128)(2,1)} %param.6) | copy-start | bytes 10616836
  19.0 39.8 %all-to-all-start.4 = ((bf16[8,2,12288]{2,1,0:T(2,128)(2,1)}), bf16[8,2,12288]{2,1,0:T(2,128)(2,1)}, u32[]{:S(2)}, u32[]{:S(2)}) async-start(bf16[8,2,12288]{2,1,0:T(2,128)(2,1)} %reshape.211), calls=%async_computation.4 | async-start | bytes 786432 | tf_op jit(solution)/shard_map/all_to_all | solution.py:74
  44.4 4.9 %copy-start.2 = (bf16[512,384]{0,1:T(8,128)(2,1)S(1)}, bf16[512,384]{0,1:T(8,128)(2,1)}, u32[]{:S(2)}) copy-start(bf16[512,384]{0,1:T(8,128)(2,1)} %copy.56) | copy-start | bytes 1179652
  44.4 4.9 %copy-start.6 = (f32[6,512,512]{1,2,0:T(8,128)S(1)}, f32[6,512,512]{1,2,0:T(8,128)}, u32[]{:S(2)}) copy-start(f32[6,512,512]{1,2,0:T(8,128)} %get-tuple-element.29) | copy-start | bytes 18874372
  49.3 1.4 copy-start.3
  58.8 30.6 %all-to-all-start.2 = ((bf16[8,2,12288]{2,1,0:T(2,128)(2,1)}), bf16[8,2,12288]{2,1,0:T(2,128)(2,1)}, u32[]{:S(2)}, u32[]{:S(2)}) async-start(bf16[8,2,12288]{2,1,0:T(2,128)(2,1)} %reshape.215), calls=%async_computation.2 | async-start | bytes 786432 | tf_op jit(solution)/shard_map/all_to_all | solution.py:74
  64.8 4.9 %copy-start.1 = (bf16[1,512,384]{2,1,0:T(8,128)(2,1)S(1)}, bf16[1,512,384]{2,1,0:T(8,128)(2,1)}, u32[]{:S(2)}) copy-start(bf16[1,512,384]{2,1,0:T(8,128)(2,1)} %get-tuple-element.20) | copy-start | bytes 1179652
  89.4 47.6 %all-to-all-start.1 = ((bf16[8,2,12288]{2,1,0:T(2,128)(2,1)}), bf16[8,2,12288]{2,1,0:T(2,128)(2,1)}, u32[]{:S(2)}, u32[]{:S(2)}) async-start(bf16[8,2,12288]{2,1,0:T(2,128)(2,1)} %reshape.217), calls=%async_computation.1 | async-start | bytes 786432 | tf_op jit(solution)/shard_map/all_to_all | solution.py:74
  137.0 22.5 %all-to-all-start = ((bf16[8,2,12288]{2,1,0:T(2,128)(2,1)}), bf16[8,2,12288]{2,1,0:T(2,128)(2,1)}, u32[]{:S(2)}, u32[]{:S(2)}) async-start(bf16[8,2,12288]{2,1,0:T(2,128)(2,1)} %reshape.213), calls=%async_computation | async-start | bytes 786432 | tf_op jit(solution)/shard_map/all_to_all | solution.py:74
  181.0 19.6 %all-to-all-start.3 = ((bf16[8,64,384]{2,1,0:T(8,128)(2,1)}), bf16[8,64,384]{2,1,0:T(8,128)(2,1)}, u32[]{:S(2)}, u32[]{:S(2)}) async-start(bf16[8,64,384]{2,1,0:T(8,128)(2,1)} %reshape.185), calls=%async_computation.3 | async-start | bytes 786432 | tf_op jit(solution)/shard_map/all_to_all | solution.py:96
  200.6 23.4 %all-to-all-start.5 = ((bf16[8,64,384]{2,1,0:T(8,128)(2,1)}), bf16[8,64,384]{2,1,0:T(8,128)(2,1)}, u32[]{:S(2)}, u32[]{:S(2)}) async-start(bf16[8,64,384]{2,1,0:T(8,128)(2,1)} %reshape.191), calls=%async_computation.5 | async-start | bytes 786432 | tf_op jit(solution)/shard_map/all_to_all | solution.py:96
  206.3 76.6 %reduce-scatter.9.cloned.1.call-start = ((), (), s32[]{:S(2)}) async-start(), calls=%async_computation.11 | async-start | bytes 1253376
  223.9 14.1 %all-to-all-start.6 = ((bf16[8,64,384]{2,1,0:T(8,128)(2,1)}), bf16[8,64,384]{2,1,0:T(8,128)(2,1)}, u32[]{:S(2)}, u32[]{:S(2)}) async-start(bf16[8,64,384]{2,1,0:T(8,128)(2,1)} %reshape.194), calls=%async_computation.6 | async-start | bytes 786432 | tf_op jit(solution)/shard_map/all_to_all | solution.py:96
  238.0 13.8 %all-to-all-start.7 = ((bf16[8,64,384]{2,1,0:T(8,128)(2,1)}), bf16[8,64,384]{2,1,0:T(8,128)(2,1)}, u32[]{:S(2)}, u32[]{:S(2)}) async-start(bf16[8,64,384]{2,1,0:T(8,128)(2,1)} %reshape.197), calls=%async_computation.7 | async-start | bytes 786432 | tf_op jit(solution)/shard_map/all_to_all | solution.py:96
  243.7 119.9 %reduce-scatter.7.cloned.1.call-start = ((), (), s32[]{:S(2)}) async-start(), calls=%async_computation.10 | async-start | bytes 3760128
  265.2 176.5 %all-reduce.3.cloned.1.call-start = ((), (), s32[]{:S(2)}) async-start(), calls=%async_computation.12 | async-start | bytes 1572864 | tf_op jit(solution)/shard_map/psum | solution.py:121
  365.6 4.7 %copy-start.4 = (bf16[512,384]{1,0:T(8,128)(2,1)S(1)}, bf16[512,384]{1,0:T(8,128)(2,1)}, u32[]{:S(2)}) copy-start(bf16[512,384]{1,0:T(8,128)(2,1)} %copy.71) | copy-start | bytes 1179652
  365.6 4.7 %copy-start.5 = (bf16[768,768]{1,0:T(8,128)(2,1)S(1)}, bf16[768,768]{1,0:T(8,128)(2,1)}, u32[]{:S(2)}) copy-start(bf16[768,768]{1,0:T(8,128)(2,1)} %param.7) | copy-start | bytes 3538948
Sparse Core Ops, SparseCore 0:
  212.0 70.8 reduce-scatter.8
  287.5 76.0 reduce-scatter.6
  366.9 74.7 all-reduce.2
where the time goes:
time: 459 us; the launch traced here: 452 us
  waiting for transfers between devices  168 us (37%)
  local copies, waits for them, and re-layouts  116 us (25%)
  matrix products  86.9 us (19%)
  starting transfers between devices  47.4 us (10%)
  other arithmetic  19.6 us (4%)
  between operations  14.2 us (3%)
    unnamed x5, waiting for transfers between devices  96.8 us
    psum x1, waiting for transfers between devices, body(): lax.psum(qkv_term.astype(jnp.bfloat16), 'ctx').astype(jnp.float32)  68.7 us
    unnamed x34, local copies, waits for them, and re-layouts  46.2 us
    all_to_all x4, starting transfers between devices, body(): lax.all_to_all(shortened(column_send), 'ctx', split_axis=1, concat_axis=0...  24.2 us
    all_to_all x4, starting transfers between devices, body(): lax.all_to_all(shortened(column_flat), 'ctx', split_axis=0, concat_axis=1...  23.1 us
    unnamed x4, other arithmetic  18.8 us
    dot_general x2, matrix products, attend(): jnp.einsum('ghij,gjhd->gihd', grad_scores, key_part, preferred_element_ty...  17.2 us
    all_to_all x4, local copies, waits for them, and re-layouts, body(): lax.all_to_all(shortened(column_send), 'ctx', split_axis=1, concat_axis=0...  16.7 us
  transfers between devices with their start and end apart: 11, of which 4 were waited for; matrix products, arithmetic and copies ran while one was open for 41% of the time, Pallas kernels for 0%

commit v1 on v0

v1 whole, which is shorter than its diff:
```python
import functools

import jax
import jax.numpy as jnp
from jax import lax
from jax.experimental import pallas as pl
from jax.experimental.pallas import tpu as pltpu
from jax.sharding import PartitionSpec as P

WIDTH = 768
HALF_WIDTH = 384
HEAD_DIM = 64
POSITIONS = 512
ROWS = 8
COLUMNS = 64
PAIR = 128
PAIRS = HALF_WIDTH // PAIR
BLOCK = 256
CHUNK = 16
BF = jnp.bfloat16
F32 = jnp.float32
VMEM_LIMIT = 48 * 1024 * 1024


def dot(a, b):
    return lax.dot_general(a, b, (((1,), (0,)), ((), ())), preferred_element_type=F32)


def dot_nt(a, b):
    return lax.dot_general(a, b, (((1,), (1,)), ((), ())), preferred_element_type=F32)


def dot_tn(a, b):
    return lax.dot_general(a, b, (((0,), (0,)), ((), ())), preferred_element_type=F32)


def half_lanes(array, half):
    lane = lax.broadcasted_iota(jnp.int32, array.shape, array.ndim - 1)
    inside = (lane >= HEAD_DIM) if half else (lane < HEAD_DIM)
    return jnp.where(inside, array, jnp.zeros_like(array))


def probabilities(scores, allowed):
    scores = jnp.where(allowed, scores, -1e30)
    top = jnp.max(scores, axis=-1, keepdims=True)
    weights = jnp.exp(scores - top)
    return weights * (1.0 / jnp.sum(weights, axis=-1, keepdims=True))


def project(x_ref, c_ref, qkv_ref, out_ref, proj, gctx, first):
    x = x_ref[...].reshape(POSITIONS, WIDTH)
    for part in range(3):
        start = part * WIDTH + first
        piece = dot(x, qkv_ref[:, start : start + HALF_WIDTH]).astype(BF)
        if part == 0:
            piece = piece * BF(HEAD_DIM ** -0.5)
        proj[:, part * HALF_WIDTH : (part + 1) * HALF_WIDTH] = piece
    c = c_ref[...].reshape(POSITIONS, WIDTH)
    gctx[...] = dot(c, out_ref[:, first : first + HALF_WIDTH]).astype(BF)


def weight_terms(x_ref, c_ref, grads, ctx, terms, keep_ref, send_ref, core_ref, sems):
    x_t = jnp.transpose(x_ref[...].reshape(POSITIONS, WIDTH))
    for part in range(3):
        res = dot(x_t, grads[:, part * HALF_WIDTH : (part + 1) * HALF_WIDTH]).astype(BF)
        terms[:, :, part] = res.reshape(ROWS, 2, 48, HALF_WIDTH)
    c_t = jnp.transpose(c_ref[...].reshape(POSITIONS, WIDTH))
    terms[:, :, 3] = dot(c_t, ctx[...]).astype(BF).reshape(ROWS, 2, 48, HALF_WIDTH)
    core = core_ref[0]
    keep = pltpu.make_async_copy(terms.at[:, core], keep_ref, sems.at[0])
    send = pltpu.make_async_copy(terms.at[:, 1 - core], send_ref, sems.at[1])
    send.start()
    keep.start()
    send.wait()
    keep.wait()


def row_kernel(
    core_ref, x_ref, c_ref, qkv_ref, out_ref, grads, ctx, keep_ref, send_ref, proj, gctx, probs, dscores, terms, sems
):
    project(x_ref, c_ref, qkv_ref, out_ref, proj, gctx, 0)
    for pair in range(PAIRS):
        lanes = slice(pair * PAIR, (pair + 1) * PAIR)
        k_lanes = slice(HALF_WIDTH + pair * PAIR, HALF_WIDTH + (pair + 1) * PAIR)
        v_lanes = slice(2 * HALF_WIDTH + pair * PAIR, 2 * HALF_WIDTH + (pair + 1) * PAIR)
        keys = [half_lanes(proj[:, k_lanes], half) for half in range(2)]
        values = [half_lanes(proj[:, v_lanes], half) for half in range(2)]
        for start in range(0, POSITIONS, BLOCK):
            stop = start + BLOCK
            query = proj[start:stop, lanes]
            grad = gctx[start:stop, lanes]
            allowed = lax.broadcasted_iota(jnp.int32, (BLOCK, stop), 1) <= (
                lax.broadcasted_iota(jnp.int32, (BLOCK, stop), 0) + start
            )
            outs, dqs = [], []
            for half in range(2):
                key, value = keys[half][:stop], values[half][:stop]
                weights = probabilities(dot_nt(query, key), allowed)
                rounded = weights.astype(BF)
                probs[half, start:stop, :stop] = rounded
                outs.append(dot(rounded, value))
                grad_weights = dot_nt(grad, value)
                delta = jnp.sum(weights * grad_weights, axis=-1, keepdims=True)
                ds = (weights * (grad_weights - delta)).astype(BF)
                dscores[half, start:stop, :stop] = ds
                dqs.append(dot(ds, key))
            ctx[start:stop, lanes] = (outs[0] + outs[1]).astype(BF)
            grads[start:stop, lanes] = ((dqs[0] + dqs[1]) * (HEAD_DIM ** -0.5)).astype(BF)
        queries = [half_lanes(proj[:, lanes], half) for half in range(2)]
        grad_parts = [half_lanes(gctx[:, lanes], half) for half in range(2)]
        for start in range(0, POSITIONS, BLOCK):
            stop = start + BLOCK
            dk = sum(dot_tn(dscores[half, start:, start:stop], queries[half][start:]) for half in range(2))
            dv = sum(dot_tn(probs[half, start:, start:stop], grad_parts[half][start:]) for half in range(2))
            grads[start:stop, k_lanes] = dk.astype(BF)
            grads[start:stop, v_lanes] = dv.astype(BF)
    weight_terms(x_ref, c_ref, grads, ctx, terms, keep_ref, send_ref, core_ref, sems)


def column_kernel(
    core_ref, x_ref, c_ref, qkv_ref, out_ref, grads, ctx, keep_ref, send_ref, proj, gctx, terms, sems
):
    project(x_ref, c_ref, qkv_ref, out_ref, proj, gctx, HALF_WIDTH)
    size = ROWS * CHUNK
    chunks = COLUMNS // CHUNK
    line = lax.broadcasted_iota(jnp.int32, (size, size), 0)
    across = lax.broadcasted_iota(jnp.int32, (size, size), 1)
    allowed = ((line % CHUNK) == (across % CHUNK)) & (across <= line)
    allowed = jnp.concatenate([allowed.astype(F32)] * chunks, axis=0) > 0

    def gather(ref, base):
        whole = ref[:, base : base + PAIR].reshape(ROWS, COLUMNS, PAIR)
        return [
            whole[:, t * CHUNK : (t + 1) * CHUNK].reshape(size, PAIR) for t in range(chunks)
        ]

    def scatter(ref, base, pieces):
        whole = jnp.concatenate([p.reshape(ROWS, CHUNK, PAIR) for p in pieces], axis=1)
        ref[:, base : base + PAIR] = whole.reshape(POSITIONS, PAIR)

    for pair in range(PAIRS):
        base = pair * PAIR
        query, key, value = [gather(proj, part * HALF_WIDTH + base) for part in range(3)]
        grad = gather(gctx, base)
        outs, dqs, dks, dvs = [], [], [], []
        for half in range(2):
            key_h = [half_lanes(t, half) for t in key]
            value_h = [half_lanes(t, half) for t in value]
            query_h = [half_lanes(t, half) for t in query]
            grad_h = [half_lanes(t, half) for t in grad]
            scores = jnp.concatenate([dot_nt(a, b) for a, b in zip(query, key_h)], axis=0)
            grad_weights = jnp.concatenate([dot_nt(a, b) for a, b in zip(grad, value_h)], axis=0)
            weights = probabilities(scores, allowed)
            rounded = weights.astype(BF)
            delta = jnp.sum(weights * grad_weights, axis=-1, keepdims=True)
            ds = (weights * (grad_weights - delta)).astype(BF)
            rounded = [rounded[t * size : (t + 1) * size] for t in range(chunks)]
            ds = [ds[t * size : (t + 1) * size] for t in range(chunks)]
            outs.append([dot(a, b) for a, b in zip(rounded, value_h)])
            dqs.append([dot(a, b) for a, b in zip(ds, key_h)])
            dks.append([dot_tn(a, b) for a, b in zip(ds, query_h)])
            dvs.append([dot_tn(a, b) for a, b in zip(rounded, grad_h)])
        scatter(ctx, base, [(a + b).astype(BF) for a, b in zip(*outs)])
        scatter(grads, base, [((a + b) * (HEAD_DIM ** -0.5)).astype(BF) for a, b in zip(*dqs)])
        scatter(grads, HALF_WIDTH + base, [(a + b).astype(BF) for a, b in zip(*dks)])
        scatter(grads, 2 * HALF_WIDTH + base, [(a + b).astype(BF) for a, b in zip(*dvs)])
    weight_terms(x_ref, c_ref, grads, ctx, terms, keep_ref, send_ref, core_ref, sems)


def return_kernel(grads, ctx, qkv_ref, back_ref):
    total = sum(
        dot_nt(
            grads[:, part * HALF_WIDTH : (part + 1) * HALF_WIDTH],
            qkv_ref[:, part * WIDTH + HALF_WIDTH : (part + 1) * WIDTH],
        )
        for part in range(3)
    )
    back_ref[:, :WIDTH] = total.astype(BF)
    back_ref[:, WIDTH:] = ctx[...]


def final_kernel(grads, ctx, back_ref, qkv_ref, out_ref, attention_ref, normed_ref):
    total = back_ref[:, :WIDTH].astype(F32)
    for part in range(3):
        total += dot_nt(
            grads[:, part * HALF_WIDTH : (part + 1) * HALF_WIDTH],
            qkv_ref[:, part * WIDTH : part * WIDTH + HALF_WIDTH],
        )
    normed_ref[...] = total.astype(BF)
    attention_ref[...] = (
        dot_nt(ctx[...], out_ref[:, :HALF_WIDTH]) + dot_nt(back_ref[:, WIDTH:], out_ref[:, HALF_WIDTH:])
    ).astype(BF)


VMEM = pl.BlockSpec(memory_space=pltpu.VMEM)


def cost(flops, transcendentals=0):
    return pl.CostEstimate(flops=flops, bytes_accessed=8 * 2 ** 20, transcendentals=transcendentals)


def sublayer(kernel, scratch, core, x, c, qkv_weight, out_weight):
    return pl.pallas_call(
        kernel,
        out_shape=(
            jax.ShapeDtypeStruct((POSITIONS, 3 * HALF_WIDTH), BF),
            jax.ShapeDtypeStruct((POSITIONS, HALF_WIDTH), BF),
            jax.ShapeDtypeStruct((ROWS, 4, 48, HALF_WIDTH), BF),
            jax.ShapeDtypeStruct((ROWS, 4, 48, HALF_WIDTH), BF),
        ),
        in_specs=[pl.BlockSpec(memory_space=pltpu.SMEM)] + [VMEM] * 4,
        out_specs=(VMEM, VMEM, pl.BlockSpec(memory_space=pl.ANY), pl.BlockSpec(memory_space=pl.ANY)),
        scratch_shapes=[
            pltpu.VMEM((POSITIONS, 3 * HALF_WIDTH), BF),
            pltpu.VMEM((POSITIONS, HALF_WIDTH), BF),
            *scratch,
            pltpu.VMEM((ROWS, 2, 4, 48, HALF_WIDTH), BF),
            pltpu.SemaphoreType.DMA((2,)),
        ],
        compiler_params=pltpu.CompilerParams(vmem_limit_bytes=VMEM_LIMIT),
        cost_estimate=cost(4 * 10 ** 9),
    )(core, x, c, qkv_weight, out_weight)


def swap(part, axis, groups=None):
    return lax.all_to_all(part, axis, split_axis=0, concat_axis=0, tiled=True, axis_index_groups=groups)


def other_groups():
    def flat(x, z_hi, core, z_lo, y):
        return ((x * 2 + z_hi) * 2 + core) * 8 + z_lo * 4 + y

    return [
        [flat(x, z_hi, core, z_lo, y) for x in range(4) for z_hi in range(2) for y in range(4) for z_lo in range(2)]
        for core in range(2)
    ]


def summed(keep, send):
    received = lax.ppermute(send, "dp", [(i, i ^ 1) for i in range(16)])
    both = (keep.astype(F32) + received.astype(F32)).astype(BF)
    pieces = swap(both.reshape(64, 24, HALF_WIDTH), ("dp", "ctx"), other_groups())
    return jnp.sum(pieces.astype(F32), axis=0).astype(BF)


def body(normed, cotangent, qkv_weight, out_weight):
    x, c = normed[0], cotangent[0]
    core = (lax.axis_index("dp") % 2).reshape(1)
    both = jnp.concatenate([x, c], axis=1).reshape(ROWS, COLUMNS, 2 * WIDTH)
    moved = swap(both, "ctx").reshape(POSITIONS, 2 * WIDTH)
    x_col, c_col = moved[:, :WIDTH], moved[:, WIDTH:]
    grads_row, ctx_row, keep_row, send_row = sublayer(
        row_kernel,
        [pltpu.VMEM((2, POSITIONS, POSITIONS), BF)] * 2,
        core, x, c, qkv_weight, out_weight,
    )
    sum_row = summed(keep_row, send_row)
    grads_col, ctx_col, keep_col, send_col = sublayer(
        column_kernel, [], core, x_col, c_col, qkv_weight, out_weight
    )
    sum_col = summed(keep_col, send_col)
    back = pl.pallas_call(
        return_kernel,
        out_shape=jax.ShapeDtypeStruct((POSITIONS, WIDTH + HALF_WIDTH), BF),
        in_specs=[VMEM] * 3,
        out_specs=VMEM,
        compiler_params=pltpu.CompilerParams(vmem_limit_bytes=VMEM_LIMIT),
        cost_estimate=cost(10 ** 9),
    )(grads_col, ctx_col, qkv_weight)
    back = swap(back.reshape(ROWS, COLUMNS, WIDTH + HALF_WIDTH), "ctx").reshape(POSITIONS, WIDTH + HALF_WIDTH)
    attention_out, normed_grad = pl.pallas_call(
        final_kernel,
        out_shape=(jax.ShapeDtypeStruct((POSITIONS, WIDTH), BF),) * 2,
        in_specs=[VMEM] * 5,
        out_specs=(VMEM, VMEM),
        compiler_params=pltpu.CompilerParams(vmem_limit_bytes=VMEM_LIMIT),
        cost_estimate=cost(2 * 10 ** 9),
    )(grads_row, ctx_row, back, qkv_weight, out_weight)
    own = jnp.stack([sum_row, sum_col])
    whole = swap(jnp.broadcast_to(own[None], (8,) + own.shape), "ctx")
    factor = (lax.axis_size("dp") * lax.axis_size("ctx") * POSITIONS) ** (-0.5)
    whole = whole.reshape(2, 4, 2, 24, HALF_WIDTH).astype(F32) * factor
    whole = jnp.transpose(whole, (0, 3, 1, 2, 4)).reshape(48, 8 * HALF_WIDTH)
    return (attention_out[None], normed_grad[None], whole[:, : 3 * WIDTH], whole[:, 3 * WIDTH :])


def solution(mesh):
    placed = (P("dp", "ctx", None), P("dp", "ctx", None), P(), P())
    return jax.shard_map(
        body,
        mesh=mesh,
        in_specs=placed,
        out_specs=(P("dp", "ctx", None), P("dp", "ctx", None), P("dp", None), P("dp", None)),
        check_vma=False,
    )
```

time: 459 us -> 136 us (0.30); the launches traced: 452 us -> 135 us
  waiting for transfers between devices: 168 us -> 49.8 us
  local copies, waits for them, and re-layouts: 116 us -> 9.14 us
  matrix products: 86.9 us -> 0 us
  Pallas kernels: 0 us -> 33.7 us
  starting transfers between devices: 47.4 us -> 28.3 us
  between operations: 14.2 us -> 0.81 us
  other arithmetic: 19.6 us -> 13.6 us
    unnamed x5 -> x0, waiting for transfers between devices: 96.8 us -> none
    dot_general x16 -> x0, matrix products: 75.6 us -> none  [the longest x2 17.2 us: attend(): jnp.einsum('ghij,gjhd->gihd', grad_scores, key_part, preferred_element_ty...]
    psum x1 -> x0, waiting for transfers between devices: 68.7 us -> none  [body(): lax.psum(qkv_term.astype(jnp.bfloat16), 'ctx').astype(jnp.float32)]
    all_to_all x8 -> x5, waiting for transfers between devices: 2.59 us -> 49.8 us  [swap(): lax.all_to_all(part, axis, split_axis=0, concat_axis=0, tiled=True, axis_...]
    unnamed x34 -> x22, local copies, waits for them, and re-layouts: 46.2 us -> 3.92 us
    reshape x17 -> x1, local copies, waits for them, and re-layouts: 35.3 us -> 0.47 us  [body(): whole = jnp.transpose(whole, (0, 3, 1, 2, 4)).reshape(48, 8 * HALF_WIDTH)]
    pallas_call x0 -> x4, Pallas kernels: none -> 33.7 us  [the longest x2 24.1 us: sublayer(): pl.pallas_call(kernel, out_shape=(jax.ShapeDtypeStruct((POSITIONS, 3 * HA...]
    all_to_all x8 -> x5, starting transfers between devices: 47.3 us -> 28.3 us  [swap(): lax.all_to_all(part, axis, split_axis=0, concat_axis=0, tiled=True, axis_...]
  transfers between devices with their start and end apart: 11 -> 7, of which waited for: 4 -> 5; matrix products, arithmetic and copies ran while one was open for 41% -> 8% of each run, Pallas kernels for 0% -> 25%
where the time goes in v1:
time: 136 us; the launch traced here: 135 us
  waiting for transfers between devices  49.8 us (37%)
  Pallas kernels  33.7 us (25%)
  starting transfers between devices  28.3 us (21%)
  other arithmetic  13.6 us (10%)
  local copies, waits for them, and re-layouts  9.14 us (7%)
    all_to_all x5, waiting for transfers between devices, swap(): lax.all_to_all(part, axis, split_axis=0, concat_axis=0, tiled=True, axis_...  49.8 us
    all_to_all x5, starting transfers between devices, swap(): lax.all_to_all(part, axis, split_axis=0, concat_axis=0, tiled=True, axis_...  28.3 us
    pallas_call x2, Pallas kernels, sublayer(): pl.pallas_call(kernel, out_shape=(jax.ShapeDtypeStruct((POSITIONS, 3 * HA...  24.1 us
    convert_element_type x2, other arithmetic, summed(): both = (keep.astype(F32) + received.astype(F32)).astype(BF)  5.65 us
    pallas_call x1, Pallas kernels, body(): pl.pallas_call(final_kernel, out_shape=(jax.ShapeDtypeStruct((POSITIONS,...  5.23 us
    pallas_call x1, Pallas kernels, body(): pl.pallas_call(return_kernel, out_shape=jax.ShapeDtypeStruct((POSITIONS,...  4.44 us
    unnamed x22, local copies, waits for them, and re-layouts  3.92 us
    reduce_sum x2, other arithmetic, summed(): return jnp.sum(pieces.astype(F32), axis=0).astype(BF)  2.97 us
  transfers between devices with their start and end apart: 7, of which 5 were waited for; matrix products, arithmetic and copies ran while one was open for 8% of the time, Pallas kernels for 25%

profile of v1, /device:TPU:0, one launch (start us, length us, event | category | flops | bytes accessed | tf_op | source)
XLA Modules:
  0.0 135.4 jit_solution(13700479679023198049)
XLA Ops:
  0.6 2.6 %pad_maximum_fusion = bf16[8,64,1536]{2,1,0:T(8,128)(2,1)} fusion(bf16[8,64,768]{2,1,0:T(8,128)(2,1)} %bitcast.20, bf16[8,64,768]{2,1,0:T(8,128)(2,1)} %bitcast.18), kind=kLoop, calls=%fused_computation.2 | loop fusion | flops 3145728 | bytes 3145728 | tf_op jit(solution)/shard_map/concatenate | solution.py:249
  3.3 6.0 %all-to-all-start = ((bf16[8,64,1536]{2,1,0:T(8,128)(2,1)}), bf16[8,64,1536]{2,1,0:T(8,128)(2,1)}, u32[]{:S(2)}, u32[]{:S(2)}) async-start(bf16[8,64,1536]{2,1,0:T(8,128)(2,1)} %pad_maximum_fusion), calls=%async_computation | async-start | bytes 3145728 | tf_op jit(solution)/shard_map/all_to_all | solution.py:226
  9.3 1.1 copy-done.4
  10.4 13.8 %shard_map.75 = (bf16[512,1152]{1,0:T(8,128)(2,1)S(1)}, bf16[512,384]{1,0:T(8,128)(2,1)S(1)}, bf16[8,4,48,384]{3,2,1,0:T(8,128)(2,1)S(1)}, bf16[8,4,48,384]{3,2,1,0:T(8,128)(2,1)}) custom-call(s32[1]{0:T(128)} %bitcast.core_ref, bf16[512,768]{1,0:T(8,128)(2,1)S(1)} %bitcast.19, bf16[512,768]{1,0:T(8,128)(2,1)S(1)} %bitcast.21, bf16[768,2304]{1,0:T(8,128)(2,1)} %qkv_ref.7, ...), custom_call_target="tpu_custom_call" | custom-call | flops 4000000000 | bytes 8388608 | tf_op jit(solution)/shard_map/pallas_call | solution.py:203
  25.0 5.7 %all-to-all-done = bf16[8,64,1536]{2,1,0:T(8,128)(2,1)} async-done(((bf16[8,64,1536]{2,1,0:T(8,128)(2,1)}), bf16[8,64,1536]{2,1,0:T(8,128)(2,1)}, u32[]{:S(2)}, u32[]{:S(2)}) %all-to-all-start) | async-done | bytes 1572896 | tf_op jit(solution)/shard_map/all_to_all | solution.py:226
  30.7 1.5 %fusion = (bf16[512,768]{1,0:T(8,128)(2,1)S(1)}, bf16[512,768]{1,0:T(8,128)(2,1)S(1)}) fusion(bf16[512,1536]{1,0:T(8,128)(2,1)} %bitcast.5), kind=kLoop, calls=%fused_computation.5 | loop fusion | bytes 3145728 | tf_op jit(solution)/shard_map/slice | solution.py:251
  32.2 10.3 %shard_map.76 = (bf16[512,1152]{1,0:T(8,128)(2,1)S(1)}, bf16[512,384]{1,0:T(8,128)(2,1)S(1)}, bf16[8,4,48,384]{3,2,1,0:T(8,128)(2,1)S(1)}, bf16[8,4,48,384]{3,2,1,0:T(8,128)(2,1)}) custom-call(s32[1]{0:T(128)} %bitcast.core_ref, bf16[512,768]{1,0:T(8,128)(2,1)S(1)} %get-tuple-element.25.x_ref, bf16[512,768]{1,0:T(8,128)(2,1)S(1)} %get-tuple-element.24.c_ref, ...), custom_call_target="tpu_custom_call" | custom-call | flops 4000000000 | bytes 8388608 | tf_op jit(solution)/shard_map/pallas_call | solution.py:203
  42.6 3.1 %add_convert_fusion.1 = bf16[8,4,48,384]{3,2,1,0:T(8,128)(2,1)} fusion(bf16[8,4,48,384]{3,2,1,0:T(8,128)(2,1)} %collective-permute-done, bf16[8,4,48,384]{3,2,1,0:T(8,128)(2,1)S(1)} %get-tuple-element.20), kind=kLoop, calls=%fused_computation.1 | loop fusion | flops 2359296 | bytes 3538944 | tf_op jit(solution)/shard_map/convert_element_type | solution.py:241
  45.7 8.6 %all-to-all-start.2 = ((bf16[64,24,384]{2,1,0:T(8,128)(2,1)}), bf16[64,24,384]{2,1,0:T(8,128)(2,1)S(1)}, u32[]{:S(2)}, u32[]{:S(2)}) async-start(bf16[64,24,384]{2,1,0:T(8,128)(2,1)} %bitcast.23), calls=%async_computation.2 | async-start | bytes 2359296 | tf_op jit(solution)/shard_map/all_to_all | solution.py:226
  54.3 2.6 %add_convert_fusion = bf16[8,4,48,384]{3,2,1,0:T(8,128)(2,1)} fusion(bf16[8,4,48,384]{3,2,1,0:T(8,128)(2,1)} %collective-permute-done.1, bf16[8,4,48,384]{3,2,1,0:T(8,128)(2,1)S(1)} %get-tuple-element.22), kind=kLoop, calls=%fused_computation | loop fusion | flops 2359296 | bytes 3538944 | tf_op jit(solution)/shard_map/convert_element_type | solution.py:241
  56.9 17.8 %all-to-all-done.2 = bf16[64,24,384]{2,1,0:T(8,128)(2,1)S(1)} async-done(((bf16[64,24,384]{2,1,0:T(8,128)(2,1)}), bf16[64,24,384]{2,1,0:T(8,128)(2,1)S(1)}, u32[]{:S(2)}, u32[]{:S(2)}) %all-to-all-start.2) | async-done | bytes 1179680 | tf_op jit(solution)/shard_map/all_to_all | solution.py:226
  74.7 1.0 copy-done.9
  75.8 5.6 %all-to-all-start.3 = ((bf16[64,24,384]{2,1,0:T(8,128)(2,1)}), bf16[64,24,384]{2,1,0:T(8,128)(2,1)}, u32[]{:S(2)}, u32[]{:S(2)}) async-start(bf16[64,24,384]{2,1,0:T(8,128)(2,1)} %bitcast.22), calls=%async_computation.3 | async-start | bytes 2359296 | tf_op jit(solution)/shard_map/all_to_all | solution.py:226
  81.4 4.4 %shard_map.77 = bf16[512,1152]{1,0:T(8,128)(2,1)} custom-call(bf16[512,1152]{1,0:T(8,128)(2,1)S(1)} %copy-done.2, bf16[512,384]{1,0:T(8,128)(2,1)S(1)} %copy-done.8, bf16[768,2304]{1,0:T(8,128)(2,1)} %qkv_ref.7), custom_call_target="tpu_custom_call" | custom-call | flops 1000000000 | bytes 8388608 | tf_op jit(solution)/shard_map/pallas_call | solution.py:262
  85.9 14.5 %all-to-all-done.3 = bf16[64,24,384]{2,1,0:T(8,128)(2,1)} async-done(((bf16[64,24,384]{2,1,0:T(8,128)(2,1)}), bf16[64,24,384]{2,1,0:T(8,128)(2,1)}, u32[]{:S(2)}, u32[]{:S(2)}) %all-to-all-start.3) | async-done | bytes 1179680 | tf_op jit(solution)/shard_map/all_to_all | solution.py:226
  100.4 3.7 %all-to-all-start.1 = ((bf16[8,64,1152]{2,1,0:T(8,128)(2,1)}), bf16[8,64,1152]{2,1,0:T(8,128)(2,1)S(1)}, u32[]{:S(2)}, u32[]{:S(2)}) async-start(bf16[8,64,1152]{2,1,0:T(8,128)(2,1)} %bitcast.6), calls=%async_computation.1 | async-start | bytes 2359296 | tf_op jit(solution)/shard_map/all_to_all | solution.py:226
  104.9 2.2 %reduce_sum.25 = bf16[24,384]{1,0:T(8,128)(2,1)} reduce(bf16[64,24,384]{2,1,0:T(8,128)(2,1)} %all-to-all-done.3, bf16[]{:T(256)} %constant.23.clone.1), dimensions={0}, to_apply=%region_1.2 | reduce | flops 580608 | bytes 1198082 | tf_op jit(solution)/shard_map/reduce_sum | solution.py:243
  107.1 1.4 %pad_maximum_fusion.1 = bf16[2,24,384]{2,1,0:T(8,128)(2,1)} fusion(bf16[1,24,384]{2,1,0:T(8,128)(2,1)} %bitcast.26, bf16[1,24,384]{2,1,0:T(8,128)(2,1)} %bitcast.25), kind=kLoop, calls=%fused_computation.4 | loop fusion | flops 18432 | bytes 73728 | tf_op jit(solution)/shard_map/stack | solution.py:279
  108.4 10.5 %all-to-all-done.1 = bf16[8,64,1152]{2,1,0:T(8,128)(2,1)S(1)} async-done(((bf16[8,64,1152]{2,1,0:T(8,128)(2,1)}), bf16[8,64,1152]{2,1,0:T(8,128)(2,1)S(1)}, u32[]{:S(2)}, u32[]{:S(2)}) %all-to-all-start.1) | async-done | bytes 1179680 | tf_op jit(solution)/shard_map/all_to_all | solution.py:226
  119.0 1.5 %broadcast_in_dim.14 = bf16[8,2,24,384]{3,2,1,0:T(8,128)(2,1)} broadcast(bf16[2,24,384]{2,1,0:T(8,128)(2,1)} %pad_maximum_fusion.1), dimensions={1,2,3} | broadcast | bytes 331776 | tf_op jit(solution)/shard_map/broadcast_in_dim | solution.py:280
  120.5 4.3 %all-to-all-start.4 = ((bf16[8,2,24,384]{3,2,1,0:T(8,128)(2,1)}), bf16[8,2,24,384]{3,2,1,0:T(8,128)(2,1)}, u32[]{:S(2)}, u32[]{:S(2)}) async-start(bf16[8,2,24,384]{3,2,1,0:T(8,128)(2,1)} %broadcast_in_dim.14), calls=%async_computation.4 | async-start | bytes 589824 | tf_op jit(solution)/shard_map/all_to_all | solution.py:226
  125.8 5.2 %shard_map.78 = (bf16[512,768]{1,0:T(8,128)(2,1)}, bf16[512,768]{1,0:T(8,128)(2,1)}) custom-call(bf16[512,1152]{1,0:T(8,128)(2,1)S(1)} %get-tuple-element.14.grads, bf16[512,384]{1,0:T(8,128)(2,1)S(1)} %copy-done.6, bf16[512,1152]{1,0:T(8,128)(2,1)S(1)} %bitcast.17, bf16[768,2304]{1,0:T(8,128)(2,1)} %qkv_ref.7, bf16[768,768]{1,0:T(8,128)(2,1)S(1)} %copy-done), custom_call_target="tpu_custom_call" | custom-call | flops 2000000000 | bytes 8388608 | tf_op jit(solution)/shard_map/pallas_call | solution.py:271
  131.0 1.1 all-to-all-done.4
  132.2 1.0 convert_multiply_fusion
  (29 shorter events, 4.9 us)
Async XLA Ops:
  3.2 6.0 %copy-start.3 = (bf16[1,512,768]{2,1,0:T(8,128)(2,1)S(1)}, bf16[1,512,768]{2,1,0:T(8,128)(2,1)}, u32[]{:S(2)}) copy-start(bf16[1,512,768]{2,1,0:T(8,128)(2,1)} %param.4) | copy-start | bytes 2359300
  3.3 27.5 %all-to-all-start = ((bf16[8,64,1536]{2,1,0:T(8,128)(2,1)}), bf16[8,64,1536]{2,1,0:T(8,128)(2,1)}, u32[]{:S(2)}, u32[]{:S(2)}) async-start(bf16[8,64,1536]{2,1,0:T(8,128)(2,1)} %pad_maximum_fusion), calls=%async_computation | async-start | bytes 3145728 | tf_op jit(solution)/shard_map/all_to_all | solution.py:226
  9.3 1.1 copy-start.4
  24.2 0.7 copy-start.5
  25.0 17.6 %collective-permute-start = (bf16[8,4,48,384]{3,2,1,0:T(8,128)(2,1)}, bf16[8,4,48,384]{3,2,1,0:T(8,128)(2,1)}, u32[]{:S(2)}, u32[]{:S(2)}) collective-permute-start(bf16[8,4,48,384]{3,2,1,0:T(8,128)(2,1)} %get-tuple-element.21), channel_id=1, source_target_pairs={{0,8},{8,0},{16,24},{24,16},{32,40},{40,32},{48,56},{56,48},{64,72... | collective-permute-start | bytes 3538952 | tf_op jit(solution)/shard_map/ppermute | solution.py:240
  42.5 3.2 %copy-start.1 = (bf16[512,1152]{1,0:T(8,128)(2,1)}, bf16[512,1152]{1,0:T(8,128)(2,1)S(1)}, u32[]{:S(2)}) copy-start(bf16[512,1152]{1,0:T(8,128)(2,1)S(1)} %get-tuple-element.16.grads) | copy-start | bytes 3538948
  42.5 3.2 %copy-start.7 = (bf16[512,384]{1,0:T(8,128)(2,1)}, bf16[512,384]{1,0:T(8,128)(2,1)S(1)}, u32[]{:S(2)}) copy-start(bf16[512,384]{1,0:T(8,128)(2,1)S(1)} %get-tuple-element.17.ctx) | copy-start | bytes 1179652
  42.5 11.8 %collective-permute-start.1 = (bf16[8,4,48,384]{3,2,1,0:T(8,128)(2,1)}, bf16[8,4,48,384]{3,2,1,0:T(8,128)(2,1)}, u32[]{:S(2)}, u32[]{:S(2)}) collective-permute-start(bf16[8,4,48,384]{3,2,1,0:T(8,128)(2,1)} %get-tuple-element.23), channel_id=1, source_target_pairs={{0,8},{8,0},{16,24},{24,16},{32,40},{40,32},{48,56},{56,48},{64,72... | collective-permute-start | bytes 3538952 | tf_op jit(solution)/shard_map/ppermute | solution.py:240
  45.7 29.0 %all-to-all-start.2 = ((bf16[64,24,384]{2,1,0:T(8,128)(2,1)}), bf16[64,24,384]{2,1,0:T(8,128)(2,1)S(1)}, u32[]{:S(2)}, u32[]{:S(2)}) async-start(bf16[64,24,384]{2,1,0:T(8,128)(2,1)} %bitcast.23), calls=%async_computation.2 | async-start | bytes 2359296 | tf_op jit(solution)/shard_map/all_to_all | solution.py:226
  74.7 1.0 copy-start.9
  75.8 5.6 %copy-start.2 = (bf16[512,1152]{1,0:T(8,128)(2,1)S(1)}, bf16[512,1152]{1,0:T(8,128)(2,1)}, u32[]{:S(2)}) copy-start(bf16[512,1152]{1,0:T(8,128)(2,1)} %copy-done.1) | copy-start | bytes 3538948
  75.8 5.6 %copy-start.8 = (bf16[512,384]{1,0:T(8,128)(2,1)S(1)}, bf16[512,384]{1,0:T(8,128)(2,1)}, u32[]{:S(2)}) copy-start(bf16[512,384]{1,0:T(8,128)(2,1)} %copy-done.7) | copy-start | bytes 1179652
  75.8 24.6 %all-to-all-start.3 = ((bf16[64,24,384]{2,1,0:T(8,128)(2,1)}), bf16[64,24,384]{2,1,0:T(8,128)(2,1)}, u32[]{:S(2)}, u32[]{:S(2)}) async-start(bf16[64,24,384]{2,1,0:T(8,128)(2,1)} %bitcast.22), calls=%async_computation.3 | async-start | bytes 2359296 | tf_op jit(solution)/shard_map/all_to_all | solution.py:226
  100.4 3.7 %copy-start.10 = (bf16[64,24,384]{2,1,0:T(8,128)(2,1)S(1)}, bf16[64,24,384]{2,1,0:T(8,128)(2,1)}, u32[]{:S(2)}) copy-start(bf16[64,24,384]{2,1,0:T(8,128)(2,1)} %copy-done.9) | copy-start | bytes 3538948
  100.4 18.6 %all-to-all-start.1 = ((bf16[8,64,1152]{2,1,0:T(8,128)(2,1)}), bf16[8,64,1152]{2,1,0:T(8,128)(2,1)S(1)}, u32[]{:S(2)}, u32[]{:S(2)}) async-start(bf16[8,64,1152]{2,1,0:T(8,128)(2,1)} %bitcast.6), calls=%async_computation.1 | async-start | bytes 2359296 | tf_op jit(solution)/shard_map/all_to_all | solution.py:226
  104.9 19.9 %copy-start = (bf16[768,768]{1,0:T(8,128)(2,1)S(1)}, bf16[768,768]{1,0:T(8,128)(2,1)}, u32[]{:S(2)}) copy-start(bf16[768,768]{1,0:T(8,128)(2,1)} %out_ref.5) | copy-start | bytes 3538948
  120.5 11.7 %all-to-all-start.4 = ((bf16[8,2,24,384]{3,2,1,0:T(8,128)(2,1)}), bf16[8,2,24,384]{3,2,1,0:T(8,128)(2,1)}, u32[]{:S(2)}, u32[]{:S(2)}) async-start(bf16[8,2,24,384]{3,2,1,0:T(8,128)(2,1)} %broadcast_in_dim.14), calls=%async_computation.4 | async-start | bytes 589824 | tf_op jit(solution)/shard_map/all_to_all | solution.py:226
  124.8 1.0 copy-start.6

commit v2 on v1

v2 whole, which is shorter than its diff:
```python
import functools

import jax
import jax.numpy as jnp
from jax import lax
from jax.experimental import pallas as pl
from jax.experimental.pallas import tpu as pltpu
from jax.sharding import PartitionSpec as P

WIDTH = 768
HALF_WIDTH = 384
HEAD_DIM = 64
POSITIONS = 512
ROWS = 8
COLUMNS = 64
PAIR = 128
PAIRS = HALF_WIDTH // PAIR
BLOCK = 256
CHUNK = 16
BF = jnp.bfloat16
F32 = jnp.float32
MIB = 1024 * 1024


def dot(a, b):
    return lax.dot_general(a, b, (((1,), (0,)), ((), ())), preferred_element_type=F32)


def dot_nt(a, b):
    return lax.dot_general(a, b, (((1,), (1,)), ((), ())), preferred_element_type=F32)


def dot_tn(a, b):
    return lax.dot_general(a, b, (((0,), (0,)), ((), ())), preferred_element_type=F32)


def half_lanes(array, half):
    lane = lax.broadcasted_iota(jnp.int32, array.shape, array.ndim - 1)
    inside = (lane >= HEAD_DIM) if half else (lane < HEAD_DIM)
    return jnp.where(inside, array, jnp.zeros_like(array))


def probabilities(scores, allowed):
    scores = jnp.where(allowed, scores, -1e30)
    top = jnp.max(scores, axis=-1, keepdims=True)
    weights = jnp.exp(scores - top)
    return weights * (1.0 / jnp.sum(weights, axis=-1, keepdims=True))


def load(x_hbm, c_hbm, qkv_hbm, out_hbm, x, c, w_qkv, w_out, sems, first):
    copies = [pltpu.make_async_copy(x_hbm, x, sems.at[0])]
    for part in range(3):
        columns = pl.ds(part * WIDTH + first, HALF_WIDTH)
        place = pl.ds(part * HALF_WIDTH, HALF_WIDTH)
        copies.append(pltpu.make_async_copy(qkv_hbm.at[:, columns], w_qkv.at[:, place], sems.at[1 + part]))
    copies.append(pltpu.make_async_copy(c_hbm, c, sems.at[4]))
    copies.append(pltpu.make_async_copy(out_hbm.at[:, pl.ds(first, HALF_WIDTH)], w_out, sems.at[5]))
    for copy in copies:
        copy.start()
    return copies


def project(copies, x, c, w_qkv, w_out, proj, gctx):
    for copy in copies[:4]:
        copy.wait()
    for part, piece in enumerate(jnp.split(dot(x[...].reshape(POSITIONS, WIDTH), w_qkv[...]), 3, axis=1)):
        piece = piece.astype(BF)
        if part == 0:
            piece = piece * BF(HEAD_DIM ** -0.5)
        proj[:, part * HALF_WIDTH : (part + 1) * HALF_WIDTH] = piece
    copies[4].wait()
    copies[5].wait()
    gctx[...] = dot(c[...].reshape(POSITIONS, WIDTH), w_out[...]).astype(BF)


def weight_terms(x, c, grads, ctx, terms, targets, sems, extra):
    copies = []
    for part in range(4):
        for index, (place, target) in enumerate(targets):
            copies.append(
                pltpu.make_async_copy(terms.at[:, place, part], target.at[:, part], sems.at[2 + 4 * index + part])
            )
    extra = start_all(
        [pltpu.make_async_copy(source, target, sems.at[index]) for index, (source, target) in enumerate(extra)]
    )
    x_t = jnp.transpose(x[...].reshape(POSITIONS, WIDTH))
    for part in range(3):
        res = dot(x_t, grads[:, part * HALF_WIDTH : (part + 1) * HALF_WIDTH]).astype(BF)
        terms[:, :, part] = res.reshape(ROWS, 2, 48, HALF_WIDTH)
        copies[2 * part].start()
        copies[2 * part + 1].start()
    c_t = jnp.transpose(c[...].reshape(POSITIONS, WIDTH))
    terms[:, :, 3] = dot(c_t, ctx[...]).astype(BF).reshape(ROWS, 2, 48, HALF_WIDTH)
    copies[6].start()
    copies[7].start()
    wait_all(extra + copies)


def row_kernel(
    core_ref, x_hbm, c_hbm, qkv_hbm, out_hbm, grads_hbm, ctx_hbm, keep_hbm, send_hbm,
    x, c, w_qkv, w_out, proj, gctx, grads, ctx, terms, sems, probs, dscores,
):
    copies = load(x_hbm, c_hbm, qkv_hbm, out_hbm, x, c, w_qkv, w_out, sems, 0)
    project(copies, x, c, w_qkv, w_out, proj, gctx)
    for pair in range(PAIRS):
        lanes = slice(pair * PAIR, (pair + 1) * PAIR)
        k_lanes = slice(HALF_WIDTH + pair * PAIR, HALF_WIDTH + (pair + 1) * PAIR)
        v_lanes = slice(2 * HALF_WIDTH + pair * PAIR, 2 * HALF_WIDTH + (pair + 1) * PAIR)
        keys = [half_lanes(proj[:, k_lanes], half) for half in range(2)]
        values = [half_lanes(proj[:, v_lanes], half) for half in range(2)]
        for start in range(0, POSITIONS, BLOCK):
            stop = start + BLOCK
            query = proj[start:stop, lanes]
            grad = gctx[start:stop, lanes]
            allowed = lax.broadcasted_iota(jnp.int32, (BLOCK, stop), 1) <= (
                lax.broadcasted_iota(jnp.int32, (BLOCK, stop), 0) + start
            )
            outs, dqs = [], []
            for half in range(2):
                key, value = keys[half][:stop], values[half][:stop]
                weights = probabilities(dot_nt(query, key), allowed)
                rounded = weights.astype(BF)
                probs[half, start:stop, :stop] = rounded
                outs.append(dot(rounded, value))
                grad_weights = dot_nt(grad, value)
                delta = jnp.sum(weights * grad_weights, axis=-1, keepdims=True)
                ds = (weights * (grad_weights - delta)).astype(BF)
                dscores[half, start:stop, :stop] = ds
                dqs.append(dot(ds, key))
            ctx[start:stop, lanes] = (outs[0] + outs[1]).astype(BF)
            grads[start:stop, lanes] = ((dqs[0] + dqs[1]) * (HEAD_DIM ** -0.5)).astype(BF)
        queries = [half_lanes(proj[:, lanes], half) for half in range(2)]
        grad_parts = [half_lanes(gctx[:, lanes], half) for half in range(2)]
        for start in range(0, POSITIONS, BLOCK):
            stop = start + BLOCK
            dk = sum(dot_tn(dscores[half, start:, start:stop], queries[half][start:]) for half in range(2))
            dv = sum(dot_tn(probs[half, start:, start:stop], grad_parts[half][start:]) for half in range(2))
            grads[start:stop, k_lanes] = dk.astype(BF)
            grads[start:stop, v_lanes] = dv.astype(BF)
    core = core_ref[0]
    targets = [(1 - core, send_hbm), (core, keep_hbm)]
    weight_terms(x, c, grads, ctx, terms, targets, sems, [(grads, grads_hbm), (ctx, ctx_hbm)])


def column_kernel(
    core_ref, both_hbm, qkv_hbm, out_hbm, after, back_hbm, keep_hbm, send_hbm,
    x, c, w_qkv, w_out, proj, gctx, grads, ctx, terms, sems, back,
):
    x_hbm, c_hbm = both_hbm.at[:, 0], both_hbm.at[:, 1]
    copies = load(x_hbm, c_hbm, qkv_hbm, out_hbm, x, c, w_qkv, w_out, sems, HALF_WIDTH)
    project(copies, x, c, w_qkv, w_out, proj, gctx)
    size = ROWS * CHUNK
    chunks = COLUMNS // CHUNK
    line = lax.broadcasted_iota(jnp.int32, (size, size), 0)
    across = lax.broadcasted_iota(jnp.int32, (size, size), 1)
    allowed = ((line % CHUNK) == (across % CHUNK)) & (across <= line)
    allowed = jnp.concatenate([allowed.astype(F32)] * chunks, axis=0) > 0

    def twice(array):
        return jnp.concatenate([half_lanes(array, 0), half_lanes(array, 1)], axis=0)

    def gather(ref, base):
        whole = ref[:, base : base + PAIR].reshape(ROWS, COLUMNS, PAIR)
        return [
            whole[:, t * CHUNK : (t + 1) * CHUNK].reshape(size, PAIR) for t in range(chunks)
        ]

    def scatter(ref, base, pieces):
        whole = jnp.concatenate([p.reshape(ROWS, CHUNK, PAIR) for p in pieces], axis=1)
        ref[:, base : base + PAIR] = whole.reshape(POSITIONS, PAIR)

    for pair in range(PAIRS):
        base = pair * PAIR
        query, key, value = [gather(proj, part * HALF_WIDTH + base) for part in range(3)]
        grad = gather(gctx, base)
        keys, values, queries, grad_parts = [[twice(t) for t in part] for part in (key, value, query, grad)]
        scores = jnp.concatenate([dot_nt(a, b) for a, b in zip(query, keys)], axis=0)
        grad_weights = jnp.concatenate([dot_nt(a, b) for a, b in zip(grad, values)], axis=0)
        rounded, dscores = [], []
        for half in range(2):
            lanes = slice(half * size, (half + 1) * size)
            weights = probabilities(scores[:, lanes], allowed)
            rounded.append(weights.astype(BF))
            part = grad_weights[:, lanes]
            delta = jnp.sum(weights * part, axis=-1, keepdims=True)
            dscores.append((weights * (part - delta)).astype(BF))
        outs, dqs, dks, dvs = [], [], [], []
        for t in range(chunks):
            rows = slice(t * size, (t + 1) * size)
            wide = [jnp.concatenate([pieces[0][rows], pieces[1][rows]], axis=1) for pieces in (rounded, dscores)]
            tall = [jnp.concatenate([pieces[0][rows], pieces[1][rows]], axis=0) for pieces in (rounded, dscores)]
            outs.append(dot(wide[0], values[t]).astype(BF))
            dqs.append((dot(wide[1], keys[t]) * (HEAD_DIM ** -0.5)).astype(BF))
            dks.append(dot_tn(tall[1], queries[t]).astype(BF))
            dvs.append(dot_tn(tall[0], grad_parts[t]).astype(BF))
        scatter(ctx, base, outs)
        scatter(grads, base, dqs)
        scatter(grads, HALF_WIDTH + base, dks)
        scatter(grads, 2 * HALF_WIDTH + base, dvs)
    core = core_ref[0]
    targets = [(1 - core, send_hbm), (core, keep_hbm)]
    back[:, WIDTH:] = ctx[...]
    for start in range(0, WIDTH, BLOCK):
        columns = slice(start, start + BLOCK)
        back[:, columns] = dot_nt(grads[...], w_qkv[columns]).astype(BF)
    weight_terms(x, c, grads, ctx, terms, targets, sems, [(back, back_hbm)])


def wait_all(copies):
    for copy in copies:
        copy.wait()


def start_all(copies):
    for copy in copies:
        copy.start()
    return copies


def weight_copies(qkv_hbm, w_qkv, sems, first):
    return [
        pltpu.make_async_copy(
            qkv_hbm.at[:, pl.ds(part * WIDTH + first, HALF_WIDTH)], w_qkv.at[part], sems.at[part]
        )
        for part in range(3)
    ]


def grads_times_weights(grads, w_qkv, columns):
    return sum(
        dot_nt(grads[:, part * HALF_WIDTH : (part + 1) * HALF_WIDTH], w_qkv[part, columns]) for part in range(3)
    )


def final_kernel(
    grads_hbm, ctx_hbm, back_hbm, qkv_hbm, out_hbm, attention_hbm, normed_hbm,
    grads, ctx, back, w_qkv, w_out, attention, normed, sems, out_sems,
):
    ins = start_all(
        [
            pltpu.make_async_copy(source, target, sems.at[3 + index])
            for index, (source, target) in enumerate(
                ((ctx_hbm, ctx), (back_hbm, back), (out_hbm, w_out), (grads_hbm, grads))
            )
        ]
        + weight_copies(qkv_hbm, w_qkv, sems, 0)
    )
    outs = []
    wait_all(ins[:3])
    for index in range(3):
        columns = slice(index * BLOCK, (index + 1) * BLOCK)
        span = pl.ds(index * BLOCK, BLOCK)
        attention[:, columns] = (
            dot_nt(ctx[...], w_out[columns, :HALF_WIDTH]) + dot_nt(back[:, WIDTH:], w_out[columns, HALF_WIDTH:])
        ).astype(BF)
        outs += start_all(
            [pltpu.make_async_copy(attention.at[:, span], attention_hbm.at[:, span], out_sems.at[0, index])]
        )
    wait_all(ins[3:])
    for index in range(3):
        columns = slice(index * BLOCK, (index + 1) * BLOCK)
        span = pl.ds(index * BLOCK, BLOCK)
        normed[:, columns] = (
            back[:, columns].astype(F32) + grads_times_weights(grads, w_qkv, columns)
        ).astype(BF)
        outs += start_all([pltpu.make_async_copy(normed.at[:, span], normed_hbm.at[:, span], out_sems.at[1, index])])
    wait_all(outs)


def order_kernel(back_hbm, first, second, third, out_hbm, zeros, sems):
    zeros[...] = jnp.zeros_like(zeros)
    wait_all(start_all([pltpu.make_async_copy(zeros, out_hbm, sems.at[0])]))


def pack_kernel(x_hbm, c_hbm, both_hbm, both, sems, out_sems):
    spans = [pl.ds(2 * index, 2) for index in range(4)]
    ins = start_all(
        [
            pltpu.make_async_copy(source.at[span], both.at[span, place], sems.at[place, index])
            for index, span in enumerate(spans)
            for place, source in enumerate((x_hbm, c_hbm))
        ]
    )
    outs = []
    for index, span in enumerate(spans):
        wait_all(ins[2 * index : 2 * index + 2])
        outs += start_all([pltpu.make_async_copy(both.at[span], both_hbm.at[span], out_sems.at[index])])
    wait_all(outs)


def pair_sum_kernel(x_ref, keep_hbm, received_hbm, *refs):
    out_hbms = refs[-8:-4]
    terms, totals, sems, out_sems = refs[-4:]
    ins, outs = [], []
    order = (1, 3, 2, 0)
    for step in order:
        place = pl.ds(2 * lax.rem(x_ref[0] + step, 4), 2)
        for index, source in enumerate((keep_hbm, received_hbm)):
            ins += start_all(
                [pltpu.make_async_copy(source.at[place], terms.at[step, index], sems.at[index, step])]
            )
    for index, step in enumerate(order):
        wait_all(ins[2 * index : 2 * index + 2])
        totals[step] = (terms[step, 0].astype(F32) + terms[step, 1].astype(F32)).astype(BF)
        outs += start_all([pltpu.make_async_copy(totals.at[step], out_hbms[step], out_sems.at[step])])
    wait_all(outs)


def ring_sum_kernel(*refs):
    in_hbms, (out_hbm, terms, totals, sems, out_sems) = refs[:8], refs[9:]
    ins = start_all(
        [pltpu.make_async_copy(source, terms.at[index], sems.at[index]) for index, source in enumerate(in_hbms)]
    )
    outs = []
    for half in range(2):
        wait_all(ins[4 * half : 4 * half + 4])
        for z_hi in range(2):
            total = sum(terms[4 * half + step, z_hi].astype(F32) for step in range(4))
            for z_lo in range(2):
                totals[z_hi, :, z_lo, half] = total[:, 24 * z_lo : 24 * z_lo + 24].astype(BF)
    for z_hi in range(2):
        outs += start_all([pltpu.make_async_copy(totals.at[z_hi], out_hbm.at[z_hi], out_sems.at[z_hi])])
    wait_all(outs)


def group_sum_kernel(pieces_hbm, out_hbm, pieces, total, sems):
    wait_all(start_all([pltpu.make_async_copy(pieces_hbm, pieces, sems.at[8])]))
    total[...] = jnp.sum(pieces[...].astype(F32), axis=0).astype(BF)
    wait_all(
        start_all([pltpu.make_async_copy(total, out_hbm.at[place], sems.at[place]) for place in range(8)])
    )


def assemble_kernel(factor, whole_hbm, qkv_hbm, out_hbm, whole, qkv_grad, out_grad, sems):
    wait_all(start_all([pltpu.make_async_copy(whole_hbm, whole, sems.at[0])]))
    for place in range(8):
        rows = slice(place // 4 * 24, place // 4 * 24 + 24)
        part = place % 4
        for half in range(2):
            start = half * HALF_WIDTH
            value = whole[place, half].astype(F32) * factor
            if part < 3:
                start += part * WIDTH
                qkv_grad[rows, start : start + HALF_WIDTH] = value
            else:
                out_grad[rows, start : start + HALF_WIDTH] = value
    wait_all(
        start_all(
            [
                pltpu.make_async_copy(qkv_grad, qkv_hbm, sems.at[1]),
                pltpu.make_async_copy(out_grad, out_hbm, sems.at[2]),
            ]
        )
    )


SMEM = pl.BlockSpec(memory_space=pltpu.SMEM)
HBM = pl.BlockSpec(memory_space=pltpu.HBM)


def buffer(*dims, dtype=BF):
    return pltpu.VMEM(dims, dtype)


def copy_sems(*dims):
    return pltpu.SemaphoreType.DMA(dims)


def shape(*dims, dtype=BF):
    return jax.ShapeDtypeStruct(dims, dtype)


def call(kernel, out_shape, flops, scratch, arrays, mib=64):
    scalars = sum(1 for array in arrays if array.ndim == 1)
    return pl.pallas_call(
        kernel,
        out_shape=out_shape,
        in_specs=[SMEM] * scalars + [HBM] * (len(arrays) - scalars),
        out_specs=jax.tree.map(lambda _: HBM, out_shape),
        scratch_shapes=scratch,
        compiler_params=pltpu.CompilerParams(vmem_limit_bytes=mib * MIB),
        cost_estimate=pl.CostEstimate(flops=flops, bytes_accessed=2 ** 16, transcendentals=0),
    )(*arrays)


def sublayer(kernel, dims, out_shapes, scratch, *arrays):
    return call(
        kernel,
        (*out_shapes, shape(ROWS, 4, 48, HALF_WIDTH), shape(ROWS, 4, 48, HALF_WIDTH)),
        2 * 10 ** 10,
        [
            buffer(*dims),
            buffer(*dims),
            buffer(WIDTH, 3 * HALF_WIDTH),
            buffer(WIDTH, HALF_WIDTH),
            buffer(POSITIONS, 3 * HALF_WIDTH),
            buffer(POSITIONS, HALF_WIDTH),
            buffer(POSITIONS, 3 * HALF_WIDTH),
            buffer(POSITIONS, HALF_WIDTH),
            buffer(ROWS, 2, 4, 48, HALF_WIDTH),
            copy_sems(10),
            *scratch,
        ],
        arrays,
        mib=64,
    )


def swap(part, axis, groups=None):
    return lax.all_to_all(part, axis, split_axis=0, concat_axis=0, tiled=True, axis_index_groups=groups)


def plane_groups():
    def flat(x, z_hi, core, z_lo, y):
        return ((x * 2 + z_hi) * 2 + core) * 8 + z_lo * 4 + y

    return [
        [flat(x, z_hi, core, z_lo, y) for z_hi in range(2) for y in range(4) for z_lo in range(2)]
        for x in range(4)
        for core in range(2)
    ]


def exchange(send):
    return lax.ppermute(send, "dp", [(i, i ^ 1) for i in range(16)])


def pair_sum(x_index, keep, send, *after):
    return call(
        pair_sum_kernel,
        (shape(2, 4, 48, HALF_WIDTH),) * 4,
        2 * 10 ** 9,
        [buffer(4, 2, 2, 4, 48, HALF_WIDTH), buffer(4, 2, 4, 48, HALF_WIDTH), copy_sems(2, 4), copy_sems(4)],
        (x_index, keep, exchange(send), *after),
    )


def ring(parts):
    return [parts[0]] + [
        lax.ppermute(parts[step], "dp", [(i, (i + 4 * step) % 16) for i in range(16)]) for step in range(1, 4)
    ]


def body(normed, cotangent, qkv_weight, out_weight):
    x, c = normed[0], cotangent[0]
    dp = lax.axis_index("dp")
    core = (dp % 2).reshape(1)
    x_index = (dp // 4).reshape(1)
    grid_dims = (ROWS, COLUMNS, WIDTH)
    both = call(
        pack_kernel,
        shape(ROWS, 2, COLUMNS, WIDTH),
        10 ** 6,
        [buffer(ROWS, 2, COLUMNS, WIDTH), copy_sems(2, 4), copy_sems(4)],
        (x.reshape(grid_dims), c.reshape(grid_dims)),
    )
    both = swap(both, "ctx")
    grads_row, ctx_row, keep_row, send_row = sublayer(
        row_kernel,
        (POSITIONS, WIDTH),
        [shape(POSITIONS, 3 * HALF_WIDTH), shape(POSITIONS, HALF_WIDTH)],
        [buffer(2, POSITIONS, POSITIONS)] * 2,
        core, x, c, qkv_weight, out_weight,
    )
    terms_row = ring(pair_sum(x_index, keep_row, send_row))
    back_width = WIDTH + HALF_WIDTH
    back, keep_col, send_col = sublayer(
        column_kernel,
        grid_dims,
        [shape(POSITIONS, back_width)],
        [buffer(POSITIONS, back_width)],
        core, both, qkv_weight, out_weight, terms_row[0],
    )
    order = call(order_kernel, shape(8, PAIR, dtype=F32), 4 * 10 ** 10, [buffer(8, PAIR, dtype=F32), copy_sems(1)], (back, *terms_row[1:]))
    parts = pair_sum(x_index, keep_col, send_col, order)
    terms_col = ring(parts)
    back = swap(back.reshape(ROWS, COLUMNS, back_width), "ctx").reshape(POSITIONS, back_width)
    attention_out, normed_grad = call(
        final_kernel,
        (shape(POSITIONS, WIDTH),) * 2,
        4 * 10 ** 9,
        [
            buffer(POSITIONS, 3 * HALF_WIDTH),
            buffer(POSITIONS, HALF_WIDTH),
            buffer(POSITIONS, back_width),
            buffer(3, WIDTH, HALF_WIDTH),
            buffer(WIDTH, WIDTH),
            buffer(POSITIONS, WIDTH),
            buffer(POSITIONS, WIDTH),
            copy_sems(7),
            copy_sems(2, 4),
        ],
        (grads_row, ctx_row, back, qkv_weight, out_weight),
        mib=64,
    )
    terms = call(
        ring_sum_kernel,
        shape(2, 4, 2, 2, 24, HALF_WIDTH),
        2 * 10 ** 9,
        [buffer(8, 2, 4, 48, HALF_WIDTH), buffer(2, 4, 2, 2, 24, HALF_WIDTH), copy_sems(8), copy_sems(2)],
        (*terms_row, *terms_col, back),
    )
    pieces = swap(terms.reshape(16, 2, 24, HALF_WIDTH), ("dp", "ctx"), plane_groups())
    own = call(
        group_sum_kernel,
        shape(8, 2, 24, HALF_WIDTH),
        10 ** 9,
        [buffer(16, 2, 24, HALF_WIDTH), buffer(2, 24, HALF_WIDTH), copy_sems(9)],
        (pieces,),
    )
    whole = swap(own, "ctx")
    factor = (lax.axis_size("dp") * lax.axis_size("ctx") * POSITIONS) ** (-0.5)
    qkv_grad, out_grad = call(
        functools.partial(assemble_kernel, factor),
        (shape(48, 3 * WIDTH, dtype=F32), shape(48, WIDTH, dtype=F32)),
        10 ** 6,
        [
            buffer(8, 2, 24, HALF_WIDTH),
            buffer(48, 3 * WIDTH, dtype=F32),
            buffer(48, WIDTH, dtype=F32),
            copy_sems(3),
        ],
        (whole,),
    )
    return (attention_out[None], normed_grad[None], qkv_grad, out_grad)


def solution(mesh):
    placed = (P("dp", "ctx", None), P("dp", "ctx", None), P(), P())
    return jax.shard_map(
        body,
        mesh=mesh,
        in_specs=placed,
        out_specs=(P("dp", "ctx", None), P("dp", "ctx", None), P("dp", None), P("dp", None)),
        check_vma=False,
    )
```

time: 136 us -> 109 us (0.80)
  waiting for transfers between devices: 49.8 us -> 19 us
  blocking collectives: 0 us -> 18.9 us
  other arithmetic: 13.6 us -> 0 us
  Pallas kernels: 33.7 us -> 43.7 us
  local copies, waits for them, and re-layouts: 9.14 us -> 0 us
  starting transfers between devices: 28.3 us -> 25 us
    all_to_all x5 -> x3, waiting for transfers between devices: 49.8 us -> 12.9 us  [swap(): lax.all_to_all(part, axis, split_axis=0, concat_axis=0, tiled=True, axis_...]
    all_to_all x0 -> x1, blocking collectives: none -> 18.9 us  [swap(): lax.all_to_all(part, axis, split_axis=0, concat_axis=0, tiled=True, axis_...]
    all_to_all x5 -> x3, starting transfers between devices: 28.3 us -> 15.7 us  [swap(): lax.all_to_all(part, axis, split_axis=0, concat_axis=0, tiled=True, axis_...]
    pallas_call x4 -> x10, Pallas kernels: 33.7 us -> 43.7 us  [call(): pl.pallas_call(kernel, out_shape=out_shape, in_specs=[SMEM] * scalars + [...]
    ppermute x2 -> x8, starting transfers between devices: 0.09 us -> 9.34 us  [the longest x6 9.16 us: ring(): lax.ppermute(parts[step], 'dp', [(i, (i + 4 * step) % 16) for i in range(...]
    ppermute x2 -> x8, waiting for transfers between devices: 0.01 us -> 6.11 us  [the longest x2 3.16 us: exchange(): return lax.ppermute(send, 'dp', [(i, i ^ 1) for i in range(16)])]
    convert_element_type x2 -> x0, other arithmetic: 5.65 us -> none  [summed(): both = (keep.astype(F32) + received.astype(F32)).astype(BF)]
    unnamed x22 -> x0, local copies, waits for them, and re-layouts: 3.92 us -> none
  transfers between devices with their start and end apart: 7 -> 11, of which waited for: 5 -> 5; matrix products, arithmetic and copies ran while one was open for 8% -> 0% of each run, Pallas kernels for 25% -> 32%
where the time goes in v2:
time: 109 us; the launch traced here: 108 us
  Pallas kernels  43.7 us (40%)
  starting transfers between devices  25 us (23%)
  waiting for transfers between devices  19 us (17%)
  blocking collectives  18.9 us (17%)
    pallas_call x10, Pallas kernels, call(): pl.pallas_call(kernel, out_shape=out_shape, in_specs=[SMEM] * scalars + [...  43.7 us
    all_to_all x1, blocking collectives, swap(): lax.all_to_all(part, axis, split_axis=0, concat_axis=0, tiled=True, axis_...  18.9 us
    all_to_all x3, starting transfers between devices, swap(): lax.all_to_all(part, axis, split_axis=0, concat_axis=0, tiled=True, axis_...  15.7 us
    all_to_all x3, waiting for transfers between devices, swap(): lax.all_to_all(part, axis, split_axis=0, concat_axis=0, tiled=True, axis_...  12.9 us
    ppermute x6, starting transfers between devices, ring(): lax.ppermute(parts[step], 'dp', [(i, (i + 4 * step) % 16) for i in range(...  9.16 us
    ppermute x2, waiting for transfers between devices, exchange(): return lax.ppermute(send, 'dp', [(i, i ^ 1) for i in range(16)])  3.16 us
    ppermute x6, waiting for transfers between devices, ring(): lax.ppermute(parts[step], 'dp', [(i, (i + 4 * step) % 16) for i in range(...  2.94 us
  transfers between devices with their start and end apart: 11, of which 5 were waited for; matrix products, arithmetic and copies ran while one was open for 0% of the time, Pallas kernels for 32%

profile of v2, /device:TPU:0, one launch (start us, length us, event | category | flops | bytes accessed | tf_op | source)
XLA Modules:
  0.0 107.6 jit_solution(12468331217879768001)
XLA Ops:
  0.6 2.3 %shard_map.76 = bf16[8,2,64,768]{3,2,1,0:T(8,128)(2,1)} custom-call(bf16[8,64,768]{2,1,0:T(8,128)(2,1)} %bitcast.12, bf16[8,64,768]{2,1,0:T(8,128)(2,1)} %bitcast.14), custom_call_target="tpu_custom_call" | custom-call | flops 1000000 | bytes 65536 | tf_op jit(solution)/shard_map/pallas_call | solution.py:375
  3.0 5.9 %all-to-all-start = ((bf16[8,2,64,768]{3,2,1,0:T(8,128)(2,1)}), bf16[8,2,64,768]{3,2,1,0:T(8,128)(2,1)}, u32[]{:S(2)}, u32[]{:S(2)}) async-start(bf16[8,2,64,768]{3,2,1,0:T(8,128)(2,1)} %shard_map.76), calls=%async_computation | async-start | bytes 3145728 | tf_op jit(solution)/shard_map/all_to_all | solution.py:410
  8.9 13.1 %shard_map.75 = (bf16[512,1152]{1,0:T(8,128)(2,1)}, bf16[512,384]{1,0:T(8,128)(2,1)}, bf16[8,4,48,384]{3,2,1,0:T(8,128)(2,1)}, bf16[8,4,48,384]{3,2,1,0:T(8,128)(2,1)}) custom-call(s32[1]{0:T(128)} %bitcast.core_ref, bf16[512,768]{1,0:T(8,128)(2,1)} %bitcast.13, bf16[512,768]{1,0:T(8,128)(2,1)} %bitcast.15, bf16[768,2304]{1,0:T(8,128)(2,1)} %qkv_hbm.5, ...), custom_call_target="tpu_custom_call" | custom-call | flops 20000000000 | bytes 65536 | tf_op jit(solution)/shard_map/pallas_call | solution.py:375
  22.1 3.2 %collective-permute-done.received_hbm = bf16[8,4,48,384]{3,2,1,0:T(8,128)(2,1)} collective-permute-done((bf16[8,4,48,384]{3,2,1,0:T(8,128)(2,1)}, bf16[8,4,48,384]{3,2,1,0:T(8,128)(2,1)}, u32[]{:S(2)}, u32[]{:S(2)}) %collective-permute-start) | collective-permute-done | bytes 1179680 | tf_op jit(solution)/shard_map/ppermute | solution.py:425
  25.3 2.5 %shard_map.77 = (bf16[2,4,48,384]{3,2,1,0:T(8,128)(2,1)}, bf16[2,4,48,384]{3,2,1,0:T(8,128)(2,1)}, bf16[2,4,48,384]{3,2,1,0:T(8,128)(2,1)}, bf16[2,4,48,384]{3,2,1,0:T(8,128)(2,1)}) custom-call(s32[1]{0:T(128)} %bitcast.5.x_ref, bf16[8,4,48,384]{3,2,1,0:T(8,128)(2,1)} %get-tuple-element.25.keep_hbm, bf16[8,4,48,384]{3,2,1,0:T(8,128)(2,1)} %collective-permute-done.received_hbm), custom_call_target="tpu_custom_call" | custom-call | flops 2000000000 | bytes 65536 | tf_op jit(solution)/shard_map/pallas_call | solution.py:375
  27.8 1.6 %collective-permute-start.1 = (bf16[2,4,48,384]{3,2,1,0:T(8,128)(2,1)}, bf16[2,4,48,384]{3,2,1,0:T(8,128)(2,1)}, u32[]{:S(2)}, u32[]{:S(2)}) collective-permute-start(bf16[2,4,48,384]{3,2,1,0:T(8,128)(2,1)} %get-tuple-element.31), channel_id=1, source_target_pairs={{0,32},{8,40},{16,48},{24,56},{32,64},{40,72},{48,80},{56,88},{64,... | collective-permute-start | bytes 884744 | tf_op jit(solution)/shard_map/ppermute | solution.py:440
  29.3 2.7 %collective-permute-start.2 = (bf16[2,4,48,384]{3,2,1,0:T(8,128)(2,1)}, bf16[2,4,48,384]{3,2,1,0:T(8,128)(2,1)}, u32[]{:S(2)}, u32[]{:S(2)}) collective-permute-start(bf16[2,4,48,384]{3,2,1,0:T(8,128)(2,1)} %get-tuple-element.32), channel_id=1, source_target_pairs={{0,64},{8,72},{16,80},{24,88},{32,96},{40,104},{48,112},{56,120},{... | collective-permute-start | bytes 884744 | tf_op jit(solution)/shard_map/ppermute | solution.py:440
  32.1 1.4 %collective-permute-start.3 = (bf16[2,4,48,384]{3,2,1,0:T(8,128)(2,1)}, bf16[2,4,48,384]{3,2,1,0:T(8,128)(2,1)}, u32[]{:S(2)}, u32[]{:S(2)}) collective-permute-start(bf16[2,4,48,384]{3,2,1,0:T(8,128)(2,1)} %get-tuple-element.33), channel_id=1, source_target_pairs={{0,96},{8,104},{16,112},{24,120},{32,0},{40,8},{48,16},{56,24},{64... | collective-permute-start | bytes 884744 | tf_op jit(solution)/shard_map/ppermute | solution.py:440
  33.5 10.4 %shard_map.78 = (bf16[512,1152]{1,0:T(8,128)(2,1)}, bf16[8,4,48,384]{3,2,1,0:T(8,128)(2,1)}, bf16[8,4,48,384]{3,2,1,0:T(8,128)(2,1)}) custom-call(s32[1]{0:T(128)} %bitcast.core_ref, bf16[8,2,64,768]{3,2,1,0:T(8,128)(2,1)} %all-to-all-done.both_hbm, bf16[768,2304]{1,0:T(8,128)(2,1)} %qkv_hbm.5, bf16[768,768]{1,0:T(8,128)(2,1)} %out_hbm.5, ...), custom_call_target="tpu_custom_call" | custom-call | flops 20000000000 | bytes 65536 | tf_op jit(solution)/shard_map/pallas_call | solution.py:375
  44.1 5.7 %all-to-all-start.1 = ((bf16[8,64,1152]{2,1,0:T(8,128)(2,1)}), bf16[8,64,1152]{2,1,0:T(8,128)(2,1)}, u32[]{:S(2)}, u32[]{:S(2)}) async-start(bf16[8,64,1152]{2,1,0:T(8,128)(2,1)} %bitcast.11), calls=%async_computation.1 | async-start | bytes 2359296 | tf_op jit(solution)/shard_map/all_to_all | solution.py:410
  50.4 2.5 %shard_map.81 = (bf16[2,4,48,384]{3,2,1,0:T(8,128)(2,1)}, bf16[2,4,48,384]{3,2,1,0:T(8,128)(2,1)}, bf16[2,4,48,384]{3,2,1,0:T(8,128)(2,1)}, bf16[2,4,48,384]{3,2,1,0:T(8,128)(2,1)}) custom-call(s32[1]{0:T(128)} %bitcast.5.x_ref, bf16[8,4,48,384]{3,2,1,0:T(8,128)(2,1)} %get-tuple-element.34.keep_hbm, ...), custom_call_target="tpu_custom_call" | custom-call | flops 2000000000 | bytes 65536 | tf_op jit(solution)/shard_map/pallas_call | solution.py:375
  52.9 0.7 collective-permute-start.5
  53.6 0.9 collective-permute-start.6
  54.4 1.9 %collective-permute-start.7 = (bf16[2,4,48,384]{3,2,1,0:T(8,128)(2,1)}, bf16[2,4,48,384]{3,2,1,0:T(8,128)(2,1)}, u32[]{:S(2)}, u32[]{:S(2)}) collective-permute-start(bf16[2,4,48,384]{3,2,1,0:T(8,128)(2,1)} %get-tuple-element.39), channel_id=1, source_target_pairs={{0,96},{8,104},{16,112},{24,120},{32,0},{40,8},{48,16},{56,24},{64... | collective-permute-start | bytes 884744 | tf_op jit(solution)/shard_map/ppermute | solution.py:440
  56.3 11.3 %all-to-all-done.1 = bf16[8,64,1152]{2,1,0:T(8,128)(2,1)} async-done(((bf16[8,64,1152]{2,1,0:T(8,128)(2,1)}), bf16[8,64,1152]{2,1,0:T(8,128)(2,1)}, u32[]{:S(2)}, u32[]{:S(2)}) %all-to-all-start.1) | async-done | bytes 1179680 | tf_op jit(solution)/shard_map/all_to_all | solution.py:410
  67.6 2.3 %collective-permute-done.5.refs_5_ = bf16[2,4,48,384]{3,2,1,0:T(8,128)(2,1)} collective-permute-done((bf16[2,4,48,384]{3,2,1,0:T(8,128)(2,1)}, bf16[2,4,48,384]{3,2,1,0:T(8,128)(2,1)}, u32[]{:S(2)}, u32[]{:S(2)}) %collective-permute-start.5) | collective-permute-done | bytes 294944 | tf_op jit(solution)/shard_map/ppermute | solution.py:440
  69.9 0.6 collective-permute-done.7.refs_7_
  70.6 2.6 %shard_map.82 = bf16[2,4,2,2,24,384]{5,4,3,2,1,0:T(8,128)(2,1)} custom-call(bf16[2,4,48,384]{3,2,1,0:T(8,128)(2,1)} %get-tuple-element.27.after.refs_0_, bf16[2,4,48,384]{3,2,1,0:T(8,128)(2,1)} %collective-permute-done.1.first.refs_1_, bf16[2,4,48,384]{3,2,1,0:T(8,128)(2,1)} %collective-permute-done.2.second.refs_2_, ...), custom_call_target="tpu_custom_call" | custom-call | flops 2000000000 | bytes 65536 | tf_op jit(solution)/shard_map/pallas_call | solution.py:375
  73.2 18.9 %all_to_all.20.pieces_hbm = bf16[16,2,24,384]{3,2,1,0:T(8,128)(2,1)} all-to-all(bf16[16,2,24,384]{3,2,1,0:T(8,128)(2,1)} %bitcast.16), channel_id=1, replica_groups={{0,4,1,5,2,6,3,7,16,20,17,21,18,22,19,23},{8,12,9,13,10,14,11,15,24,28,..., dimensions={0} | all-to-all | bytes 1179648 | tf_op jit(solution)/shard_map/all_to_all | solution.py:410
  92.1 2.0 %shard_map.83 = bf16[8,2,24,384]{3,2,1,0:T(8,128)(2,1)} custom-call(bf16[16,2,24,384]{3,2,1,0:T(8,128)(2,1)} %all_to_all.20.pieces_hbm), custom_call_target="tpu_custom_call" | custom-call | flops 1000000000 | bytes 65536 | tf_op jit(solution)/shard_map/pallas_call | solution.py:375
  94.1 4.1 %all-to-all-start.3 = ((bf16[8,2,24,384]{3,2,1,0:T(8,128)(2,1)}), bf16[8,2,24,384]{3,2,1,0:T(8,128)(2,1)}, u32[]{:S(2)}, u32[]{:S(2)}) async-start(bf16[8,2,24,384]{3,2,1,0:T(8,128)(2,1)} %shard_map.83), calls=%async_computation.3 | async-start | bytes 589824 | tf_op jit(solution)/shard_map/all_to_all | solution.py:410
  98.1 5.8 %shard_map.79 = (bf16[512,768]{1,0:T(8,128)(2,1)}, bf16[512,768]{1,0:T(8,128)(2,1)}) custom-call(bf16[512,1152]{1,0:T(8,128)(2,1)} %get-tuple-element.23.grads_hbm, bf16[512,384]{1,0:T(8,128)(2,1)} %get-tuple-element.24.ctx_hbm, bf16[512,1152]{1,0:T(8,128)(2,1)} %bitcast.7.back_hbm.refs_8_, bf16[768,2304]{1,0:T(8,128)(2,1)} %qkv_hbm.5, bf16[768,768]{1,0:T(8,128)(2,1)} %out_hbm.5), custom_call_target="tpu_custom_call" | custom-call | flops 4000000000 | bytes 65536 | tf_op jit(solution)/shard_map/pallas_call | solution.py:375
  104.0 1.6 %all-to-all-done.3.whole_hbm = bf16[8,2,24,384]{3,2,1,0:T(8,128)(2,1)} async-done(((bf16[8,2,24,384]{3,2,1,0:T(8,128)(2,1)}), bf16[8,2,24,384]{3,2,1,0:T(8,128)(2,1)}, u32[]{:S(2)}, u32[]{:S(2)}) %all-to-all-start.3) | async-done | bytes 294944 | tf_op jit(solution)/shard_map/all_to_all | solution.py:410
  105.6 1.8 %shard_map.84 = (f32[48,2304]{1,0:T(8,128)}, f32[48,768]{1,0:T(8,128)}) custom-call(bf16[8,2,24,384]{3,2,1,0:T(8,128)(2,1)} %all-to-all-done.3.whole_hbm), custom_call_target="tpu_custom_call" | custom-call | flops 1000000 | bytes 65536 | tf_op jit(solution)/shard_map/pallas_call | solution.py:375
  (9 shorter events, 0.8 us)
Async XLA Ops:
  3.0 30.5 %all-to-all-start = ((bf16[8,2,64,768]{3,2,1,0:T(8,128)(2,1)}), bf16[8,2,64,768]{3,2,1,0:T(8,128)(2,1)}, u32[]{:S(2)}, u32[]{:S(2)}) async-start(bf16[8,2,64,768]{3,2,1,0:T(8,128)(2,1)} %shard_map.76), calls=%async_computation | async-start | bytes 3145728 | tf_op jit(solution)/shard_map/all_to_all | solution.py:410
  22.0 3.3 %collective-permute-start = (bf16[8,4,48,384]{3,2,1,0:T(8,128)(2,1)}, bf16[8,4,48,384]{3,2,1,0:T(8,128)(2,1)}, u32[]{:S(2)}, u32[]{:S(2)}) collective-permute-start(bf16[8,4,48,384]{3,2,1,0:T(8,128)(2,1)} %get-tuple-element.26), channel_id=1, source_target_pairs={{0,8},{8,0},{16,24},{24,16},{32,40},{40,32},{48,56},{56,48},{64,72... | collective-permute-start | bytes 3538952 | tf_op jit(solution)/shard_map/ppermute | solution.py:425
  27.8 22.0 %collective-permute-start.1 = (bf16[2,4,48,384]{3,2,1,0:T(8,128)(2,1)}, bf16[2,4,48,384]{3,2,1,0:T(8,128)(2,1)}, u32[]{:S(2)}, u32[]{:S(2)}) collective-permute-start(bf16[2,4,48,384]{3,2,1,0:T(8,128)(2,1)} %get-tuple-element.31), channel_id=1, source_target_pairs={{0,32},{8,40},{16,48},{24,56},{32,64},{40,72},{48,80},{56,88},{64,... | collective-permute-start | bytes 884744 | tf_op jit(solution)/shard_map/ppermute | solution.py:440
  29.3 20.4 %collective-permute-start.2 = (bf16[2,4,48,384]{3,2,1,0:T(8,128)(2,1)}, bf16[2,4,48,384]{3,2,1,0:T(8,128)(2,1)}, u32[]{:S(2)}, u32[]{:S(2)}) collective-permute-start(bf16[2,4,48,384]{3,2,1,0:T(8,128)(2,1)} %get-tuple-element.32), channel_id=1, source_target_pairs={{0,64},{8,72},{16,80},{24,88},{32,96},{40,104},{48,112},{56,120},{... | collective-permute-start | bytes 884744 | tf_op jit(solution)/shard_map/ppermute | solution.py:440
  32.1 17.7 %collective-permute-start.3 = (bf16[2,4,48,384]{3,2,1,0:T(8,128)(2,1)}, bf16[2,4,48,384]{3,2,1,0:T(8,128)(2,1)}, u32[]{:S(2)}, u32[]{:S(2)}) collective-permute-start(bf16[2,4,48,384]{3,2,1,0:T(8,128)(2,1)} %get-tuple-element.33), channel_id=1, source_target_pairs={{0,96},{8,104},{16,112},{24,120},{32,0},{40,8},{48,16},{56,24},{64... | collective-permute-start | bytes 884744 | tf_op jit(solution)/shard_map/ppermute | solution.py:440
  44.0 6.4 %collective-permute-start.4 = (bf16[8,4,48,384]{3,2,1,0:T(8,128)(2,1)}, bf16[8,4,48,384]{3,2,1,0:T(8,128)(2,1)}, u32[]{:S(2)}, u32[]{:S(2)}) collective-permute-start(bf16[8,4,48,384]{3,2,1,0:T(8,128)(2,1)} %get-tuple-element.35), channel_id=1, source_target_pairs={{0,8},{8,0},{16,24},{24,16},{32,40},{40,32},{48,56},{56,48},{64,72... | collective-permute-start | bytes 3538952 | tf_op jit(solution)/shard_map/ppermute | solution.py:425
  44.1 23.6 %all-to-all-start.1 = ((bf16[8,64,1152]{2,1,0:T(8,128)(2,1)}), bf16[8,64,1152]{2,1,0:T(8,128)(2,1)}, u32[]{:S(2)}, u32[]{:S(2)}) async-start(bf16[8,64,1152]{2,1,0:T(8,128)(2,1)} %bitcast.11), calls=%async_computation.1 | async-start | bytes 2359296 | tf_op jit(solution)/shard_map/all_to_all | solution.py:410
  52.9 17.0 %collective-permute-start.5 = (bf16[2,4,48,384]{3,2,1,0:T(8,128)(2,1)}, bf16[2,4,48,384]{3,2,1,0:T(8,128)(2,1)}, u32[]{:S(2)}, u32[]{:S(2)}) collective-permute-start(bf16[2,4,48,384]{3,2,1,0:T(8,128)(2,1)} %get-tuple-element.37), channel_id=1, source_target_pairs={{0,32},{8,40},{16,48},{24,56},{32,64},{40,72},{48,80},{56,88},{64,... | collective-permute-start | bytes 884744 | tf_op jit(solution)/shard_map/ppermute | solution.py:440
  53.6 16.4 %collective-permute-start.6 = (bf16[2,4,48,384]{3,2,1,0:T(8,128)(2,1)}, bf16[2,4,48,384]{3,2,1,0:T(8,128)(2,1)}, u32[]{:S(2)}, u32[]{:S(2)}) collective-permute-start(bf16[2,4,48,384]{3,2,1,0:T(8,128)(2,1)} %get-tuple-element.38), channel_id=1, source_target_pairs={{0,64},{8,72},{16,80},{24,88},{32,96},{40,104},{48,112},{56,120},{... | collective-permute-start | bytes 884744 | tf_op jit(solution)/shard_map/ppermute | solution.py:440
  54.4 16.1 %collective-permute-start.7 = (bf16[2,4,48,384]{3,2,1,0:T(8,128)(2,1)}, bf16[2,4,48,384]{3,2,1,0:T(8,128)(2,1)}, u32[]{:S(2)}, u32[]{:S(2)}) collective-permute-start(bf16[2,4,48,384]{3,2,1,0:T(8,128)(2,1)} %get-tuple-element.39), channel_id=1, source_target_pairs={{0,96},{8,104},{16,112},{24,120},{32,0},{40,8},{48,16},{56,24},{64... | collective-permute-start | bytes 884744 | tf_op jit(solution)/shard_map/ppermute | solution.py:440
  94.1 11.6 %all-to-all-start.3 = ((bf16[8,2,24,384]{3,2,1,0:T(8,128)(2,1)}), bf16[8,2,24,384]{3,2,1,0:T(8,128)(2,1)}, u32[]{:S(2)}, u32[]{:S(2)}) async-start(bf16[8,2,24,384]{3,2,1,0:T(8,128)(2,1)} %shard_map.83), calls=%async_computation.3 | async-start | bytes 589824 | tf_op jit(solution)/shard_map/all_to_all | solution.py:410

commit v3 on v2

--- a/solution.py
+++ b/solution.py
@@ -40,7 +40,17 @@
     return jnp.where(inside, array, jnp.zeros_like(array))
 
 
-def probabilities(scores, allowed):
+def probabilities(scores, start):
+    square = scores[:, start:]
+    row = lax.broadcasted_iota(jnp.int32, square.shape, 0)
+    square = jnp.where(lax.broadcasted_iota(jnp.int32, square.shape, 1) <= row, square, -1e30)
+    scores = jnp.concatenate([scores[:, :start], square], axis=1) if start else square
+    top = jnp.max(scores, axis=-1, keepdims=True)
+    weights = jnp.exp(scores - top)
+    return weights * (1.0 / jnp.sum(weights, axis=-1, keepdims=True))
+
+
+def chunk_probabilities(scores, allowed):
     scores = jnp.where(allowed, scores, -1e30)
     top = jnp.max(scores, axis=-1, keepdims=True)
     weights = jnp.exp(scores - top)
@@ -61,13 +71,14 @@
 
 
 def project(copies, x, c, w_qkv, w_out, proj, gctx):
-    for copy in copies[:4]:
-        copy.wait()
-    for part, piece in enumerate(jnp.split(dot(x[...].reshape(POSITIONS, WIDTH), w_qkv[...]), 3, axis=1)):
-        piece = piece.astype(BF)
+    copies[0].wait()
+    for part in range(3):
+        copies[1 + part].wait()
+        columns = slice(part * HALF_WIDTH, (part + 1) * HALF_WIDTH)
+        piece = dot(x[...].reshape(POSITIONS, WIDTH), w_qkv[:, columns]).astype(BF)
         if part == 0:
             piece = piece * BF(HEAD_DIM ** -0.5)
-        proj[:, part * HALF_WIDTH : (part + 1) * HALF_WIDTH] = piece
+        proj[:, columns] = piece
     copies[4].wait()
     copies[5].wait()
     gctx[...] = dot(c[...].reshape(POSITIONS, WIDTH), w_out[...]).astype(BF)
@@ -102,41 +113,61 @@
 ):
     copies = load(x_hbm, c_hbm, qkv_hbm, out_hbm, x, c, w_qkv, w_out, sems, 0)
     project(copies, x, c, w_qkv, w_out, proj, gctx)
-    for pair in range(PAIRS):
+    def products(pair, start):
+        lanes = slice(pair * PAIR, (pair + 1) * PAIR)
+        stop = start + BLOCK
+        query, grad = proj[start:stop, lanes], gctx[start:stop, lanes]
+        keys = [half_lanes(proj[:stop, HALF_WIDTH + pair * PAIR : HALF_WIDTH + (pair + 1) * PAIR], h) for h in range(2)]
+        values = [
+            half_lanes(proj[:stop, 2 * HALF_WIDTH + pair * PAIR : 2 * HALF_WIDTH + (pair + 1) * PAIR], h)
+            for h in range(2)
+        ]
+        scores = [dot_nt(query, key) for key in keys]
+        return pair, start, keys, values, scores, [dot_nt(grad, value) for value in values]
+
+    def softmax(pair, start, keys, values, scores, grad_weights):
+        lanes = slice(pair * PAIR, (pair + 1) * PAIR)
+        stop = start + BLOCK
+        outs, dqs = [], []
+        weights = [probabilities(scores[half], start) for half in range(2)]
+        for half in range(2):
+            rounded = weights[half].astype(BF)
+            probs[pair, half, start:stop, :stop] = rounded
+            outs.append(dot(rounded, values[half]))
+            delta = jnp.sum(weights[half] * grad_weights[half], axis=-1, keepdims=True)
+            ds = (weights[half] * (grad_weights[half] - delta)).astype(BF)
+            dscores[pair, half, start:stop, :stop] = ds
+            dqs.append(dot(ds, keys[half]))
+        ctx[start:stop, lanes] = (outs[0] + outs[1]).astype(BF)
+        grads[start:stop, lanes] = ((dqs[0] + dqs[1]) * (HEAD_DIM ** -0.5)).astype(BF)
+
+    def key_sums(pair):
         lanes = slice(pair * PAIR, (pair + 1) * PAIR)
         k_lanes = slice(HALF_WIDTH + pair * PAIR, HALF_WIDTH + (pair + 1) * PAIR)
         v_lanes = slice(2 * HALF_WIDTH + pair * PAIR, 2 * HALF_WIDTH + (pair + 1) * PAIR)
-        keys = [half_lanes(proj[:, k_lanes], half) for half in range(2)]
-        values = [half_lanes(proj[:, v_lanes], half) for half in range(2)]
+        query_t = jnp.transpose(proj[:, lanes])
+        grad_t = jnp.transpose(gctx[:, lanes])
         for start in range(0, POSITIONS, BLOCK):
             stop = start + BLOCK
-            query = proj[start:stop, lanes]
-            grad = gctx[start:stop, lanes]
-            allowed = lax.broadcasted_iota(jnp.int32, (BLOCK, stop), 1) <= (
-                lax.broadcasted_iota(jnp.int32, (BLOCK, stop), 0) + start
-            )
-            outs, dqs = [], []
-            for half in range(2):
-                key, value = keys[half][:stop], values[half][:stop]
-                weights = probabilities(dot_nt(query, key), allowed)
-                rounded = weights.astype(BF)
-                probs[half, start:stop, :stop] = rounded
-                outs.append(dot(rounded, value))
-                grad_weights = dot_nt(grad, value)
-                delta = jnp.sum(weights * grad_weights, axis=-1, keepdims=True)
-                ds = (weights * (grad_weights - delta)).astype(BF)
-                dscores[half, start:stop, :stop] = ds
-                dqs.append(dot(ds, key))
-            ctx[start:stop, lanes] = (outs[0] + outs[1]).astype(BF)
-            grads[start:stop, lanes] = ((dqs[0] + dqs[1]) * (HEAD_DIM ** -0.5)).astype(BF)
-        queries = [half_lanes(proj[:, lanes], half) for half in range(2)]
-        grad_parts = [half_lanes(gctx[:, lanes], half) for half in range(2)]
-        for start in range(0, POSITIONS, BLOCK):
-            stop = start + BLOCK
-            dk = sum(dot_tn(dscores[half, start:, start:stop], queries[half][start:]) for half in range(2))
-            dv = sum(dot_tn(probs[half, start:, start:stop], grad_parts[half][start:]) for half in range(2))
-            grads[start:stop, k_lanes] = dk.astype(BF)
-            grads[start:stop, v_lanes] = dv.astype(BF)
+            for place, left, right in ((k_lanes, query_t, dscores), (v_lanes, grad_t, probs)):
+                both = jnp.concatenate(
+                    [
+                        dot(left[half * HEAD_DIM : (half + 1) * HEAD_DIM, start:], right[pair, half, start:, start:stop])
+                        for half in range(2)
+                    ],
+                    axis=0,
+                )
+                grads[start:stop, place] = jnp.transpose(both.astype(BF))
+
+    order = [(pair, start) for pair in range(PAIRS) for start in range(0, POSITIONS, BLOCK)]
+    held = products(*order[0])
+    for index, (pair, start) in enumerate(order):
+        following = products(*order[index + 1]) if index + 1 < len(order) else None
+        softmax(*held)
+        held = following
+        if start and pair:
+            key_sums(pair - 1)
+    key_sums(PAIRS - 1)
     core = core_ref[0]
     targets = [(1 - core, send_hbm), (core, keep_hbm)]
     weight_terms(x, c, grads, ctx, terms, targets, sems, [(grads, grads_hbm), (ctx, ctx_hbm)])
@@ -169,17 +200,20 @@
         whole = jnp.concatenate([p.reshape(ROWS, CHUNK, PAIR) for p in pieces], axis=1)
         ref[:, base : base + PAIR] = whole.reshape(POSITIONS, PAIR)
 
-    for pair in range(PAIRS):
+    def products(pair):
         base = pair * PAIR
         query, key, value = [gather(proj, part * HALF_WIDTH + base) for part in range(3)]
         grad = gather(gctx, base)
         keys, values, queries, grad_parts = [[twice(t) for t in part] for part in (key, value, query, grad)]
         scores = jnp.concatenate([dot_nt(a, b) for a, b in zip(query, keys)], axis=0)
         grad_weights = jnp.concatenate([dot_nt(a, b) for a, b in zip(grad, values)], axis=0)
+        return base, keys, values, queries, grad_parts, scores, grad_weights
+
+    def finish(base, keys, values, queries, grad_parts, scores, grad_weights):
         rounded, dscores = [], []
         for half in range(2):
             lanes = slice(half * size, (half + 1) * size)
-            weights = probabilities(scores[:, lanes], allowed)
+            weights = chunk_probabilities(scores[:, lanes], allowed)
             rounded.append(weights.astype(BF))
             part = grad_weights[:, lanes]
             delta = jnp.sum(weights * part, axis=-1, keepdims=True)
@@ -197,6 +231,9 @@
         scatter(grads, base, dqs)
         scatter(grads, HALF_WIDTH + base, dks)
         scatter(grads, 2 * HALF_WIDTH + base, dvs)
+
+    for item in [products(pair) for pair in range(PAIRS)]:
+        finish(*item)
     core = core_ref[0]
     targets = [(1 - core, send_hbm), (core, keep_hbm)]
     back[:, WIDTH:] = ctx[...]
@@ -308,50 +345,70 @@
 
 def ring_sum_kernel(*refs):
     in_hbms, (out_hbm, terms, totals, sems, out_sems) = refs[:8], refs[9:]
-    ins = start_all(
-        [pltpu.make_async_copy(source, terms.at[index], sems.at[index]) for index, source in enumerate(in_hbms)]
-    )
+    ins = [
+        start_all(
+            [
+                pltpu.make_async_copy(source.at[z_hi], terms.at[index, z_hi], sems.at[index, z_hi])
+                for index, source in enumerate(in_hbms)
+            ]
+        )
+        for z_hi in range(2)
+    ]
     outs = []
-    for half in range(2):
-        wait_all(ins[4 * half : 4 * half + 4])
-        for z_hi in range(2):
+    for z_hi in range(2):
+        wait_all(ins[z_hi])
+        for half in range(2):
             total = sum(terms[4 * half + step, z_hi].astype(F32) for step in range(4))
             for z_lo in range(2):
                 totals[z_hi, :, z_lo, half] = total[:, 24 * z_lo : 24 * z_lo + 24].astype(BF)
-    for z_hi in range(2):
         outs += start_all([pltpu.make_async_copy(totals.at[z_hi], out_hbm.at[z_hi], out_sems.at[z_hi])])
     wait_all(outs)
 
 
-def group_sum_kernel(pieces_hbm, out_hbm, pieces, total, sems):
-    wait_all(start_all([pltpu.make_async_copy(pieces_hbm, pieces, sems.at[8])]))
-    total[...] = jnp.sum(pieces[...].astype(F32), axis=0).astype(BF)
+def group_sum_kernel(pieces_hbm, after, out_hbm, pieces, total, sems, in_sems):
+    ins = start_all(
+        [
+            pltpu.make_async_copy(pieces_hbm.at[pl.ds(4 * index, 4)], pieces.at[pl.ds(4 * index, 4)], in_sems.at[index])
+            for index in range(4)
+        ]
+    )
+    parts = []
+    for index in range(4):
+        ins[index].wait()
+        parts.append(jnp.sum(pieces[4 * index : 4 * index + 4].astype(F32), axis=0))
+    total[...] = sum(parts).astype(BF)
     wait_all(
         start_all([pltpu.make_async_copy(total, out_hbm.at[place], sems.at[place]) for place in range(8)])
     )
 
 
 def assemble_kernel(factor, whole_hbm, qkv_hbm, out_hbm, whole, qkv_grad, out_grad, sems):
-    wait_all(start_all([pltpu.make_async_copy(whole_hbm, whole, sems.at[0])]))
-    for place in range(8):
-        rows = slice(place // 4 * 24, place // 4 * 24 + 24)
-        part = place % 4
-        for half in range(2):
-            start = half * HALF_WIDTH
-            value = whole[place, half].astype(F32) * factor
-            if part < 3:
-                start += part * WIDTH
-                qkv_grad[rows, start : start + HALF_WIDTH] = value
-            else:
-                out_grad[rows, start : start + HALF_WIDTH] = value
-    wait_all(
-        start_all(
+    ins = start_all(
+        [
+            pltpu.make_async_copy(whole_hbm.at[pl.ds(4 * z_lo, 4)], whole.at[pl.ds(4 * z_lo, 4)], sems.at[0, z_lo])
+            for z_lo in range(2)
+        ]
+    )
+    outs = []
+    for z_lo in range(2):
+        ins[z_lo].wait()
+        rows, span = slice(24 * z_lo, 24 * z_lo + 24), pl.ds(24 * z_lo, 24)
+        for part in range(4):
+            for half in range(2):
+                value = whole[4 * z_lo + part, half].astype(F32) * factor
+                start = half * HALF_WIDTH
+                if part < 3:
+                    start += part * WIDTH
+                    qkv_grad[rows, start : start + HALF_WIDTH] = value
+                else:
+                    out_grad[rows, start : start + HALF_WIDTH] = value
+        outs += start_all(
             [
-                pltpu.make_async_copy(qkv_grad, qkv_hbm, sems.at[1]),
-                pltpu.make_async_copy(out_grad, out_hbm, sems.at[2]),
+                pltpu.make_async_copy(qkv_grad.at[span], qkv_hbm.at[span], sems.at[1, z_lo]),
+                pltpu.make_async_copy(out_grad.at[span], out_hbm.at[span], sems.at[2, z_lo]),
             ]
         )
-    )
+    wait_all(outs)
 
 
 SMEM = pl.BlockSpec(memory_space=pltpu.SMEM)
@@ -459,7 +516,7 @@
         row_kernel,
         (POSITIONS, WIDTH),
         [shape(POSITIONS, 3 * HALF_WIDTH), shape(POSITIONS, HALF_WIDTH)],
-        [buffer(2, POSITIONS, POSITIONS)] * 2,
+        [buffer(PAIRS, 2, POSITIONS, POSITIONS)] * 2,
         core, x, c, qkv_weight, out_weight,
     )
     terms_row = ring(pair_sum(x_index, keep_row, send_row))
@@ -497,7 +554,7 @@
         ring_sum_kernel,
         shape(2, 4, 2, 2, 24, HALF_WIDTH),
         2 * 10 ** 9,
-        [buffer(8, 2, 4, 48, HALF_WIDTH), buffer(2, 4, 2, 2, 24, HALF_WIDTH), copy_sems(8), copy_sems(2)],
+        [buffer(8, 2, 4, 48, HALF_WIDTH), buffer(2, 4, 2, 2, 24, HALF_WIDTH), copy_sems(8, 2), copy_sems(2)],
         (*terms_row, *terms_col, back),
     )
     pieces = swap(terms.reshape(16, 2, 24, HALF_WIDTH), ("dp", "ctx"), plane_groups())
@@ -505,8 +562,8 @@
         group_sum_kernel,
         shape(8, 2, 24, HALF_WIDTH),
         10 ** 9,
-        [buffer(16, 2, 24, HALF_WIDTH), buffer(2, 24, HALF_WIDTH), copy_sems(9)],
-        (pieces,),
+        [buffer(16, 2, 24, HALF_WIDTH), buffer(2, 24, HALF_WIDTH), copy_sems(8), copy_sems(4)],
+        (pieces, attention_out),
     )
     whole = swap(own, "ctx")
     factor = (lax.axis_size("dp") * lax.axis_size("ctx") * POSITIONS) ** (-0.5)
@@ -518,7 +575,7 @@
             buffer(8, 2, 24, HALF_WIDTH),
             buffer(48, 3 * WIDTH, dtype=F32),
             buffer(48, WIDTH, dtype=F32),
-            copy_sems(3),
+            copy_sems(3, 2),
         ],
         (whole,),
     )

time: 109 us -> 106 us (0.972)
  blocking collectives: 18.9 us -> 11.7 us
  starting transfers between devices: 25 us -> 29.2 us
  Pallas kernels: 43.7 us -> 40.2 us
  waiting for transfers between devices: 19 us -> 22.4 us
    all_to_all x1, blocking collectives: 18.9 us -> 11.7 us  [swap(): lax.all_to_all(part, axis, split_axis=0, concat_axis=0, tiled=True, axis_...]
    all_to_all x3, starting transfers between devices: 15.7 us -> 19.3 us  [swap(): lax.all_to_all(part, axis, split_axis=0, concat_axis=0, tiled=True, axis_...]
    pallas_call x10, Pallas kernels: 43.7 us -> 40.2 us  [call(): pl.pallas_call(kernel, out_shape=out_shape, in_specs=[SMEM] * scalars + [...]
    all_to_all x3, waiting for transfers between devices: 12.9 us -> 16.3 us  [swap(): lax.all_to_all(part, axis, split_axis=0, concat_axis=0, tiled=True, axis_...]
  transfers between devices with their start and end apart: 11 -> 11, of which waited for: 5 -> 5; matrix products, arithmetic and copies ran while one was open for 0% -> 0% of each run, Pallas kernels for 32% -> 30%
where the time goes in v3:
time: 106 us; the launch traced here: 104 us
  Pallas kernels  40.2 us (38%)
  starting transfers between devices  29.2 us (28%)
  waiting for transfers between devices  22.4 us (21%)
  blocking collectives  11.7 us (11%)
    pallas_call x10, Pallas kernels, call(): pl.pallas_call(kernel, out_shape=out_shape, in_specs=[SMEM] * scalars + [...  40.2 us
    all_to_all x3, starting transfers between devices, swap(): lax.all_to_all(part, axis, split_axis=0, concat_axis=0, tiled=True, axis_...  19.3 us
    all_to_all x3, waiting for transfers between devices, swap(): lax.all_to_all(part, axis, split_axis=0, concat_axis=0, tiled=True, axis_...  16.3 us
    all_to_all x1, blocking collectives, swap(): lax.all_to_all(part, axis, split_axis=0, concat_axis=0, tiled=True, axis_...  11.7 us
    ppermute x6, starting transfers between devices, ring(): lax.ppermute(parts[step], 'dp', [(i, (i + 4 * step) % 16) for i in range(...  9.72 us
    ppermute x2, waiting for transfers between devices, exchange(): return lax.ppermute(send, 'dp', [(i, i ^ 1) for i in range(16)])  3.16 us
    ppermute x6, waiting for transfers between devices, ring(): lax.ppermute(parts[step], 'dp', [(i, (i + 4 * step) % 16) for i in range(...  2.94 us
  transfers between devices with their start and end apart: 11, of which 5 were waited for; matrix products, arithmetic and copies ran while one was open for 0% of the time, Pallas kernels for 30%

profile of v3, /device:TPU:0, one launch (start us, length us, event | category | flops | bytes accessed | tf_op | source)
XLA Modules:
  0.0 104.5 jit_solution(7708071854921773443)
XLA Ops:
  0.6 2.3 %shard_map.76 = bf16[8,2,64,768]{3,2,1,0:T(8,128)(2,1)} custom-call(bf16[8,64,768]{2,1,0:T(8,128)(2,1)} %bitcast.12, bf16[8,64,768]{2,1,0:T(8,128)(2,1)} %bitcast.14), custom_call_target="tpu_custom_call" | custom-call | flops 1000000 | bytes 65536 | tf_op jit(solution)/shard_map/pallas_call | solution.py:432
  3.0 5.9 %all-to-all-start = ((bf16[8,2,64,768]{3,2,1,0:T(8,128)(2,1)}), bf16[8,2,64,768]{3,2,1,0:T(8,128)(2,1)}, u32[]{:S(2)}, u32[]{:S(2)}) async-start(bf16[8,2,64,768]{3,2,1,0:T(8,128)(2,1)} %shard_map.76), calls=%async_computation | async-start | bytes 3145728 | tf_op jit(solution)/shard_map/all_to_all | solution.py:467
  8.9 10.2 %shard_map.75 = (bf16[512,1152]{1,0:T(8,128)(2,1)}, bf16[512,384]{1,0:T(8,128)(2,1)}, bf16[8,4,48,384]{3,2,1,0:T(8,128)(2,1)}, bf16[8,4,48,384]{3,2,1,0:T(8,128)(2,1)}) custom-call(s32[1]{0:T(128)} %bitcast.core_ref, bf16[512,768]{1,0:T(8,128)(2,1)} %bitcast.13, bf16[512,768]{1,0:T(8,128)(2,1)} %bitcast.15, bf16[768,2304]{1,0:T(8,128)(2,1)} %qkv_hbm.5, ...), custom_call_target="tpu_custom_call" | custom-call | flops 20000000000 | bytes 65536 | tf_op jit(solution)/shard_map/pallas_call | solution.py:432
  19.2 3.2 %collective-permute-done.received_hbm = bf16[8,4,48,384]{3,2,1,0:T(8,128)(2,1)} collective-permute-done((bf16[8,4,48,384]{3,2,1,0:T(8,128)(2,1)}, bf16[8,4,48,384]{3,2,1,0:T(8,128)(2,1)}, u32[]{:S(2)}, u32[]{:S(2)}) %collective-permute-start) | collective-permute-done | bytes 1179680 | tf_op jit(solution)/shard_map/ppermute | solution.py:482
  22.4 2.5 %shard_map.77 = (bf16[2,4,48,384]{3,2,1,0:T(8,128)(2,1)}, bf16[2,4,48,384]{3,2,1,0:T(8,128)(2,1)}, bf16[2,4,48,384]{3,2,1,0:T(8,128)(2,1)}, bf16[2,4,48,384]{3,2,1,0:T(8,128)(2,1)}) custom-call(s32[1]{0:T(128)} %bitcast.5.x_ref, bf16[8,4,48,384]{3,2,1,0:T(8,128)(2,1)} %get-tuple-element.25.keep_hbm, bf16[8,4,48,384]{3,2,1,0:T(8,128)(2,1)} %collective-permute-done.received_hbm), custom_call_target="tpu_custom_call" | custom-call | flops 2000000000 | bytes 65536 | tf_op jit(solution)/shard_map/pallas_call | solution.py:432
  24.9 1.6 %collective-permute-start.1 = (bf16[2,4,48,384]{3,2,1,0:T(8,128)(2,1)}, bf16[2,4,48,384]{3,2,1,0:T(8,128)(2,1)}, u32[]{:S(2)}, u32[]{:S(2)}) collective-permute-start(bf16[2,4,48,384]{3,2,1,0:T(8,128)(2,1)} %get-tuple-element.31), channel_id=1, source_target_pairs={{0,32},{8,40},{16,48},{24,56},{32,64},{40,72},{48,80},{56,88},{64,... | collective-permute-start | bytes 884744 | tf_op jit(solution)/shard_map/ppermute | solution.py:497
  26.4 2.7 %collective-permute-start.2 = (bf16[2,4,48,384]{3,2,1,0:T(8,128)(2,1)}, bf16[2,4,48,384]{3,2,1,0:T(8,128)(2,1)}, u32[]{:S(2)}, u32[]{:S(2)}) collective-permute-start(bf16[2,4,48,384]{3,2,1,0:T(8,128)(2,1)} %get-tuple-element.32), channel_id=1, source_target_pairs={{0,64},{8,72},{16,80},{24,88},{32,96},{40,104},{48,112},{56,120},{... | collective-permute-start | bytes 884744 | tf_op jit(solution)/shard_map/ppermute | solution.py:497
  29.2 1.4 %collective-permute-start.3 = (bf16[2,4,48,384]{3,2,1,0:T(8,128)(2,1)}, bf16[2,4,48,384]{3,2,1,0:T(8,128)(2,1)}, u32[]{:S(2)}, u32[]{:S(2)}) collective-permute-start(bf16[2,4,48,384]{3,2,1,0:T(8,128)(2,1)} %get-tuple-element.33), channel_id=1, source_target_pairs={{0,96},{8,104},{16,112},{24,120},{32,0},{40,8},{48,16},{56,24},{64... | collective-permute-start | bytes 884744 | tf_op jit(solution)/shard_map/ppermute | solution.py:497
  30.6 9.8 %shard_map.78 = (bf16[512,1152]{1,0:T(8,128)(2,1)}, bf16[8,4,48,384]{3,2,1,0:T(8,128)(2,1)}, bf16[8,4,48,384]{3,2,1,0:T(8,128)(2,1)}) custom-call(s32[1]{0:T(128)} %bitcast.core_ref, bf16[8,2,64,768]{3,2,1,0:T(8,128)(2,1)} %all-to-all-done.both_hbm, bf16[768,2304]{1,0:T(8,128)(2,1)} %qkv_hbm.5, bf16[768,768]{1,0:T(8,128)(2,1)} %out_hbm.5, ...), custom_call_target="tpu_custom_call" | custom-call | flops 20000000000 | bytes 65536 | tf_op jit(solution)/shard_map/pallas_call | solution.py:432
  40.5 5.7 %all-to-all-start.1 = ((bf16[8,64,1152]{2,1,0:T(8,128)(2,1)}), bf16[8,64,1152]{2,1,0:T(8,128)(2,1)}, u32[]{:S(2)}, u32[]{:S(2)}) async-start(bf16[8,64,1152]{2,1,0:T(8,128)(2,1)} %bitcast.11), calls=%async_computation.1 | async-start | bytes 2359296 | tf_op jit(solution)/shard_map/all_to_all | solution.py:467
  46.9 2.5 %shard_map.81 = (bf16[2,4,48,384]{3,2,1,0:T(8,128)(2,1)}, bf16[2,4,48,384]{3,2,1,0:T(8,128)(2,1)}, bf16[2,4,48,384]{3,2,1,0:T(8,128)(2,1)}, bf16[2,4,48,384]{3,2,1,0:T(8,128)(2,1)}) custom-call(s32[1]{0:T(128)} %bitcast.5.x_ref, bf16[8,4,48,384]{3,2,1,0:T(8,128)(2,1)} %get-tuple-element.34.keep_hbm, ...), custom_call_target="tpu_custom_call" | custom-call | flops 2000000000 | bytes 65536 | tf_op jit(solution)/shard_map/pallas_call | solution.py:432
  49.4 0.7 collective-permute-start.5
  50.0 1.9 %collective-permute-start.6 = (bf16[2,4,48,384]{3,2,1,0:T(8,128)(2,1)}, bf16[2,4,48,384]{3,2,1,0:T(8,128)(2,1)}, u32[]{:S(2)}, u32[]{:S(2)}) collective-permute-start(bf16[2,4,48,384]{3,2,1,0:T(8,128)(2,1)} %get-tuple-element.38), channel_id=1, source_target_pairs={{0,64},{8,72},{16,80},{24,88},{32,96},{40,104},{48,112},{56,120},{... | collective-permute-start | bytes 884744 | tf_op jit(solution)/shard_map/ppermute | solution.py:497
  51.9 1.4 %collective-permute-start.7 = (bf16[2,4,48,384]{3,2,1,0:T(8,128)(2,1)}, bf16[2,4,48,384]{3,2,1,0:T(8,128)(2,1)}, u32[]{:S(2)}, u32[]{:S(2)}) collective-permute-start(bf16[2,4,48,384]{3,2,1,0:T(8,128)(2,1)} %get-tuple-element.39), channel_id=1, source_target_pairs={{0,96},{8,104},{16,112},{24,120},{32,0},{40,8},{48,16},{56,24},{64... | collective-permute-start | bytes 884744 | tf_op jit(solution)/shard_map/ppermute | solution.py:497
  53.4 10.7 %all-to-all-done.1 = bf16[8,64,1152]{2,1,0:T(8,128)(2,1)} async-done(((bf16[8,64,1152]{2,1,0:T(8,128)(2,1)}), bf16[8,64,1152]{2,1,0:T(8,128)(2,1)}, u32[]{:S(2)}, u32[]{:S(2)}) %all-to-all-start.1) | async-done | bytes 1179680 | tf_op jit(solution)/shard_map/all_to_all | solution.py:467
  64.1 2.3 %collective-permute-done.5.refs_5_ = bf16[2,4,48,384]{3,2,1,0:T(8,128)(2,1)} collective-permute-done((bf16[2,4,48,384]{3,2,1,0:T(8,128)(2,1)}, bf16[2,4,48,384]{3,2,1,0:T(8,128)(2,1)}, u32[]{:S(2)}, u32[]{:S(2)}) %collective-permute-start.5) | collective-permute-done | bytes 294944 | tf_op jit(solution)/shard_map/ppermute | solution.py:497
  66.4 0.6 collective-permute-done.7.refs_7_
  67.0 2.7 %shard_map.82 = bf16[2,4,2,2,24,384]{5,4,3,2,1,0:T(8,128)(2,1)} custom-call(bf16[2,4,48,384]{3,2,1,0:T(8,128)(2,1)} %get-tuple-element.27.after.refs_0_, bf16[2,4,48,384]{3,2,1,0:T(8,128)(2,1)} %collective-permute-done.1.first.refs_1_, bf16[2,4,48,384]{3,2,1,0:T(8,128)(2,1)} %collective-permute-done.2.second.refs_2_, ...), custom_call_target="tpu_custom_call" | custom-call | flops 2000000000 | bytes 65536 | tf_op jit(solution)/shard_map/pallas_call | solution.py:432
  69.8 7.7 %all-to-all-start.2 = ((bf16[16,2,24,384]{3,2,1,0:T(8,128)(2,1)}), bf16[16,2,24,384]{3,2,1,0:T(8,128)(2,1)}, u32[]{:S(2)}, u32[]{:S(2)}) async-start(bf16[16,2,24,384]{3,2,1,0:T(8,128)(2,1)} %bitcast.16), calls=%async_computation.2 | async-start | bytes 1179648 | tf_op jit(solution)/shard_map/all_to_all | solution.py:467
  77.5 5.8 %shard_map.79 = (bf16[512,768]{1,0:T(8,128)(2,1)}, bf16[512,768]{1,0:T(8,128)(2,1)}) custom-call(bf16[512,1152]{1,0:T(8,128)(2,1)} %get-tuple-element.23.grads_hbm, bf16[512,384]{1,0:T(8,128)(2,1)} %get-tuple-element.24.ctx_hbm, bf16[512,1152]{1,0:T(8,128)(2,1)} %bitcast.7.back_hbm.refs_8_, bf16[768,2304]{1,0:T(8,128)(2,1)} %qkv_hbm.5, bf16[768,768]{1,0:T(8,128)(2,1)} %out_hbm.5), custom_call_target="tpu_custom_call" | custom-call | flops 4000000000 | bytes 65536 | tf_op jit(solution)/shard_map/pallas_call | solution.py:432
  83.3 5.5 %all-to-all-done.2.pieces_hbm = bf16[16,2,24,384]{3,2,1,0:T(8,128)(2,1)} async-done(((bf16[16,2,24,384]{3,2,1,0:T(8,128)(2,1)}), bf16[16,2,24,384]{3,2,1,0:T(8,128)(2,1)}, u32[]{:S(2)}, u32[]{:S(2)}) %all-to-all-start.2) | async-done | bytes 589856 | tf_op jit(solution)/shard_map/all_to_all | solution.py:467
  88.8 2.0 %shard_map.83 = bf16[8,2,24,384]{3,2,1,0:T(8,128)(2,1)} custom-call(bf16[16,2,24,384]{3,2,1,0:T(8,128)(2,1)} %all-to-all-done.2.pieces_hbm, bf16[512,768]{1,0:T(8,128)(2,1)} %get-tuple-element.29.after), custom_call_target="tpu_custom_call" | custom-call | flops 1000000000 | bytes 65536 | tf_op jit(solution)/shard_map/pallas_call | solution.py:432
  90.8 11.7 %all_to_all.20.whole_hbm = bf16[8,2,24,384]{3,2,1,0:T(8,128)(2,1)} all-to-all(bf16[8,2,24,384]{3,2,1,0:T(8,128)(2,1)} %shard_map.83), channel_id=1, replica_groups=mesh['dp'=16,'ctx'=8] {'ctx'}, dimensions={0} | all-to-all | bytes 589824 | tf_op jit(solution)/shard_map/all_to_all | solution.py:467
  102.5 1.8 %shard_map.84 = (f32[48,2304]{1,0:T(8,128)}, f32[48,768]{1,0:T(8,128)}) custom-call(bf16[8,2,24,384]{3,2,1,0:T(8,128)(2,1)} %all_to_all.20.whole_hbm), custom_call_target="tpu_custom_call" | custom-call | flops 1000000 | bytes 65536 | tf_op jit(solution)/shard_map/pallas_call | solution.py:432
  (9 shorter events, 0.8 us)
Async XLA Ops:
  3.0 27.6 %all-to-all-start = ((bf16[8,2,64,768]{3,2,1,0:T(8,128)(2,1)}), bf16[8,2,64,768]{3,2,1,0:T(8,128)(2,1)}, u32[]{:S(2)}, u32[]{:S(2)}) async-start(bf16[8,2,64,768]{3,2,1,0:T(8,128)(2,1)} %shard_map.76), calls=%async_computation | async-start | bytes 3145728 | tf_op jit(solution)/shard_map/all_to_all | solution.py:467
  19.1 3.3 %collective-permute-start = (bf16[8,4,48,384]{3,2,1,0:T(8,128)(2,1)}, bf16[8,4,48,384]{3,2,1,0:T(8,128)(2,1)}, u32[]{:S(2)}, u32[]{:S(2)}) collective-permute-start(bf16[8,4,48,384]{3,2,1,0:T(8,128)(2,1)} %get-tuple-element.26), channel_id=1, source_target_pairs={{0,8},{8,0},{16,24},{24,16},{32,40},{40,32},{48,56},{56,48},{64,72... | collective-permute-start | bytes 3538952 | tf_op jit(solution)/shard_map/ppermute | solution.py:482
  24.9 21.4 %collective-permute-start.1 = (bf16[2,4,48,384]{3,2,1,0:T(8,128)(2,1)}, bf16[2,4,48,384]{3,2,1,0:T(8,128)(2,1)}, u32[]{:S(2)}, u32[]{:S(2)}) collective-permute-start(bf16[2,4,48,384]{3,2,1,0:T(8,128)(2,1)} %get-tuple-element.31), channel_id=1, source_target_pairs={{0,32},{8,40},{16,48},{24,56},{32,64},{40,72},{48,80},{56,88},{64,... | collective-permute-start | bytes 884744 | tf_op jit(solution)/shard_map/ppermute | solution.py:497
  26.4 19.8 %collective-permute-start.2 = (bf16[2,4,48,384]{3,2,1,0:T(8,128)(2,1)}, bf16[2,4,48,384]{3,2,1,0:T(8,128)(2,1)}, u32[]{:S(2)}, u32[]{:S(2)}) collective-permute-start(bf16[2,4,48,384]{3,2,1,0:T(8,128)(2,1)} %get-tuple-element.32), channel_id=1, source_target_pairs={{0,64},{8,72},{16,80},{24,88},{32,96},{40,104},{48,112},{56,120},{... | collective-permute-start | bytes 884744 | tf_op jit(solution)/shard_map/ppermute | solution.py:497
  29.2 17.1 %collective-permute-start.3 = (bf16[2,4,48,384]{3,2,1,0:T(8,128)(2,1)}, bf16[2,4,48,384]{3,2,1,0:T(8,128)(2,1)}, u32[]{:S(2)}, u32[]{:S(2)}) collective-permute-start(bf16[2,4,48,384]{3,2,1,0:T(8,128)(2,1)} %get-tuple-element.33), channel_id=1, source_target_pairs={{0,96},{8,104},{16,112},{24,120},{32,0},{40,8},{48,16},{56,24},{64... | collective-permute-start | bytes 884744 | tf_op jit(solution)/shard_map/ppermute | solution.py:497
  40.4 6.4 %collective-permute-start.4 = (bf16[8,4,48,384]{3,2,1,0:T(8,128)(2,1)}, bf16[8,4,48,384]{3,2,1,0:T(8,128)(2,1)}, u32[]{:S(2)}, u32[]{:S(2)}) collective-permute-start(bf16[8,4,48,384]{3,2,1,0:T(8,128)(2,1)} %get-tuple-element.35), channel_id=1, source_target_pairs={{0,8},{8,0},{16,24},{24,16},{32,40},{40,32},{48,56},{56,48},{64,72... | collective-permute-start | bytes 3538952 | tf_op jit(solution)/shard_map/ppermute | solution.py:482
  40.5 23.6 %all-to-all-start.1 = ((bf16[8,64,1152]{2,1,0:T(8,128)(2,1)}), bf16[8,64,1152]{2,1,0:T(8,128)(2,1)}, u32[]{:S(2)}, u32[]{:S(2)}) async-start(bf16[8,64,1152]{2,1,0:T(8,128)(2,1)} %bitcast.11), calls=%async_computation.1 | async-start | bytes 2359296 | tf_op jit(solution)/shard_map/all_to_all | solution.py:467
  49.4 17.0 %collective-permute-start.5 = (bf16[2,4,48,384]{3,2,1,0:T(8,128)(2,1)}, bf16[2,4,48,384]{3,2,1,0:T(8,128)(2,1)}, u32[]{:S(2)}, u32[]{:S(2)}) collective-permute-start(bf16[2,4,48,384]{3,2,1,0:T(8,128)(2,1)} %get-tuple-element.37), channel_id=1, source_target_pairs={{0,32},{8,40},{16,48},{24,56},{32,64},{40,72},{48,80},{56,88},{64,... | collective-permute-start | bytes 884744 | tf_op jit(solution)/shard_map/ppermute | solution.py:497
  50.0 16.4 %collective-permute-start.6 = (bf16[2,4,48,384]{3,2,1,0:T(8,128)(2,1)}, bf16[2,4,48,384]{3,2,1,0:T(8,128)(2,1)}, u32[]{:S(2)}, u32[]{:S(2)}) collective-permute-start(bf16[2,4,48,384]{3,2,1,0:T(8,128)(2,1)} %get-tuple-element.38), channel_id=1, source_target_pairs={{0,64},{8,72},{16,80},{24,88},{32,96},{40,104},{48,112},{56,120},{... | collective-permute-start | bytes 884744 | tf_op jit(solution)/shard_map/ppermute | solution.py:497
  51.9 15.1 %collective-permute-start.7 = (bf16[2,4,48,384]{3,2,1,0:T(8,128)(2,1)}, bf16[2,4,48,384]{3,2,1,0:T(8,128)(2,1)}, u32[]{:S(2)}, u32[]{:S(2)}) collective-permute-start(bf16[2,4,48,384]{3,2,1,0:T(8,128)(2,1)} %get-tuple-element.39), channel_id=1, source_target_pairs={{0,96},{8,104},{16,112},{24,120},{32,0},{40,8},{48,16},{56,24},{64... | collective-permute-start | bytes 884744 | tf_op jit(solution)/shard_map/ppermute | solution.py:497
  69.8 19.1 %all-to-all-start.2 = ((bf16[16,2,24,384]{3,2,1,0:T(8,128)(2,1)}), bf16[16,2,24,384]{3,2,1,0:T(8,128)(2,1)}, u32[]{:S(2)}, u32[]{:S(2)}) async-start(bf16[16,2,24,384]{3,2,1,0:T(8,128)(2,1)} %bitcast.16), calls=%async_computation.2 | async-start | bytes 1179648 | tf_op jit(solution)/shard_map/all_to_all | solution.py:467

commit v4 on v3

--- a/solution.py
+++ b/solution.py
@@ -382,16 +382,9 @@
     )
 
 
-def assemble_kernel(factor, whole_hbm, qkv_hbm, out_hbm, whole, qkv_grad, out_grad, sems):
-    ins = start_all(
-        [
-            pltpu.make_async_copy(whole_hbm.at[pl.ds(4 * z_lo, 4)], whole.at[pl.ds(4 * z_lo, 4)], sems.at[0, z_lo])
-            for z_lo in range(2)
-        ]
-    )
+def assemble_kernel(factor, whole, qkv_hbm, out_hbm, qkv_grad, out_grad, sems):
     outs = []
     for z_lo in range(2):
-        ins[z_lo].wait()
         rows, span = slice(24 * z_lo, 24 * z_lo + 24), pl.ds(24 * z_lo, 24)
         for part in range(4):
             for half in range(2):
@@ -404,8 +397,8 @@
                     out_grad[rows, start : start + HALF_WIDTH] = value
         outs += start_all(
             [
-                pltpu.make_async_copy(qkv_grad.at[span], qkv_hbm.at[span], sems.at[1, z_lo]),
-                pltpu.make_async_copy(out_grad.at[span], out_hbm.at[span], sems.at[2, z_lo]),
+                pltpu.make_async_copy(qkv_grad.at[span], qkv_hbm.at[span], sems.at[0, z_lo]),
+                pltpu.make_async_copy(out_grad.at[span], out_hbm.at[span], sems.at[1, z_lo]),
             ]
         )
     wait_all(outs)
@@ -427,12 +420,12 @@
     return jax.ShapeDtypeStruct(dims, dtype)
 
 
-def call(kernel, out_shape, flops, scratch, arrays, mib=64):
+def call(kernel, out_shape, flops, scratch, arrays, mib=64, held=None):
     scalars = sum(1 for array in arrays if array.ndim == 1)
     return pl.pallas_call(
         kernel,
         out_shape=out_shape,
-        in_specs=[SMEM] * scalars + [HBM] * (len(arrays) - scalars),
+        in_specs=[SMEM] * scalars + [held or HBM] * (len(arrays) - scalars),
         out_specs=jax.tree.map(lambda _: HBM, out_shape),
         scratch_shapes=scratch,
         compiler_params=pltpu.CompilerParams(vmem_limit_bytes=mib * MIB),
@@ -572,12 +565,13 @@
         (shape(48, 3 * WIDTH, dtype=F32), shape(48, WIDTH, dtype=F32)),
         10 ** 6,
         [
-            buffer(8, 2, 24, HALF_WIDTH),
             buffer(48, 3 * WIDTH, dtype=F32),
             buffer(48, WIDTH, dtype=F32),
-            copy_sems(3, 2),
+            copy_sems(2, 2),
         ],
         (whole,),
+        mib=8,
+        held=pl.BlockSpec(memory_space=pltpu.VMEM),
     )
     return (attention_out[None], normed_grad[None], qkv_grad, out_grad)
 

time: 106 us -> 104 us (0.981)
  transfers between devices with their start and end apart: 11 -> 11, of which waited for: 5 -> 5; matrix products, arithmetic and copies ran while one was open for 0% -> 0% of each run, Pallas kernels for 30% -> 31%
where the time goes in v4:
time: 104 us; the launch traced here: 103 us
  Pallas kernels  39.3 us (38%)
  starting transfers between devices  29.2 us (28%)
  waiting for transfers between devices  22.4 us (22%)
  blocking collectives  11 us (11%)
    pallas_call x10, Pallas kernels, call(): pl.pallas_call(kernel, out_shape=out_shape, in_specs=[SMEM] * scalars + [...  39.3 us
    all_to_all x3, starting transfers between devices, swap(): lax.all_to_all(part, axis, split_axis=0, concat_axis=0, tiled=True, axis_...  19.3 us
    all_to_all x3, waiting for transfers between devices, swap(): lax.all_to_all(part, axis, split_axis=0, concat_axis=0, tiled=True, axis_...  16.3 us
    all_to_all x1, blocking collectives, swap(): lax.all_to_all(part, axis, split_axis=0, concat_axis=0, tiled=True, axis_...  11 us
    ppermute x6, starting transfers between devices, ring(): lax.ppermute(parts[step], 'dp', [(i, (i + 4 * step) % 16) for i in range(...  9.72 us
    ppermute x2, waiting for transfers between devices, exchange(): return lax.ppermute(send, 'dp', [(i, i ^ 1) for i in range(16)])  3.16 us
    ppermute x6, waiting for transfers between devices, ring(): lax.ppermute(parts[step], 'dp', [(i, (i + 4 * step) % 16) for i in range(...  2.94 us
  transfers between devices with their start and end apart: 11, of which 5 were waited for; matrix products, arithmetic and copies ran while one was open for 0% of the time, Pallas kernels for 31%

profile of v4, /device:TPU:0, one launch (start us, length us, event | category | flops | bytes accessed | tf_op | source)
XLA Modules:
  0.0 102.8 jit_solution(11306860429444400879)
XLA Ops:
  0.6 2.3 %shard_map.76 = bf16[8,2,64,768]{3,2,1,0:T(8,128)(2,1)} custom-call(bf16[8,64,768]{2,1,0:T(8,128)(2,1)} %bitcast.12, bf16[8,64,768]{2,1,0:T(8,128)(2,1)} %bitcast.14), custom_call_target="tpu_custom_call" | custom-call | flops 1000000 | bytes 65536 | tf_op jit(solution)/shard_map/pallas_call | solution.py:425
  3.0 5.9 %all-to-all-start = ((bf16[8,2,64,768]{3,2,1,0:T(8,128)(2,1)}), bf16[8,2,64,768]{3,2,1,0:T(8,128)(2,1)}, u32[]{:S(2)}, u32[]{:S(2)}) async-start(bf16[8,2,64,768]{3,2,1,0:T(8,128)(2,1)} %shard_map.76), calls=%async_computation | async-start | bytes 3145728 | tf_op jit(solution)/shard_map/all_to_all | solution.py:460
  8.9 10.2 %shard_map.75 = (bf16[512,1152]{1,0:T(8,128)(2,1)}, bf16[512,384]{1,0:T(8,128)(2,1)}, bf16[8,4,48,384]{3,2,1,0:T(8,128)(2,1)}, bf16[8,4,48,384]{3,2,1,0:T(8,128)(2,1)}) custom-call(s32[1]{0:T(128)} %bitcast.core_ref, bf16[512,768]{1,0:T(8,128)(2,1)} %bitcast.13, bf16[512,768]{1,0:T(8,128)(2,1)} %bitcast.15, bf16[768,2304]{1,0:T(8,128)(2,1)} %qkv_hbm.5, ...), custom_call_target="tpu_custom_call" | custom-call | flops 20000000000 | bytes 65536 | tf_op jit(solution)/shard_map/pallas_call | solution.py:425
  19.2 3.2 %collective-permute-done.received_hbm = bf16[8,4,48,384]{3,2,1,0:T(8,128)(2,1)} collective-permute-done((bf16[8,4,48,384]{3,2,1,0:T(8,128)(2,1)}, bf16[8,4,48,384]{3,2,1,0:T(8,128)(2,1)}, u32[]{:S(2)}, u32[]{:S(2)}) %collective-permute-start) | collective-permute-done | bytes 1179680 | tf_op jit(solution)/shard_map/ppermute | solution.py:475
  22.4 2.5 %shard_map.77 = (bf16[2,4,48,384]{3,2,1,0:T(8,128)(2,1)}, bf16[2,4,48,384]{3,2,1,0:T(8,128)(2,1)}, bf16[2,4,48,384]{3,2,1,0:T(8,128)(2,1)}, bf16[2,4,48,384]{3,2,1,0:T(8,128)(2,1)}) custom-call(s32[1]{0:T(128)} %bitcast.5.x_ref, bf16[8,4,48,384]{3,2,1,0:T(8,128)(2,1)} %get-tuple-element.25.keep_hbm, bf16[8,4,48,384]{3,2,1,0:T(8,128)(2,1)} %collective-permute-done.received_hbm), custom_call_target="tpu_custom_call" | custom-call | flops 2000000000 | bytes 65536 | tf_op jit(solution)/shard_map/pallas_call | solution.py:425
  24.9 1.6 %collective-permute-start.1 = (bf16[2,4,48,384]{3,2,1,0:T(8,128)(2,1)}, bf16[2,4,48,384]{3,2,1,0:T(8,128)(2,1)}, u32[]{:S(2)}, u32[]{:S(2)}) collective-permute-start(bf16[2,4,48,384]{3,2,1,0:T(8,128)(2,1)} %get-tuple-element.31), channel_id=1, source_target_pairs={{0,32},{8,40},{16,48},{24,56},{32,64},{40,72},{48,80},{56,88},{64,... | collective-permute-start | bytes 884744 | tf_op jit(solution)/shard_map/ppermute | solution.py:490
  26.4 2.7 %collective-permute-start.2 = (bf16[2,4,48,384]{3,2,1,0:T(8,128)(2,1)}, bf16[2,4,48,384]{3,2,1,0:T(8,128)(2,1)}, u32[]{:S(2)}, u32[]{:S(2)}) collective-permute-start(bf16[2,4,48,384]{3,2,1,0:T(8,128)(2,1)} %get-tuple-element.32), channel_id=1, source_target_pairs={{0,64},{8,72},{16,80},{24,88},{32,96},{40,104},{48,112},{56,120},{... | collective-permute-start | bytes 884744 | tf_op jit(solution)/shard_map/ppermute | solution.py:490
  29.2 1.4 %collective-permute-start.3 = (bf16[2,4,48,384]{3,2,1,0:T(8,128)(2,1)}, bf16[2,4,48,384]{3,2,1,0:T(8,128)(2,1)}, u32[]{:S(2)}, u32[]{:S(2)}) collective-permute-start(bf16[2,4,48,384]{3,2,1,0:T(8,128)(2,1)} %get-tuple-element.33), channel_id=1, source_target_pairs={{0,96},{8,104},{16,112},{24,120},{32,0},{40,8},{48,16},{56,24},{64... | collective-permute-start | bytes 884744 | tf_op jit(solution)/shard_map/ppermute | solution.py:490
  30.6 9.8 %shard_map.78 = (bf16[512,1152]{1,0:T(8,128)(2,1)}, bf16[8,4,48,384]{3,2,1,0:T(8,128)(2,1)}, bf16[8,4,48,384]{3,2,1,0:T(8,128)(2,1)}) custom-call(s32[1]{0:T(128)} %bitcast.core_ref, bf16[8,2,64,768]{3,2,1,0:T(8,128)(2,1)} %all-to-all-done.both_hbm, bf16[768,2304]{1,0:T(8,128)(2,1)} %qkv_hbm.5, bf16[768,768]{1,0:T(8,128)(2,1)} %out_hbm.5, ...), custom_call_target="tpu_custom_call" | custom-call | flops 20000000000 | bytes 65536 | tf_op jit(solution)/shard_map/pallas_call | solution.py:425
  40.5 5.7 %all-to-all-start.1 = ((bf16[8,64,1152]{2,1,0:T(8,128)(2,1)}), bf16[8,64,1152]{2,1,0:T(8,128)(2,1)}, u32[]{:S(2)}, u32[]{:S(2)}) async-start(bf16[8,64,1152]{2,1,0:T(8,128)(2,1)} %bitcast.11), calls=%async_computation.1 | async-start | bytes 2359296 | tf_op jit(solution)/shard_map/all_to_all | solution.py:460
  46.9 2.5 %shard_map.81 = (bf16[2,4,48,384]{3,2,1,0:T(8,128)(2,1)}, bf16[2,4,48,384]{3,2,1,0:T(8,128)(2,1)}, bf16[2,4,48,384]{3,2,1,0:T(8,128)(2,1)}, bf16[2,4,48,384]{3,2,1,0:T(8,128)(2,1)}) custom-call(s32[1]{0:T(128)} %bitcast.5.x_ref, bf16[8,4,48,384]{3,2,1,0:T(8,128)(2,1)} %get-tuple-element.34.keep_hbm, ...), custom_call_target="tpu_custom_call" | custom-call | flops 2000000000 | bytes 65536 | tf_op jit(solution)/shard_map/pallas_call | solution.py:425
  49.4 0.7 collective-permute-start.5
  50.0 1.9 %collective-permute-start.6 = (bf16[2,4,48,384]{3,2,1,0:T(8,128)(2,1)}, bf16[2,4,48,384]{3,2,1,0:T(8,128)(2,1)}, u32[]{:S(2)}, u32[]{:S(2)}) collective-permute-start(bf16[2,4,48,384]{3,2,1,0:T(8,128)(2,1)} %get-tuple-element.38), channel_id=1, source_target_pairs={{0,64},{8,72},{16,80},{24,88},{32,96},{40,104},{48,112},{56,120},{... | collective-permute-start | bytes 884744 | tf_op jit(solution)/shard_map/ppermute | solution.py:490
  51.9 1.4 %collective-permute-start.7 = (bf16[2,4,48,384]{3,2,1,0:T(8,128)(2,1)}, bf16[2,4,48,384]{3,2,1,0:T(8,128)(2,1)}, u32[]{:S(2)}, u32[]{:S(2)}) collective-permute-start(bf16[2,4,48,384]{3,2,1,0:T(8,128)(2,1)} %get-tuple-element.39), channel_id=1, source_target_pairs={{0,96},{8,104},{16,112},{24,120},{32,0},{40,8},{48,16},{56,24},{64... | collective-permute-start | bytes 884744 | tf_op jit(solution)/shard_map/ppermute | solution.py:490
  53.4 10.7 %all-to-all-done.1 = bf16[8,64,1152]{2,1,0:T(8,128)(2,1)} async-done(((bf16[8,64,1152]{2,1,0:T(8,128)(2,1)}), bf16[8,64,1152]{2,1,0:T(8,128)(2,1)}, u32[]{:S(2)}, u32[]{:S(2)}) %all-to-all-start.1) | async-done | bytes 1179680 | tf_op jit(solution)/shard_map/all_to_all | solution.py:460
  64.1 2.3 %collective-permute-done.5.refs_5_ = bf16[2,4,48,384]{3,2,1,0:T(8,128)(2,1)} collective-permute-done((bf16[2,4,48,384]{3,2,1,0:T(8,128)(2,1)}, bf16[2,4,48,384]{3,2,1,0:T(8,128)(2,1)}, u32[]{:S(2)}, u32[]{:S(2)}) %collective-permute-start.5) | collective-permute-done | bytes 294944 | tf_op jit(solution)/shard_map/ppermute | solution.py:490
  66.4 0.6 collective-permute-done.7.refs_7_
  67.0 2.7 %shard_map.82 = bf16[2,4,2,2,24,384]{5,4,3,2,1,0:T(8,128)(2,1)} custom-call(bf16[2,4,48,384]{3,2,1,0:T(8,128)(2,1)} %get-tuple-element.27.after.refs_0_, bf16[2,4,48,384]{3,2,1,0:T(8,128)(2,1)} %collective-permute-done.1.first.refs_1_, bf16[2,4,48,384]{3,2,1,0:T(8,128)(2,1)} %collective-permute-done.2.second.refs_2_, ...), custom_call_target="tpu_custom_call" | custom-call | flops 2000000000 | bytes 65536 | tf_op jit(solution)/shard_map/pallas_call | solution.py:425
  69.8 7.7 %all-to-all-start.2 = ((bf16[16,2,24,384]{3,2,1,0:T(8,128)(2,1)}), bf16[16,2,24,384]{3,2,1,0:T(8,128)(2,1)}, u32[]{:S(2)}, u32[]{:S(2)}) async-start(bf16[16,2,24,384]{3,2,1,0:T(8,128)(2,1)} %bitcast.16), calls=%async_computation.2 | async-start | bytes 1179648 | tf_op jit(solution)/shard_map/all_to_all | solution.py:460
  77.5 5.8 %shard_map.79 = (bf16[512,768]{1,0:T(8,128)(2,1)}, bf16[512,768]{1,0:T(8,128)(2,1)}) custom-call(bf16[512,1152]{1,0:T(8,128)(2,1)} %get-tuple-element.23.grads_hbm, bf16[512,384]{1,0:T(8,128)(2,1)} %get-tuple-element.24.ctx_hbm, bf16[512,1152]{1,0:T(8,128)(2,1)} %bitcast.7.back_hbm.refs_8_, bf16[768,2304]{1,0:T(8,128)(2,1)} %qkv_hbm.5, bf16[768,768]{1,0:T(8,128)(2,1)} %out_hbm.5), custom_call_target="tpu_custom_call" | custom-call | flops 4000000000 | bytes 65536 | tf_op jit(solution)/shard_map/pallas_call | solution.py:425
  83.3 5.5 %all-to-all-done.2.pieces_hbm = bf16[16,2,24,384]{3,2,1,0:T(8,128)(2,1)} async-done(((bf16[16,2,24,384]{3,2,1,0:T(8,128)(2,1)}), bf16[16,2,24,384]{3,2,1,0:T(8,128)(2,1)}, u32[]{:S(2)}, u32[]{:S(2)}) %all-to-all-start.2) | async-done | bytes 589856 | tf_op jit(solution)/shard_map/all_to_all | solution.py:460
  88.8 2.0 %shard_map.83 = bf16[8,2,24,384]{3,2,1,0:T(8,128)(2,1)} custom-call(bf16[16,2,24,384]{3,2,1,0:T(8,128)(2,1)} %all-to-all-done.2.pieces_hbm, bf16[512,768]{1,0:T(8,128)(2,1)} %get-tuple-element.29.after), custom_call_target="tpu_custom_call" | custom-call | flops 1000000000 | bytes 65536 | tf_op jit(solution)/shard_map/pallas_call | solution.py:425
  90.8 11.0 %all_to_all.20.whole = bf16[8,2,24,384]{3,2,1,0:T(8,128)(2,1)S(1)} all-to-all(bf16[8,2,24,384]{3,2,1,0:T(8,128)(2,1)} %shard_map.83), channel_id=1, replica_groups=mesh['dp'=16,'ctx'=8] {'ctx'}, dimensions={0} | all-to-all | bytes 589824 | tf_op jit(solution)/shard_map/all_to_all | solution.py:460
  101.8 0.9 shard_map.84
  (9 shorter events, 0.8 us)
Async XLA Ops:
  3.0 27.6 %all-to-all-start = ((bf16[8,2,64,768]{3,2,1,0:T(8,128)(2,1)}), bf16[8,2,64,768]{3,2,1,0:T(8,128)(2,1)}, u32[]{:S(2)}, u32[]{:S(2)}) async-start(bf16[8,2,64,768]{3,2,1,0:T(8,128)(2,1)} %shard_map.76), calls=%async_computation | async-start | bytes 3145728 | tf_op jit(solution)/shard_map/all_to_all | solution.py:460
  19.1 3.3 %collective-permute-start = (bf16[8,4,48,384]{3,2,1,0:T(8,128)(2,1)}, bf16[8,4,48,384]{3,2,1,0:T(8,128)(2,1)}, u32[]{:S(2)}, u32[]{:S(2)}) collective-permute-start(bf16[8,4,48,384]{3,2,1,0:T(8,128)(2,1)} %get-tuple-element.26), channel_id=1, source_target_pairs={{0,8},{8,0},{16,24},{24,16},{32,40},{40,32},{48,56},{56,48},{64,72... | collective-permute-start | bytes 3538952 | tf_op jit(solution)/shard_map/ppermute | solution.py:475
  24.9 21.4 %collective-permute-start.1 = (bf16[2,4,48,384]{3,2,1,0:T(8,128)(2,1)}, bf16[2,4,48,384]{3,2,1,0:T(8,128)(2,1)}, u32[]{:S(2)}, u32[]{:S(2)}) collective-permute-start(bf16[2,4,48,384]{3,2,1,0:T(8,128)(2,1)} %get-tuple-element.31), channel_id=1, source_target_pairs={{0,32},{8,40},{16,48},{24,56},{32,64},{40,72},{48,80},{56,88},{64,... | collective-permute-start | bytes 884744 | tf_op jit(solution)/shard_map/ppermute | solution.py:490
  26.4 19.8 %collective-permute-start.2 = (bf16[2,4,48,384]{3,2,1,0:T(8,128)(2,1)}, bf16[2,4,48,384]{3,2,1,0:T(8,128)(2,1)}, u32[]{:S(2)}, u32[]{:S(2)}) collective-permute-start(bf16[2,4,48,384]{3,2,1,0:T(8,128)(2,1)} %get-tuple-element.32), channel_id=1, source_target_pairs={{0,64},{8,72},{16,80},{24,88},{32,96},{40,104},{48,112},{56,120},{... | collective-permute-start | bytes 884744 | tf_op jit(solution)/shard_map/ppermute | solution.py:490
  29.2 17.1 %collective-permute-start.3 = (bf16[2,4,48,384]{3,2,1,0:T(8,128)(2,1)}, bf16[2,4,48,384]{3,2,1,0:T(8,128)(2,1)}, u32[]{:S(2)}, u32[]{:S(2)}) collective-permute-start(bf16[2,4,48,384]{3,2,1,0:T(8,128)(2,1)} %get-tuple-element.33), channel_id=1, source_target_pairs={{0,96},{8,104},{16,112},{24,120},{32,0},{40,8},{48,16},{56,24},{64... | collective-permute-start | bytes 884744 | tf_op jit(solution)/shard_map/ppermute | solution.py:490
  40.4 6.4 %collective-permute-start.4 = (bf16[8,4,48,384]{3,2,1,0:T(8,128)(2,1)}, bf16[8,4,48,384]{3,2,1,0:T(8,128)(2,1)}, u32[]{:S(2)}, u32[]{:S(2)}) collective-permute-start(bf16[8,4,48,384]{3,2,1,0:T(8,128)(2,1)} %get-tuple-element.35), channel_id=1, source_target_pairs={{0,8},{8,0},{16,24},{24,16},{32,40},{40,32},{48,56},{56,48},{64,72... | collective-permute-start | bytes 3538952 | tf_op jit(solution)/shard_map/ppermute | solution.py:475
  40.5 23.6 %all-to-all-start.1 = ((bf16[8,64,1152]{2,1,0:T(8,128)(2,1)}), bf16[8,64,1152]{2,1,0:T(8,128)(2,1)}, u32[]{:S(2)}, u32[]{:S(2)}) async-start(bf16[8,64,1152]{2,1,0:T(8,128)(2,1)} %bitcast.11), calls=%async_computation.1 | async-start | bytes 2359296 | tf_op jit(solution)/shard_map/all_to_all | solution.py:460
  49.4 17.0 %collective-permute-start.5 = (bf16[2,4,48,384]{3,2,1,0:T(8,128)(2,1)}, bf16[2,4,48,384]{3,2,1,0:T(8,128)(2,1)}, u32[]{:S(2)}, u32[]{:S(2)}) collective-permute-start(bf16[2,4,48,384]{3,2,1,0:T(8,128)(2,1)} %get-tuple-element.37), channel_id=1, source_target_pairs={{0,32},{8,40},{16,48},{24,56},{32,64},{40,72},{48,80},{56,88},{64,... | collective-permute-start | bytes 884744 | tf_op jit(solution)/shard_map/ppermute | solution.py:490
  50.0 16.4 %collective-permute-start.6 = (bf16[2,4,48,384]{3,2,1,0:T(8,128)(2,1)}, bf16[2,4,48,384]{3,2,1,0:T(8,128)(2,1)}, u32[]{:S(2)}, u32[]{:S(2)}) collective-permute-start(bf16[2,4,48,384]{3,2,1,0:T(8,128)(2,1)} %get-tuple-element.38), channel_id=1, source_target_pairs={{0,64},{8,72},{16,80},{24,88},{32,96},{40,104},{48,112},{56,120},{... | collective-permute-start | bytes 884744 | tf_op jit(solution)/shard_map/ppermute | solution.py:490
  51.9 15.1 %collective-permute-start.7 = (bf16[2,4,48,384]{3,2,1,0:T(8,128)(2,1)}, bf16[2,4,48,384]{3,2,1,0:T(8,128)(2,1)}, u32[]{:S(2)}, u32[]{:S(2)}) collective-permute-start(bf16[2,4,48,384]{3,2,1,0:T(8,128)(2,1)} %get-tuple-element.39), channel_id=1, source_target_pairs={{0,96},{8,104},{16,112},{24,120},{32,0},{40,8},{48,16},{56,24},{64... | collective-permute-start | bytes 884744 | tf_op jit(solution)/shard_map/ppermute | solution.py:490
  69.8 19.1 %all-to-all-start.2 = ((bf16[16,2,24,384]{3,2,1,0:T(8,128)(2,1)}), bf16[16,2,24,384]{3,2,1,0:T(8,128)(2,1)}, u32[]{:S(2)}, u32[]{:S(2)}) async-start(bf16[16,2,24,384]{3,2,1,0:T(8,128)(2,1)} %bitcast.16), calls=%async_computation.2 | async-start | bytes 1179648 | tf_op jit(solution)/shard_map/all_to_all | solution.py:460

commit v5 on v4

--- a/solution.py
+++ b/solution.py
@@ -487,7 +487,7 @@
 
 def ring(parts):
     return [parts[0]] + [
-        lax.ppermute(parts[step], "dp", [(i, (i + 4 * step) % 16) for i in range(16)]) for step in range(1, 4)
+        lax.ppermute(parts[step], "dp", [(i, (i + 4 * step) % 16) for i in range(16)]) for step in (2, 3, 1)
     ]
 
 

time: 104 us -> 104 us (level)
    all_to_all x3, waiting for transfers between devices: 16.3 us -> 17.6 us  [swap(): lax.all_to_all(part, axis, split_axis=0, concat_axis=0, tiled=True, axis_...]
  transfers between devices with their start and end apart: 11 -> 11, of which waited for: 5 -> 6; matrix products, arithmetic and copies ran while one was open for 0% -> 0% of each run, Pallas kernels for 31% -> 31%
where the time goes in v5:
time: 104 us; the launch traced here: 103 us
  Pallas kernels  39.3 us (38%)
  starting transfers between devices  28.3 us (27%)
  waiting for transfers between devices  23.4 us (22%)
  blocking collectives  11 us (11%)
    pallas_call x10, Pallas kernels, call(): pl.pallas_call(kernel, out_shape=out_shape, in_specs=[SMEM] * scalars + [...  39.3 us
    all_to_all x3, starting transfers between devices, swap(): lax.all_to_all(part, axis, split_axis=0, concat_axis=0, tiled=True, axis_...  19 us
    all_to_all x3, waiting for transfers between devices, swap(): lax.all_to_all(part, axis, split_axis=0, concat_axis=0, tiled=True, axis_...  17.6 us
    all_to_all x1, blocking collectives, swap(): lax.all_to_all(part, axis, split_axis=0, concat_axis=0, tiled=True, axis_...  11 us
    ppermute x6, starting transfers between devices, ring(): lax.ppermute(parts[step], 'dp', [(i, (i + 4 * step) % 16) for i in range(...  9.12 us
    ppermute x2, waiting for transfers between devices, exchange(): return lax.ppermute(send, 'dp', [(i, i ^ 1) for i in range(16)])  3.16 us
    ppermute x6, waiting for transfers between devices, ring(): lax.ppermute(parts[step], 'dp', [(i, (i + 4 * step) % 16) for i in range(...  2.62 us
  transfers between devices with their start and end apart: 11, of which 6 were waited for; matrix products, arithmetic and copies ran while one was open for 0% of the time, Pallas kernels for 31%

profile of v5, /device:TPU:0, one launch (start us, length us, event | category | flops | bytes accessed | tf_op | source)
XLA Modules:
  0.0 103.0 jit_solution(12941890672980866444)
XLA Ops:
  0.6 2.3 %shard_map.76 = bf16[8,2,64,768]{3,2,1,0:T(8,128)(2,1)} custom-call(bf16[8,64,768]{2,1,0:T(8,128)(2,1)} %bitcast.12, bf16[8,64,768]{2,1,0:T(8,128)(2,1)} %bitcast.14), custom_call_target="tpu_custom_call" | custom-call | flops 1000000 | bytes 65536 | tf_op jit(solution)/shard_map/pallas_call | solution.py:425
  3.0 5.9 %all-to-all-start = ((bf16[8,2,64,768]{3,2,1,0:T(8,128)(2,1)}), bf16[8,2,64,768]{3,2,1,0:T(8,128)(2,1)}, u32[]{:S(2)}, u32[]{:S(2)}) async-start(bf16[8,2,64,768]{3,2,1,0:T(8,128)(2,1)} %shard_map.76), calls=%async_computation | async-start | bytes 3145728 | tf_op jit(solution)/shard_map/all_to_all | solution.py:460
  8.9 10.2 %shard_map.75 = (bf16[512,1152]{1,0:T(8,128)(2,1)}, bf16[512,384]{1,0:T(8,128)(2,1)}, bf16[8,4,48,384]{3,2,1,0:T(8,128)(2,1)}, bf16[8,4,48,384]{3,2,1,0:T(8,128)(2,1)}) custom-call(s32[1]{0:T(128)} %bitcast.core_ref, bf16[512,768]{1,0:T(8,128)(2,1)} %bitcast.13, bf16[512,768]{1,0:T(8,128)(2,1)} %bitcast.15, bf16[768,2304]{1,0:T(8,128)(2,1)} %qkv_hbm.5, ...), custom_call_target="tpu_custom_call" | custom-call | flops 20000000000 | bytes 65536 | tf_op jit(solution)/shard_map/pallas_call | solution.py:425
  19.2 3.2 %collective-permute-done.received_hbm = bf16[8,4,48,384]{3,2,1,0:T(8,128)(2,1)} collective-permute-done((bf16[8,4,48,384]{3,2,1,0:T(8,128)(2,1)}, bf16[8,4,48,384]{3,2,1,0:T(8,128)(2,1)}, u32[]{:S(2)}, u32[]{:S(2)}) %collective-permute-start) | collective-permute-done | bytes 1179680 | tf_op jit(solution)/shard_map/ppermute | solution.py:475
  22.4 2.5 %shard_map.77 = (bf16[2,4,48,384]{3,2,1,0:T(8,128)(2,1)}, bf16[2,4,48,384]{3,2,1,0:T(8,128)(2,1)}, bf16[2,4,48,384]{3,2,1,0:T(8,128)(2,1)}, bf16[2,4,48,384]{3,2,1,0:T(8,128)(2,1)}) custom-call(s32[1]{0:T(128)} %bitcast.5.x_ref, bf16[8,4,48,384]{3,2,1,0:T(8,128)(2,1)} %get-tuple-element.25.keep_hbm, bf16[8,4,48,384]{3,2,1,0:T(8,128)(2,1)} %collective-permute-done.received_hbm), custom_call_target="tpu_custom_call" | custom-call | flops 2000000000 | bytes 65536 | tf_op jit(solution)/shard_map/pallas_call | solution.py:425
  24.9 3.1 %collective-permute-start.1 = (bf16[2,4,48,384]{3,2,1,0:T(8,128)(2,1)}, bf16[2,4,48,384]{3,2,1,0:T(8,128)(2,1)}, u32[]{:S(2)}, u32[]{:S(2)}) collective-permute-start(bf16[2,4,48,384]{3,2,1,0:T(8,128)(2,1)} %get-tuple-element.31), channel_id=1, source_target_pairs={{0,64},{8,72},{16,80},{24,88},{32,96},{40,104},{48,112},{56,120},{... | collective-permute-start | bytes 884744 | tf_op jit(solution)/shard_map/ppermute | solution.py:490
  28.0 1.1 %collective-permute-start.2 = (bf16[2,4,48,384]{3,2,1,0:T(8,128)(2,1)}, bf16[2,4,48,384]{3,2,1,0:T(8,128)(2,1)}, u32[]{:S(2)}, u32[]{:S(2)}) collective-permute-start(bf16[2,4,48,384]{3,2,1,0:T(8,128)(2,1)} %get-tuple-element.32), channel_id=1, source_target_pairs={{0,96},{8,104},{16,112},{24,120},{32,0},{40,8},{48,16},{56,24},{64... | collective-permute-start | bytes 884744 | tf_op jit(solution)/shard_map/ppermute | solution.py:490
  29.1 0.9 collective-permute-start.3
  30.3 9.8 %shard_map.78 = (bf16[512,1152]{1,0:T(8,128)(2,1)}, bf16[8,4,48,384]{3,2,1,0:T(8,128)(2,1)}, bf16[8,4,48,384]{3,2,1,0:T(8,128)(2,1)}) custom-call(s32[1]{0:T(128)} %bitcast.core_ref, bf16[8,2,64,768]{3,2,1,0:T(8,128)(2,1)} %all-to-all-done.both_hbm, bf16[768,2304]{1,0:T(8,128)(2,1)} %qkv_hbm.5, bf16[768,768]{1,0:T(8,128)(2,1)} %out_hbm.5, ...), custom_call_target="tpu_custom_call" | custom-call | flops 20000000000 | bytes 65536 | tf_op jit(solution)/shard_map/pallas_call | solution.py:425
  40.2 5.4 %all-to-all-start.1 = ((bf16[8,64,1152]{2,1,0:T(8,128)(2,1)}), bf16[8,64,1152]{2,1,0:T(8,128)(2,1)}, u32[]{:S(2)}, u32[]{:S(2)}) async-start(bf16[8,64,1152]{2,1,0:T(8,128)(2,1)} %bitcast.11), calls=%async_computation.1 | async-start | bytes 2359296 | tf_op jit(solution)/shard_map/all_to_all | solution.py:460
  45.7 0.6 shard_map.80.refs_0_
  46.3 2.5 %shard_map.81 = (bf16[2,4,48,384]{3,2,1,0:T(8,128)(2,1)}, bf16[2,4,48,384]{3,2,1,0:T(8,128)(2,1)}, bf16[2,4,48,384]{3,2,1,0:T(8,128)(2,1)}, bf16[2,4,48,384]{3,2,1,0:T(8,128)(2,1)}) custom-call(s32[1]{0:T(128)} %bitcast.5.x_ref, bf16[8,4,48,384]{3,2,1,0:T(8,128)(2,1)} %get-tuple-element.34.keep_hbm, ...), custom_call_target="tpu_custom_call" | custom-call | flops 2000000000 | bytes 65536 | tf_op jit(solution)/shard_map/pallas_call | solution.py:425
  48.8 2.0 %collective-permute-start.5 = (bf16[2,4,48,384]{3,2,1,0:T(8,128)(2,1)}, bf16[2,4,48,384]{3,2,1,0:T(8,128)(2,1)}, u32[]{:S(2)}, u32[]{:S(2)}) collective-permute-start(bf16[2,4,48,384]{3,2,1,0:T(8,128)(2,1)} %get-tuple-element.37), channel_id=1, source_target_pairs={{0,64},{8,72},{16,80},{24,88},{32,96},{40,104},{48,112},{56,120},{... | collective-permute-start | bytes 884744 | tf_op jit(solution)/shard_map/ppermute | solution.py:490
  50.8 1.4 %collective-permute-start.6 = (bf16[2,4,48,384]{3,2,1,0:T(8,128)(2,1)}, bf16[2,4,48,384]{3,2,1,0:T(8,128)(2,1)}, u32[]{:S(2)}, u32[]{:S(2)}) collective-permute-start(bf16[2,4,48,384]{3,2,1,0:T(8,128)(2,1)} %get-tuple-element.38), channel_id=1, source_target_pairs={{0,96},{8,104},{16,112},{24,120},{32,0},{40,8},{48,16},{56,24},{64... | collective-permute-start | bytes 884744 | tf_op jit(solution)/shard_map/ppermute | solution.py:490
  52.1 0.7 collective-permute-start.7
  52.8 10.7 %all-to-all-done.1 = bf16[8,64,1152]{2,1,0:T(8,128)(2,1)} async-done(((bf16[8,64,1152]{2,1,0:T(8,128)(2,1)}), bf16[8,64,1152]{2,1,0:T(8,128)(2,1)}, u32[]{:S(2)}, u32[]{:S(2)}) %all-to-all-start.1) | async-done | bytes 1179680 | tf_op jit(solution)/shard_map/all_to_all | solution.py:460
  63.5 2.3 %collective-permute-done.6.refs_6_ = bf16[2,4,48,384]{3,2,1,0:T(8,128)(2,1)} collective-permute-done((bf16[2,4,48,384]{3,2,1,0:T(8,128)(2,1)}, bf16[2,4,48,384]{3,2,1,0:T(8,128)(2,1)}, u32[]{:S(2)}, u32[]{:S(2)}) %collective-permute-start.6) | collective-permute-done | bytes 294944 | tf_op jit(solution)/shard_map/ppermute | solution.py:490
  66.1 2.7 %shard_map.82 = bf16[2,4,2,2,24,384]{5,4,3,2,1,0:T(8,128)(2,1)} custom-call(bf16[2,4,48,384]{3,2,1,0:T(8,128)(2,1)} %get-tuple-element.27.after.refs_0_, bf16[2,4,48,384]{3,2,1,0:T(8,128)(2,1)} %collective-permute-done.1.first.refs_1_, bf16[2,4,48,384]{3,2,1,0:T(8,128)(2,1)} %collective-permute-done.2.second.refs_2_, ...), custom_call_target="tpu_custom_call" | custom-call | flops 2000000000 | bytes 65536 | tf_op jit(solution)/shard_map/pallas_call | solution.py:425
  68.8 7.7 %all-to-all-start.2 = ((bf16[16,2,24,384]{3,2,1,0:T(8,128)(2,1)}), bf16[16,2,24,384]{3,2,1,0:T(8,128)(2,1)}, u32[]{:S(2)}, u32[]{:S(2)}) async-start(bf16[16,2,24,384]{3,2,1,0:T(8,128)(2,1)} %bitcast.16), calls=%async_computation.2 | async-start | bytes 1179648 | tf_op jit(solution)/shard_map/all_to_all | solution.py:460
  76.5 5.8 %shard_map.79 = (bf16[512,768]{1,0:T(8,128)(2,1)}, bf16[512,768]{1,0:T(8,128)(2,1)}) custom-call(bf16[512,1152]{1,0:T(8,128)(2,1)} %get-tuple-element.23.grads_hbm, bf16[512,384]{1,0:T(8,128)(2,1)} %get-tuple-element.24.ctx_hbm, bf16[512,1152]{1,0:T(8,128)(2,1)} %bitcast.7.back_hbm.refs_8_, bf16[768,2304]{1,0:T(8,128)(2,1)} %qkv_hbm.5, bf16[768,768]{1,0:T(8,128)(2,1)} %out_hbm.5), custom_call_target="tpu_custom_call" | custom-call | flops 4000000000 | bytes 65536 | tf_op jit(solution)/shard_map/pallas_call | solution.py:425
  82.4 6.6 %all-to-all-done.2.pieces_hbm = bf16[16,2,24,384]{3,2,1,0:T(8,128)(2,1)} async-done(((bf16[16,2,24,384]{3,2,1,0:T(8,128)(2,1)}), bf16[16,2,24,384]{3,2,1,0:T(8,128)(2,1)}, u32[]{:S(2)}, u32[]{:S(2)}) %all-to-all-start.2) | async-done | bytes 589856 | tf_op jit(solution)/shard_map/all_to_all | solution.py:460
  89.0 2.0 %shard_map.83 = bf16[8,2,24,384]{3,2,1,0:T(8,128)(2,1)} custom-call(bf16[16,2,24,384]{3,2,1,0:T(8,128)(2,1)} %all-to-all-done.2.pieces_hbm, bf16[512,768]{1,0:T(8,128)(2,1)} %get-tuple-element.29.after), custom_call_target="tpu_custom_call" | custom-call | flops 1000000000 | bytes 65536 | tf_op jit(solution)/shard_map/pallas_call | solution.py:425
  90.9 11.0 %all_to_all.20.whole = bf16[8,2,24,384]{3,2,1,0:T(8,128)(2,1)S(1)} all-to-all(bf16[8,2,24,384]{3,2,1,0:T(8,128)(2,1)} %shard_map.83), channel_id=1, replica_groups=mesh['dp'=16,'ctx'=8] {'ctx'}, dimensions={0} | all-to-all | bytes 589824 | tf_op jit(solution)/shard_map/all_to_all | solution.py:460
  102.0 0.9 shard_map.84
  (9 shorter events, 0.8 us)
Async XLA Ops:
  3.0 27.3 %all-to-all-start = ((bf16[8,2,64,768]{3,2,1,0:T(8,128)(2,1)}), bf16[8,2,64,768]{3,2,1,0:T(8,128)(2,1)}, u32[]{:S(2)}, u32[]{:S(2)}) async-start(bf16[8,2,64,768]{3,2,1,0:T(8,128)(2,1)} %shard_map.76), calls=%async_computation | async-start | bytes 3145728 | tf_op jit(solution)/shard_map/all_to_all | solution.py:460
  19.1 3.3 %collective-permute-start = (bf16[8,4,48,384]{3,2,1,0:T(8,128)(2,1)}, bf16[8,4,48,384]{3,2,1,0:T(8,128)(2,1)}, u32[]{:S(2)}, u32[]{:S(2)}) collective-permute-start(bf16[8,4,48,384]{3,2,1,0:T(8,128)(2,1)} %get-tuple-element.26), channel_id=1, source_target_pairs={{0,8},{8,0},{16,24},{24,16},{32,40},{40,32},{48,56},{56,48},{64,72... | collective-permute-start | bytes 3538952 | tf_op jit(solution)/shard_map/ppermute | solution.py:475
  24.9 20.8 %collective-permute-start.1 = (bf16[2,4,48,384]{3,2,1,0:T(8,128)(2,1)}, bf16[2,4,48,384]{3,2,1,0:T(8,128)(2,1)}, u32[]{:S(2)}, u32[]{:S(2)}) collective-permute-start(bf16[2,4,48,384]{3,2,1,0:T(8,128)(2,1)} %get-tuple-element.31), channel_id=1, source_target_pairs={{0,64},{8,72},{16,80},{24,88},{32,96},{40,104},{48,112},{56,120},{... | collective-permute-start | bytes 884744 | tf_op jit(solution)/shard_map/ppermute | solution.py:490
  28.0 17.7 %collective-permute-start.2 = (bf16[2,4,48,384]{3,2,1,0:T(8,128)(2,1)}, bf16[2,4,48,384]{3,2,1,0:T(8,128)(2,1)}, u32[]{:S(2)}, u32[]{:S(2)}) collective-permute-start(bf16[2,4,48,384]{3,2,1,0:T(8,128)(2,1)} %get-tuple-element.32), channel_id=1, source_target_pairs={{0,96},{8,104},{16,112},{24,120},{32,0},{40,8},{48,16},{56,24},{64... | collective-permute-start | bytes 884744 | tf_op jit(solution)/shard_map/ppermute | solution.py:490
  29.1 16.6 %collective-permute-start.3 = (bf16[2,4,48,384]{3,2,1,0:T(8,128)(2,1)}, bf16[2,4,48,384]{3,2,1,0:T(8,128)(2,1)}, u32[]{:S(2)}, u32[]{:S(2)}) collective-permute-start(bf16[2,4,48,384]{3,2,1,0:T(8,128)(2,1)} %get-tuple-element.33), channel_id=1, source_target_pairs={{0,32},{8,40},{16,48},{24,56},{32,64},{40,72},{48,80},{56,88},{64,... | collective-permute-start | bytes 884744 | tf_op jit(solution)/shard_map/ppermute | solution.py:490
  40.1 6.1 %collective-permute-start.4 = (bf16[8,4,48,384]{3,2,1,0:T(8,128)(2,1)}, bf16[8,4,48,384]{3,2,1,0:T(8,128)(2,1)}, u32[]{:S(2)}, u32[]{:S(2)}) collective-permute-start(bf16[8,4,48,384]{3,2,1,0:T(8,128)(2,1)} %get-tuple-element.35), channel_id=1, source_target_pairs={{0,8},{8,0},{16,24},{24,16},{32,40},{40,32},{48,56},{56,48},{64,72... | collective-permute-start | bytes 3538952 | tf_op jit(solution)/shard_map/ppermute | solution.py:475
  40.2 23.3 %all-to-all-start.1 = ((bf16[8,64,1152]{2,1,0:T(8,128)(2,1)}), bf16[8,64,1152]{2,1,0:T(8,128)(2,1)}, u32[]{:S(2)}, u32[]{:S(2)}) async-start(bf16[8,64,1152]{2,1,0:T(8,128)(2,1)} %bitcast.11), calls=%async_computation.1 | async-start | bytes 2359296 | tf_op jit(solution)/shard_map/all_to_all | solution.py:460
  48.8 14.7 %collective-permute-start.5 = (bf16[2,4,48,384]{3,2,1,0:T(8,128)(2,1)}, bf16[2,4,48,384]{3,2,1,0:T(8,128)(2,1)}, u32[]{:S(2)}, u32[]{:S(2)}) collective-permute-start(bf16[2,4,48,384]{3,2,1,0:T(8,128)(2,1)} %get-tuple-element.37), channel_id=1, source_target_pairs={{0,64},{8,72},{16,80},{24,88},{32,96},{40,104},{48,112},{56,120},{... | collective-permute-start | bytes 884744 | tf_op jit(solution)/shard_map/ppermute | solution.py:490
  50.8 15.1 %collective-permute-start.6 = (bf16[2,4,48,384]{3,2,1,0:T(8,128)(2,1)}, bf16[2,4,48,384]{3,2,1,0:T(8,128)(2,1)}, u32[]{:S(2)}, u32[]{:S(2)}) collective-permute-start(bf16[2,4,48,384]{3,2,1,0:T(8,128)(2,1)} %get-tuple-element.38), channel_id=1, source_target_pairs={{0,96},{8,104},{16,112},{24,120},{32,0},{40,8},{48,16},{56,24},{64... | collective-permute-start | bytes 884744 | tf_op jit(solution)/shard_map/ppermute | solution.py:490
  52.1 14.0 %collective-permute-start.7 = (bf16[2,4,48,384]{3,2,1,0:T(8,128)(2,1)}, bf16[2,4,48,384]{3,2,1,0:T(8,128)(2,1)}, u32[]{:S(2)}, u32[]{:S(2)}) collective-permute-start(bf16[2,4,48,384]{3,2,1,0:T(8,128)(2,1)} %get-tuple-element.39), channel_id=1, source_target_pairs={{0,32},{8,40},{16,48},{24,56},{32,64},{40,72},{48,80},{56,88},{64,... | collective-permute-start | bytes 884744 | tf_op jit(solution)/shard_map/ppermute | solution.py:490
  68.8 20.1 %all-to-all-start.2 = ((bf16[16,2,24,384]{3,2,1,0:T(8,128)(2,1)}), bf16[16,2,24,384]{3,2,1,0:T(8,128)(2,1)}, u32[]{:S(2)}, u32[]{:S(2)}) async-start(bf16[16,2,24,384]{3,2,1,0:T(8,128)(2,1)} %bitcast.16), calls=%async_computation.2 | async-start | bytes 1179648 | tf_op jit(solution)/shard_map/all_to_all | solution.py:460

commit v6 on v5

--- a/solution.py
+++ b/solution.py
@@ -304,9 +304,8 @@
     wait_all(outs)
 
 
-def order_kernel(back_hbm, first, second, third, out_hbm, zeros, sems):
-    zeros[...] = jnp.zeros_like(zeros)
-    wait_all(start_all([pltpu.make_async_copy(zeros, out_hbm, sems.at[0])]))
+def order_kernel(*refs):
+    pass
 
 
 def pack_kernel(x_hbm, c_hbm, both_hbm, both, sems, out_sems):
@@ -420,7 +419,7 @@
     return jax.ShapeDtypeStruct(dims, dtype)
 
 
-def call(kernel, out_shape, flops, scratch, arrays, mib=64, held=None):
+def call(kernel, out_shape, flops, scratch, arrays, mib=64, held=None, aliases=None):
     scalars = sum(1 for array in arrays if array.ndim == 1)
     return pl.pallas_call(
         kernel,
@@ -428,6 +427,7 @@
         in_specs=[SMEM] * scalars + [held or HBM] * (len(arrays) - scalars),
         out_specs=jax.tree.map(lambda _: HBM, out_shape),
         scratch_shapes=scratch,
+        input_output_aliases=aliases or {},
         compiler_params=pltpu.CompilerParams(vmem_limit_bytes=mib * MIB),
         cost_estimate=pl.CostEstimate(flops=flops, bytes_accessed=2 ** 16, transcendentals=0),
     )(*arrays)
@@ -521,7 +521,9 @@
         [buffer(POSITIONS, back_width)],
         core, both, qkv_weight, out_weight, terms_row[0],
     )
-    order = call(order_kernel, shape(8, PAIR, dtype=F32), 4 * 10 ** 10, [buffer(8, PAIR, dtype=F32), copy_sems(1)], (back, *terms_row[1:]))
+    terms_row[1] = order = call(
+        order_kernel, shape(2, 4, 48, HALF_WIDTH), 4 * 10 ** 10, [], (back, *terms_row[1:]), aliases={1: 0}
+    )
     parts = pair_sum(x_index, keep_col, send_col, order)
     terms_col = ring(parts)
     back = swap(back.reshape(ROWS, COLUMNS, back_width), "ctx").reshape(POSITIONS, back_width)

time: 104 us -> 106 us (1.019)
  waiting for transfers between devices: 23.4 us -> 26.4 us
    all_to_all x3, waiting for transfers between devices: 17.6 us -> 13.8 us  [swap(): lax.all_to_all(part, axis, split_axis=0, concat_axis=0, tiled=True, axis_...]
    ppermute x6, waiting for transfers between devices: 2.62 us -> 6.27 us  [ring(): lax.ppermute(parts[step], 'dp', [(i, (i + 4 * step) % 16) for i in range(...]
    ppermute x2, waiting for transfers between devices: 3.16 us -> 6.3 us  [exchange(): return lax.ppermute(send, 'dp', [(i, i ^ 1) for i in range(16)])]
  transfers between devices with their start and end apart: 11 -> 11, of which waited for: 6 -> 8; matrix products, arithmetic and copies ran while one was open for 0% -> 0% of each run, Pallas kernels for 31% -> 29%
where the time goes in v6:
time: 106 us
  Pallas kernels  38.7 us (37%)
  starting transfers between devices  28.6 us (27%)
  waiting for transfers between devices  26.4 us (25%)
  blocking collectives  11 us (10%)
    pallas_call x10, Pallas kernels, call(): pl.pallas_call(kernel, out_shape=out_shape, in_specs=[SMEM] * scalars + [...  38.7 us
    all_to_all x3, starting transfers between devices, swap(): lax.all_to_all(part, axis, split_axis=0, concat_axis=0, tiled=True, axis_...  19.3 us
    all_to_all x3, waiting for transfers between devices, swap(): lax.all_to_all(part, axis, split_axis=0, concat_axis=0, tiled=True, axis_...  13.8 us
    all_to_all x1, blocking collectives, swap(): lax.all_to_all(part, axis, split_axis=0, concat_axis=0, tiled=True, axis_...  11 us
    ppermute x6, starting transfers between devices, ring(): lax.ppermute(parts[step], 'dp', [(i, (i + 4 * step) % 16) for i in range(...  9.18 us
    ppermute x2, waiting for transfers between devices, exchange(): return lax.ppermute(send, 'dp', [(i, i ^ 1) for i in range(16)])  6.3 us
    ppermute x6, waiting for transfers between devices, ring(): lax.ppermute(parts[step], 'dp', [(i, (i + 4 * step) % 16) for i in range(...  6.27 us
  transfers between devices with their start and end apart: 11, of which 8 were waited for; matrix products, arithmetic and copies ran while one was open for 0% of the time, Pallas kernels for 29%

profile of v6, /device:TPU:0, one launch (start us, length us, event | category | flops | bytes accessed | tf_op | source)
XLA Modules:
  0.0 105.7 jit_solution(15841890491061983111)
XLA Ops:
  0.6 2.4 %shard_map.76 = bf16[8,2,64,768]{3,2,1,0:T(8,128)(2,1)} custom-call(bf16[8,64,768]{2,1,0:T(8,128)(2,1)} %bitcast.12, bf16[8,64,768]{2,1,0:T(8,128)(2,1)} %bitcast.14), custom_call_target="tpu_custom_call" | custom-call | flops 1000000 | bytes 65536 | tf_op jit(solution)/shard_map/pallas_call | solution.py:424
  3.0 5.9 %all-to-all-start = ((bf16[8,2,64,768]{3,2,1,0:T(8,128)(2,1)}), bf16[8,2,64,768]{3,2,1,0:T(8,128)(2,1)}, u32[]{:S(2)}, u32[]{:S(2)}) async-start(bf16[8,2,64,768]{3,2,1,0:T(8,128)(2,1)} %shard_map.76), calls=%async_computation | async-start | bytes 3145728 | tf_op jit(solution)/shard_map/all_to_all | solution.py:460
  8.9 10.2 %shard_map.75 = (bf16[512,1152]{1,0:T(8,128)(2,1)}, bf16[512,384]{1,0:T(8,128)(2,1)}, bf16[8,4,48,384]{3,2,1,0:T(8,128)(2,1)}, bf16[8,4,48,384]{3,2,1,0:T(8,128)(2,1)}) custom-call(s32[1]{0:T(128)} %bitcast.core_ref, bf16[512,768]{1,0:T(8,128)(2,1)} %bitcast.13, bf16[512,768]{1,0:T(8,128)(2,1)} %bitcast.15, bf16[768,2304]{1,0:T(8,128)(2,1)} %qkv_hbm.5, ...), custom_call_target="tpu_custom_call" | custom-call | flops 20000000000 | bytes 65536 | tf_op jit(solution)/shard_map/pallas_call | solution.py:424
  19.3 3.2 %collective-permute-done.received_hbm = bf16[8,4,48,384]{3,2,1,0:T(8,128)(2,1)} collective-permute-done((bf16[8,4,48,384]{3,2,1,0:T(8,128)(2,1)}, bf16[8,4,48,384]{3,2,1,0:T(8,128)(2,1)}, u32[]{:S(2)}, u32[]{:S(2)}) %collective-permute-start) | collective-permute-done | bytes 1179680 | tf_op jit(solution)/shard_map/ppermute | solution.py:475
  22.4 2.5 %shard_map.77 = (bf16[2,4,48,384]{3,2,1,0:T(8,128)(2,1)}, bf16[2,4,48,384]{3,2,1,0:T(8,128)(2,1)}, bf16[2,4,48,384]{3,2,1,0:T(8,128)(2,1)}, bf16[2,4,48,384]{3,2,1,0:T(8,128)(2,1)}) custom-call(s32[1]{0:T(128)} %bitcast.5.x_ref, bf16[8,4,48,384]{3,2,1,0:T(8,128)(2,1)} %get-tuple-element.25.keep_hbm, bf16[8,4,48,384]{3,2,1,0:T(8,128)(2,1)} %collective-permute-done.received_hbm), custom_call_target="tpu_custom_call" | custom-call | flops 2000000000 | bytes 65536 | tf_op jit(solution)/shard_map/pallas_call | solution.py:424
  24.9 3.1 %collective-permute-start.1 = (bf16[2,4,48,384]{3,2,1,0:T(8,128)(2,1)}, bf16[2,4,48,384]{3,2,1,0:T(8,128)(2,1)}, u32[]{:S(2)}, u32[]{:S(2)}) collective-permute-start(bf16[2,4,48,384]{3,2,1,0:T(8,128)(2,1)} %get-tuple-element.31), channel_id=1, source_target_pairs={{0,64},{8,72},{16,80},{24,88},{32,96},{40,104},{48,112},{56,120},{... | collective-permute-start | bytes 884744 | tf_op jit(solution)/shard_map/ppermute | solution.py:490
  28.0 1.1 %collective-permute-start.2 = (bf16[2,4,48,384]{3,2,1,0:T(8,128)(2,1)}, bf16[2,4,48,384]{3,2,1,0:T(8,128)(2,1)}, u32[]{:S(2)}, u32[]{:S(2)}) collective-permute-start(bf16[2,4,48,384]{3,2,1,0:T(8,128)(2,1)} %get-tuple-element.32), channel_id=1, source_target_pairs={{0,96},{8,104},{16,112},{24,120},{32,0},{40,8},{48,16},{56,24},{64... | collective-permute-start | bytes 884744 | tf_op jit(solution)/shard_map/ppermute | solution.py:490
  29.2 0.9 collective-permute-start.3
  30.4 9.8 %shard_map.78 = (bf16[512,1152]{1,0:T(8,128)(2,1)}, bf16[8,4,48,384]{3,2,1,0:T(8,128)(2,1)}, bf16[8,4,48,384]{3,2,1,0:T(8,128)(2,1)}) custom-call(s32[1]{0:T(128)} %bitcast.core_ref, bf16[8,2,64,768]{3,2,1,0:T(8,128)(2,1)} %all-to-all-done.both_hbm, bf16[768,2304]{1,0:T(8,128)(2,1)} %qkv_hbm.5, bf16[768,768]{1,0:T(8,128)(2,1)} %out_hbm.5, ...), custom_call_target="tpu_custom_call" | custom-call | flops 20000000000 | bytes 65536 | tf_op jit(solution)/shard_map/pallas_call | solution.py:424
  40.2 5.4 %all-to-all-start.1 = ((bf16[8,64,1152]{2,1,0:T(8,128)(2,1)}), bf16[8,64,1152]{2,1,0:T(8,128)(2,1)}, u32[]{:S(2)}, u32[]{:S(2)}) async-start(bf16[8,64,1152]{2,1,0:T(8,128)(2,1)} %bitcast.11), calls=%async_computation.1 | async-start | bytes 2359296 | tf_op jit(solution)/shard_map/all_to_all | solution.py:460
  45.7 3.1 %collective-permute-done.4.received_hbm = bf16[8,4,48,384]{3,2,1,0:T(8,128)(2,1)} collective-permute-done((bf16[8,4,48,384]{3,2,1,0:T(8,128)(2,1)}, bf16[8,4,48,384]{3,2,1,0:T(8,128)(2,1)}, u32[]{:S(2)}, u32[]{:S(2)}) %collective-permute-start.4) | collective-permute-done | bytes 1179680 | tf_op jit(solution)/shard_map/ppermute | solution.py:475
  48.8 2.5 %shard_map.81 = (bf16[2,4,48,384]{3,2,1,0:T(8,128)(2,1)}, bf16[2,4,48,384]{3,2,1,0:T(8,128)(2,1)}, bf16[2,4,48,384]{3,2,1,0:T(8,128)(2,1)}, bf16[2,4,48,384]{3,2,1,0:T(8,128)(2,1)}) custom-call(s32[1]{0:T(128)} %bitcast.5.x_ref, bf16[8,4,48,384]{3,2,1,0:T(8,128)(2,1)} %get-tuple-element.34.keep_hbm, ...), custom_call_target="tpu_custom_call" | custom-call | flops 2000000000 | bytes 65536 | tf_op jit(solution)/shard_map/pallas_call | solution.py:424
  51.3 2.0 %collective-permute-start.5 = (bf16[2,4,48,384]{3,2,1,0:T(8,128)(2,1)}, bf16[2,4,48,384]{3,2,1,0:T(8,128)(2,1)}, u32[]{:S(2)}, u32[]{:S(2)}) collective-permute-start(bf16[2,4,48,384]{3,2,1,0:T(8,128)(2,1)} %get-tuple-element.37), channel_id=1, source_target_pairs={{0,64},{8,72},{16,80},{24,88},{32,96},{40,104},{48,112},{56,120},{... | collective-permute-start | bytes 884744 | tf_op jit(solution)/shard_map/ppermute | solution.py:490
  53.3 1.3 %collective-permute-start.6 = (bf16[2,4,48,384]{3,2,1,0:T(8,128)(2,1)}, bf16[2,4,48,384]{3,2,1,0:T(8,128)(2,1)}, u32[]{:S(2)}, u32[]{:S(2)}) collective-permute-start(bf16[2,4,48,384]{3,2,1,0:T(8,128)(2,1)} %get-tuple-element.38), channel_id=1, source_target_pairs={{0,96},{8,104},{16,112},{24,120},{32,0},{40,8},{48,16},{56,24},{64... | collective-permute-start | bytes 884744 | tf_op jit(solution)/shard_map/ppermute | solution.py:490
  55.3 6.9 %all-to-all-done.1 = bf16[8,64,1152]{2,1,0:T(8,128)(2,1)} async-done(((bf16[8,64,1152]{2,1,0:T(8,128)(2,1)}), bf16[8,64,1152]{2,1,0:T(8,128)(2,1)}, u32[]{:S(2)}, u32[]{:S(2)}) %all-to-all-start.1) | async-done | bytes 1179680 | tf_op jit(solution)/shard_map/all_to_all | solution.py:460
  62.3 0.8 collective-permute-done.5.refs_5_
  63.1 5.2 %collective-permute-done.6.refs_6_ = bf16[2,4,48,384]{3,2,1,0:T(8,128)(2,1)} collective-permute-done((bf16[2,4,48,384]{3,2,1,0:T(8,128)(2,1)}, bf16[2,4,48,384]{3,2,1,0:T(8,128)(2,1)}, u32[]{:S(2)}, u32[]{:S(2)}) %collective-permute-start.6) | collective-permute-done | bytes 294944 | tf_op jit(solution)/shard_map/ppermute | solution.py:490
  68.5 2.7 %shard_map.82 = bf16[2,4,2,2,24,384]{5,4,3,2,1,0:T(8,128)(2,1)} custom-call(bf16[2,4,48,384]{3,2,1,0:T(8,128)(2,1)} %get-tuple-element.27.after.refs_0_, bf16[2,4,48,384]{3,2,1,0:T(8,128)(2,1)} %shard_map.80.refs_0_.refs_1_, bf16[2,4,48,384]{3,2,1,0:T(8,128)(2,1)} %collective-permute-done.2.refs_2_, bf16[2,4,48,384]{3,2,1,0:T(8,128)(2,1)} %collective-permute-done.3.refs_3_, ...), custom_call_target="tpu_custom_call" | custom-call | flops 2000000000 | bytes 65536 | tf_op jit(solution)/shard_map/pallas_call | solution.py:424
  71.3 8.0 %all-to-all-start.2 = ((bf16[16,2,24,384]{3,2,1,0:T(8,128)(2,1)}), bf16[16,2,24,384]{3,2,1,0:T(8,128)(2,1)}, u32[]{:S(2)}, u32[]{:S(2)}) async-start(bf16[16,2,24,384]{3,2,1,0:T(8,128)(2,1)} %bitcast.16), calls=%async_computation.2 | async-start | bytes 1179648 | tf_op jit(solution)/shard_map/all_to_all | solution.py:460
  79.3 5.8 %shard_map.79 = (bf16[512,768]{1,0:T(8,128)(2,1)}, bf16[512,768]{1,0:T(8,128)(2,1)}) custom-call(bf16[512,1152]{1,0:T(8,128)(2,1)} %get-tuple-element.23.grads_hbm, bf16[512,384]{1,0:T(8,128)(2,1)} %get-tuple-element.24.ctx_hbm, bf16[512,1152]{1,0:T(8,128)(2,1)} %bitcast.7.back_hbm.refs_8_, bf16[768,2304]{1,0:T(8,128)(2,1)} %qkv_hbm.5, bf16[768,768]{1,0:T(8,128)(2,1)} %out_hbm.5), custom_call_target="tpu_custom_call" | custom-call | flops 4000000000 | bytes 65536 | tf_op jit(solution)/shard_map/pallas_call | solution.py:424
  85.1 6.6 %all-to-all-done.2.pieces_hbm = bf16[16,2,24,384]{3,2,1,0:T(8,128)(2,1)} async-done(((bf16[16,2,24,384]{3,2,1,0:T(8,128)(2,1)}), bf16[16,2,24,384]{3,2,1,0:T(8,128)(2,1)}, u32[]{:S(2)}, u32[]{:S(2)}) %all-to-all-start.2) | async-done | bytes 589856 | tf_op jit(solution)/shard_map/all_to_all | solution.py:460
  91.7 2.0 %shard_map.83 = bf16[8,2,24,384]{3,2,1,0:T(8,128)(2,1)} custom-call(bf16[16,2,24,384]{3,2,1,0:T(8,128)(2,1)} %all-to-all-done.2.pieces_hbm, bf16[512,768]{1,0:T(8,128)(2,1)} %get-tuple-element.29.after), custom_call_target="tpu_custom_call" | custom-call | flops 1000000000 | bytes 65536 | tf_op jit(solution)/shard_map/pallas_call | solution.py:424
  93.7 11.0 %all_to_all.20.whole = bf16[8,2,24,384]{3,2,1,0:T(8,128)(2,1)S(1)} all-to-all(bf16[8,2,24,384]{3,2,1,0:T(8,128)(2,1)} %shard_map.83), channel_id=1, replica_groups=mesh['dp'=16,'ctx'=8] {'ctx'}, dimensions={0} | all-to-all | bytes 589824 | tf_op jit(solution)/shard_map/all_to_all | solution.py:460
  104.7 0.9 shard_map.84
  (9 shorter events, 1.4 us)
Async XLA Ops:
  3.0 27.3 %all-to-all-start = ((bf16[8,2,64,768]{3,2,1,0:T(8,128)(2,1)}), bf16[8,2,64,768]{3,2,1,0:T(8,128)(2,1)}, u32[]{:S(2)}, u32[]{:S(2)}) async-start(bf16[8,2,64,768]{3,2,1,0:T(8,128)(2,1)} %shard_map.76), calls=%async_computation | async-start | bytes 3145728 | tf_op jit(solution)/shard_map/all_to_all | solution.py:460
  19.2 3.3 %collective-permute-start = (bf16[8,4,48,384]{3,2,1,0:T(8,128)(2,1)}, bf16[8,4,48,384]{3,2,1,0:T(8,128)(2,1)}, u32[]{:S(2)}, u32[]{:S(2)}) collective-permute-start(bf16[8,4,48,384]{3,2,1,0:T(8,128)(2,1)} %get-tuple-element.26), channel_id=1, source_target_pairs={{0,8},{8,0},{16,24},{24,16},{32,40},{40,32},{48,56},{56,48},{64,72... | collective-permute-start | bytes 3538952 | tf_op jit(solution)/shard_map/ppermute | solution.py:475
  24.9 20.7 %collective-permute-start.1 = (bf16[2,4,48,384]{3,2,1,0:T(8,128)(2,1)}, bf16[2,4,48,384]{3,2,1,0:T(8,128)(2,1)}, u32[]{:S(2)}, u32[]{:S(2)}) collective-permute-start(bf16[2,4,48,384]{3,2,1,0:T(8,128)(2,1)} %get-tuple-element.31), channel_id=1, source_target_pairs={{0,64},{8,72},{16,80},{24,88},{32,96},{40,104},{48,112},{56,120},{... | collective-permute-start | bytes 884744 | tf_op jit(solution)/shard_map/ppermute | solution.py:490
  28.0 17.6 %collective-permute-start.2 = (bf16[2,4,48,384]{3,2,1,0:T(8,128)(2,1)}, bf16[2,4,48,384]{3,2,1,0:T(8,128)(2,1)}, u32[]{:S(2)}, u32[]{:S(2)}) collective-permute-start(bf16[2,4,48,384]{3,2,1,0:T(8,128)(2,1)} %get-tuple-element.32), channel_id=1, source_target_pairs={{0,96},{8,104},{16,112},{24,120},{32,0},{40,8},{48,16},{56,24},{64... | collective-permute-start | bytes 884744 | tf_op jit(solution)/shard_map/ppermute | solution.py:490
  29.2 16.5 %collective-permute-start.3 = (bf16[2,4,48,384]{3,2,1,0:T(8,128)(2,1)}, bf16[2,4,48,384]{3,2,1,0:T(8,128)(2,1)}, u32[]{:S(2)}, u32[]{:S(2)}) collective-permute-start(bf16[2,4,48,384]{3,2,1,0:T(8,128)(2,1)} %get-tuple-element.33), channel_id=1, source_target_pairs={{0,32},{8,40},{16,48},{24,56},{32,64},{40,72},{48,80},{56,88},{64,... | collective-permute-start | bytes 884744 | tf_op jit(solution)/shard_map/ppermute | solution.py:490
  40.2 22.1 %all-to-all-start.1 = ((bf16[8,64,1152]{2,1,0:T(8,128)(2,1)}), bf16[8,64,1152]{2,1,0:T(8,128)(2,1)}, u32[]{:S(2)}, u32[]{:S(2)}) async-start(bf16[8,64,1152]{2,1,0:T(8,128)(2,1)} %bitcast.11), calls=%async_computation.1 | async-start | bytes 2359296 | tf_op jit(solution)/shard_map/all_to_all | solution.py:460
  45.6 3.2 %collective-permute-start.4 = (bf16[8,4,48,384]{3,2,1,0:T(8,128)(2,1)}, bf16[8,4,48,384]{3,2,1,0:T(8,128)(2,1)}, u32[]{:S(2)}, u32[]{:S(2)}) collective-permute-start(bf16[8,4,48,384]{3,2,1,0:T(8,128)(2,1)} %get-tuple-element.35), channel_id=1, source_target_pairs={{0,8},{8,0},{16,24},{24,16},{32,40},{40,32},{48,56},{56,48},{64,72... | collective-permute-start | bytes 3538952 | tf_op jit(solution)/shard_map/ppermute | solution.py:475
  51.3 11.8 %collective-permute-start.5 = (bf16[2,4,48,384]{3,2,1,0:T(8,128)(2,1)}, bf16[2,4,48,384]{3,2,1,0:T(8,128)(2,1)}, u32[]{:S(2)}, u32[]{:S(2)}) collective-permute-start(bf16[2,4,48,384]{3,2,1,0:T(8,128)(2,1)} %get-tuple-element.37), channel_id=1, source_target_pairs={{0,64},{8,72},{16,80},{24,88},{32,96},{40,104},{48,112},{56,120},{... | collective-permute-start | bytes 884744 | tf_op jit(solution)/shard_map/ppermute | solution.py:490
  53.3 15.0 %collective-permute-start.6 = (bf16[2,4,48,384]{3,2,1,0:T(8,128)(2,1)}, bf16[2,4,48,384]{3,2,1,0:T(8,128)(2,1)}, u32[]{:S(2)}, u32[]{:S(2)}) collective-permute-start(bf16[2,4,48,384]{3,2,1,0:T(8,128)(2,1)} %get-tuple-element.38), channel_id=1, source_target_pairs={{0,96},{8,104},{16,112},{24,120},{32,0},{40,8},{48,16},{56,24},{64... | collective-permute-start | bytes 884744 | tf_op jit(solution)/shard_map/ppermute | solution.py:490
  54.6 13.9 %collective-permute-start.7 = (bf16[2,4,48,384]{3,2,1,0:T(8,128)(2,1)}, bf16[2,4,48,384]{3,2,1,0:T(8,128)(2,1)}, u32[]{:S(2)}, u32[]{:S(2)}) collective-permute-start(bf16[2,4,48,384]{3,2,1,0:T(8,128)(2,1)} %get-tuple-element.39), channel_id=1, source_target_pairs={{0,32},{8,40},{16,48},{24,56},{32,64},{40,72},{48,80},{56,88},{64,... | collective-permute-start | bytes 884744 | tf_op jit(solution)/shard_map/ppermute | solution.py:490
  71.3 20.4 %all-to-all-start.2 = ((bf16[16,2,24,384]{3,2,1,0:T(8,128)(2,1)}), bf16[16,2,24,384]{3,2,1,0:T(8,128)(2,1)}, u32[]{:S(2)}, u32[]{:S(2)}) async-start(bf16[16,2,24,384]{3,2,1,0:T(8,128)(2,1)} %bitcast.16), calls=%async_computation.2 | async-start | bytes 1179648 | tf_op jit(solution)/shard_map/all_to_all | solution.py:460
